TPU v7x, 32 devices: a whole 2x2x4 slice. The times are simulated.
32 devices in a mesh: dp: 2 (over core), expert: 16 (over z, y, x).
Axes of the slice: x: 2, y: 2, z: 4, core: 2. Of those that a mesh axis runs over, the one named last changes fastest.
Arguments:
- inputs: bfloat16 [32768, 512], P(('dp', 'expert')), may hold values from -6 to 6
- w_first: bfloat16 [16, 512, 256], P('expert'), may hold values from -0.25 to 0.25
- b_first: bfloat16 [16, 256], P('expert'), may hold values from -0.59765625 to 0.59765625
- w_second: bfloat16 [16, 256, 128], P('expert'), may hold values from -0.5 to 0.5
- b_second: bfloat16 [16, 128], P('expert'), may hold values from -0.59765625 to 0.59765625
- gate_weight: bfloat16 [2, 512, 16], replicated, may hold values from -0.125 to 0.125
- gate_bias: bfloat16 [2, 16], replicated, may hold values from -0.29882812 to 0.29882812
- tower_first_weight: bfloat16 [2, 128, 64], replicated, may hold values from -1 to 1
- tower_first_bias: bfloat16 [2, 64], replicated, may hold values from -0.59765625 to 0.59765625
- tower_last: bfloat16 [2, 64], replicated, may hold values from -1.5 to 1.5
- tower_out_bias: bfloat16 [2], replicated, may hold values from -2 to 2
- labels: int32 [2, 32768], P(None, ('dp', 'expert')), may hold values 0 or 1
- group_len: int32 [16], replicated, may hold values from 1 to 2048, as said below
- group_shard: int32 [16], replicated, may hold values from 0 to 1, as said below
Outputs:
- predictions: float32 [2, 32768], P(None, ('dp', 'expert'))
- input_grad: float32 [32768, 512], P(('dp', 'expert'))
- grad_w_first: float32 [16, 512, 256], P('expert')
- grad_b_first: float32 [16, 256], P('expert')
- grad_w_second: float32 [16, 256, 128], P('expert')
- grad_b_second: float32 [16, 128], P('expert')
- grad_gate: float32 [2, 512, 16], replicated
- grad_gate_bias: float32 [2, 16], replicated
- grad_tower_first: float32 [2, 128, 64], replicated
- grad_tower_bias: float32 [2, 64], replicated
- grad_tower_last: float32 [2, 64], replicated
- grad_tower_out_bias: float32 [2], replicated
Inputs may be any that keep to these rules, and one draw needn't show every extreme that they name: `group_len`: the lengths of the groups of one batch shard sum to at most 16384, and in every draw some shard's groups fill exactly 16384 slots. `group_shard`: each shard number is taken by exactly 8 groups.
All inputs are finite; a program needn't handle non-finite values. No bound on the sum of `labels` on one device may be relied on, other than what follows from the above.
Results may differ from a plain program's by a relative error of at most 0.0083.
Values may be sent and summed in bfloat16 or wider, within the bound.
No kernel may reach another device: no remote copies, remote signals or barrier semaphores. Data moves between devices by JAX's collectives and lax.ppermute only.
A program may use at most 320 MiB of HBM per device.

v0:
```python
import functools

import jax
import jax.numpy as jnp
from jax import lax
from jax.experimental import pallas as pl
from jax.experimental.pallas import tpu as pltpu
from jax.sharding import PartitionSpec as P

F32 = jnp.float32
BF16 = jnp.bfloat16
ROOT = 0.7978845608028654
CUBE = 0.044715
NN = (((1,), (0,)), ((), ()))
NT = (((1,), (1,)), ((), ()))
TN = (((0,), (0,)), ((), ()))
TT = (((0,), (1,)), ((), ()))
BIAS_ROWS = 16
SCALE = 3e8
EARLY = 6
BACK_CHUNK = 2048
TAIL = 10
PAIRS = ((0, 4), (1, 2), (5, 6), (3, 7))
PAY_ROWS = 320 + BIAS_ROWS
VMEM = pl.BlockSpec(memory_space=pltpu.VMEM)
SMEM = pl.BlockSpec(memory_space=pltpu.SMEM)
ANY = pl.BlockSpec(memory_space=pl.ANY)


def dot(a, b, dims):
    return lax.dot_general(a, b, dims, preferred_element_type=F32)


def gelu_pair(v):
    square = v * v
    upper = 0.5 + 0.5 * jnp.tanh(v * (ROOT + (ROOT * CUBE) * square))
    value = v * upper
    slope = upper + value * (1.0 - upper) * (2.0 * ROOT + (6.0 * ROOT * CUBE) * square)
    return value, slope


def call(name, kernel, ins, outs, pin, micros, scratch=(), scalars=0, limit=8, after=()):
    limit = limit if pin is not None else 60
    pinned = lambda a: pltpu.with_memory_space_constraint(a, pltpu.VMEM) if pin else a
    args = [a if n < scalars else pinned(a) for n, a in enumerate(ins)] + list(after)
    count = len(ins)
    body = kernel
    if after:

        def body(*refs):
            return kernel(*refs[:count], *refs[count + len(after) :])

    kept = pltpu.VMEM if pin else jax.ShapeDtypeStruct
    shapes = [(kept if stay else jax.ShapeDtypeStruct)(shape, dtype) for shape, dtype, stay in outs]
    return pl.pallas_call(
        body,
        name=name,
        in_specs=[SMEM] * scalars + [VMEM] * (count - scalars) + [ANY] * len(after),
        out_specs=[VMEM] * len(outs),
        out_shape=shapes,
        scratch_shapes=list(scratch),
        compiler_params=pltpu.CompilerParams(vmem_limit_bytes=limit * 2**20),
        cost_estimate=pl.CostEstimate(flops=int(micros * SCALE), bytes_accessed=0, transcendentals=0),
    )(*args)


def hold(value, after):
    count = len(after)
    return pl.pallas_call(
        lambda *refs: None,
        name="hold",
        in_specs=[ANY] * (1 + count),
        out_specs=ANY,
        out_shape=jax.ShapeDtypeStruct(value.shape, value.dtype),
        input_output_aliases={0: 0},
        compiler_params=pltpu.CompilerParams(vmem_limit_bytes=2**20),
        cost_estimate=pl.CostEstimate(flops=0, bytes_accessed=0, transcendentals=0),
    )(value, *after)


def slot_of(masks, int_ref, j):
    half = len(masks[0])
    mask = jnp.where(int_ref[0] == 0, masks[0][j], masks[1][j])
    return int_ref[0] * half + ((int_ref[1] & (half - 1)) ^ mask)


def to_column(row):
    n = row.shape[1]
    same = lax.broadcasted_iota(jnp.int32, (n, n), 0) == lax.broadcasted_iota(jnp.int32, (n, n), 1)
    return jnp.sum(jnp.where(same, jnp.broadcast_to(row, (n, n)), 0.0), axis=1, keepdims=True)


def side_by_side(columns, tall):
    lane = lax.broadcasted_iota(jnp.int32, (tall, 128), 1)
    small = jnp.zeros((tall, 128), F32)
    for n, col in enumerate(columns):
        small = jnp.where(lane == n, jnp.broadcast_to(col, (tall, 128)), small)
    return small


def fold(ref, base, block):
    deep = block.shape[0] // 4
    for k in range(4):
        ref[base : base + deep, 128 * k : 128 * (k + 1)] = block[deep * k : deep * (k + 1)]


def unfold(ref, base, deep):
    return jnp.concatenate(
        [ref[base : base + deep, 128 * k : 128 * (k + 1)] for k in range(4)], axis=0
    )


def pack_kernel(w1_ref, w2_ref, b1_ref, b2_ref, pay_ref, w1, w2, b1, b2, sems):
    copies = [
        pltpu.make_async_copy(src, dst, sems.at[n])
        for n, (src, dst) in enumerate(((w1_ref, w1), (w2_ref, w2), (b1_ref, b1), (b2_ref, b2)))
    ]
    for copy in copies:
        copy.start()
    for copy in copies[1:]:
        copy.wait()
    second = w2[0].astype(F32).T.astype(BF16)
    pay_ref[0, 256:320, :256] = second[:64]
    pay_ref[0, 256:320, 256:] = second[64:]
    row = jnp.concatenate([b1[...].astype(F32), b2[...].astype(F32), jnp.zeros((1, 128), F32)], axis=1)
    pay_ref[0, 320:, :] = jnp.broadcast_to(row, (BIAS_ROWS, 512)).astype(BF16)
    copies[0].wait()
    pay_ref[0, :256, :] = w1[0].astype(F32).T.astype(BF16)


def pack(w1, w2, b1, b2):
    arrays = (w1, w2, b1, b2)
    return pl.pallas_call(
        pack_kernel,
        name="pack",
        in_specs=[pl.BlockSpec(memory_space=pltpu.HBM)] * 4,
        out_specs=VMEM,
        out_shape=jax.ShapeDtypeStruct((1, PAY_ROWS, 512), BF16),
        scratch_shapes=[pltpu.VMEM(a.shape, a.dtype) for a in arrays] + [pltpu.SemaphoreType.DMA((4,))],
        compiler_params=pltpu.CompilerParams(vmem_limit_bytes=8 * 2**20),
        cost_estimate=pl.CostEstimate(flops=0, bytes_accessed=0, transcendentals=0),
    )(*[pltpu.with_memory_space_constraint(a, pltpu.HBM) for a in arrays])


def biases(pay):
    flipped = pay[320:, :].astype(F32).T
    return flipped[:256, 0:1], flipped[256:384, 0:1]


def second_weight(pay):
    return jnp.concatenate([pay[256:320, :256], pay[256:320, 256:]], axis=0)


def gate_kernel(masks, groups, int_ref, label_ref, there_ref, gw_ref, gb_ref, mine_ref, other_ref, *refs):
    prob_ref, low_ref, weight_ref, x_out, label_out, scratch, sems = refs
    rows = mine_ref.shape[0]
    experts = 2 * len(masks[0])
    copies = [
        pltpu.make_async_copy(src, x_out.at[pl.ds(n * rows, rows), :], sems.at[n])
        for n, src in enumerate((mine_ref, other_ref))
    ]
    for copy in copies:
        copy.start()
    for side in range(2):
        at = slice(side * rows, (side + 1) * rows)
        label_out[:, at] = (label_ref, there_ref)[side][...].astype(F32)
        copies[side].wait()
        for t in range(2):
            part = dot(gw_ref[t], x_out[at, :], NT) + to_column(gb_ref[t : t + 1, :].astype(F32))
            top = jnp.max(part, axis=0, keepdims=True)
            e = jnp.exp(part - top)
            scratch[t * experts : (t + 1) * experts, at] = e / jnp.sum(e, axis=0, keepdims=True)
        shard = int_ref[0] if side == 0 else 1 - int_ref[0]
        index = int_ref[1] * rows + lax.broadcasted_iota(jnp.int32, (1, rows), 1)
        start = jnp.int32(0)
        weight = jnp.zeros((1, rows), F32)
        for g in range(groups):
            length = int_ref[3 + groups + g]
            size = jnp.where(int_ref[3 + g] == shard, length, 0)
            inside = (index >= start) & (index < start + size)
            recip = 1.0 / jnp.full((1, rows), length, jnp.int32).astype(F32)
            weight = weight + jnp.where(inside, recip, 0.0)
            start = start + size
        weight_ref[:, at] = weight
    for j in range(experts // 2):
        slot = slot_of(masks, int_ref, j)
        for t in range(2):
            row = scratch[pl.ds(t * experts + slot, 1), :]
            prob_ref[j, t : t + 1, :] = row
            low_ref[j, t : t + 1, :] = row.astype(BF16).astype(F32)


def forward_kernel(bundles, first, block, chunk, x_ref, pay_a, pay_b, low_ref, *refs):
    if not first:
        mix_in, *refs = refs
    kept, mix_ref = (refs[:4], refs[4:8]), refs[8]
    depth = pay_a.shape[0]
    weights = {}
    for k in range(depth):
        for n, pay_ref in enumerate((pay_a, pay_b)):
            pay = pay_ref[k]
            weights[k, n] = (pay[:256], second_weight(pay), *biases(pay))
    work = [(c, k, n) for c in range(0, block, chunk) for k in range(depth) for n in range(2)]

    def step(i, _):
        base = pl.multiple_of(i * block, block)
        totals = [None, None]

        def layer_one(c, k, n):
            return dot(weights[k, n][0], x_ref[pl.ds(base + c, chunk), :], NT)

        def after_one(pre, c, k, n):
            value, slope = gelu_pair(pre + weights[k, n][2])
            hidden = value.astype(BF16)
            kept[n][0][k, :, pl.ds(base + c, chunk)] = hidden
            kept[n][1][k, :, pl.ds(base + c, chunk)] = slope.astype(kept[n][1].dtype)
            return hidden

        def after_two(pre, c, k, n):
            at = pl.ds(base + c, chunk)
            value, slope = gelu_pair(pre + weights[k, n][3])
            out = value.astype(BF16)
            kept[n][2][k, :, at] = out
            kept[n][3][k, :, at] = slope.astype(kept[n][3].dtype)
            out = out.astype(F32)
            for t in range(2):
                term = low_ref[bundles[n] * depth + k, t : t + 1, at] * out
                if k == 0 and n == 0:
                    totals[t] = term if first else mix_in[t, :, at] + term
                else:
                    totals[t] = totals[t] + term
                if k == depth - 1 and n == 1:
                    mix_ref[t, :, at] = totals[t].astype(mix_ref.dtype)

        ones, twos = {0: layer_one(*work[0])}, {}
        for i in range(len(work) + 1):
            if i + 1 < len(work):
                ones[i + 1] = layer_one(*work[i + 1])
            if i < len(work):
                hidden = after_one(ones.pop(i), *work[i])
            if i >= 1:
                after_two(twos.pop(i - 1), *work[i - 1])
            if i < len(work):
                twos[i] = dot(weights[work[i][1:]][1], hidden, NN)
        return 0

    lax.fori_loop(0, x_ref.shape[0] // block, step, 0)


def tower_kernel(
    chunk, mix_ref, come_ref, label_ref, weight_ref, tob_ref, tw_ref, tb_ref, tl_ref,
    pred_ref, dmix_ref, centre_ref, shared_ref, first, sums,
):
    rows = pred_ref.shape[1]
    first[...] = jnp.zeros_like(first)
    sums[...] = jnp.zeros_like(sums)
    tb = [to_column(tb_ref[t : t + 1, :].astype(F32)) for t in range(2)]
    tl = [to_column(tl_ref[t : t + 1, :].astype(F32)) for t in range(2)]

    def step(side, i, _):
        at = pl.ds(pl.multiple_of(side * rows + i * chunk, chunk), chunk)
        there = pl.ds(pl.multiple_of((1 - side) * rows + i * chunk, chunk), chunk)
        cols = []
        for t in range(2):
            mixed = mix_ref[t, :, at].astype(F32) + come_ref[t, :, there].astype(F32)
            low = mixed.astype(BF16)
            act, slope = gelu_pair(dot(tw_ref[t], low, NN) + tb[t])
            score = jnp.sum(act * tl[t], axis=0, keepdims=True) + tob_ref[0:1, t : t + 1].astype(F32)
            pred = 1.0 / (1.0 + jnp.exp(-score))
            d_score = weight_ref[:, at] * (pred - label_ref[t : t + 1, at])
            d_low = (d_score * tl[t] * slope).astype(BF16)
            d_mixed = dot(tw_ref[t], d_low, TN)
            dmix_ref[t, :, at] = d_mixed
            centre_ref[t : t + 1, at] = jnp.sum(d_mixed * mixed, axis=0, keepdims=True)
            if side == 0:
                pred_ref[t : t + 1, at] = pred
                first[t] += dot(d_low, low, NT)
                cols.append(jnp.sum(act * d_score, axis=1, keepdims=True))
                cols.append(jnp.sum(d_low.astype(F32), axis=1, keepdims=True))
                total = jnp.sum(d_score, axis=1, keepdims=True)
                cols.append(jnp.broadcast_to(total, (64, 1)))
        if side == 0:
            sums[...] += side_by_side([cols[3 * t + n] for n in range(3) for t in range(2)], 64)
        return 0

    lax.fori_loop(0, rows // chunk, functools.partial(step, 0), 0)
    lax.fori_loop(0, rows // chunk, functools.partial(step, 1), 0)
    for t in range(2):
        fold(shared_ref, 16 * t, first[t])
    fold(shared_ref, 32, sums[...])


def shared_rows(experts):
    return -(-(48 + 2 * experts + experts // 2) // 16) * 16


def gate_back_kernel(masks, chunk, spot_ref, x_ref, dmix_ref, centre_ref, prob_ref, tower_ref, *refs):
    outs = refs[:8]
    dgate_ref, keep_ref, give_ref, gates, shared_ref = refs[8:]
    depth = outs[0].shape[0]
    experts = 2 * len(masks[0])
    gates[...] = jnp.zeros_like(gates)

    def step(i, _):
        at = pl.ds(pl.multiple_of(i * chunk, chunk), chunk)
        for j in range(8 * depth):
            out = outs[j // depth][j % depth, :, at].astype(F32)
            slot = slot_of(masks, spot_ref, j)
            for t in range(2):
                d_prob = jnp.sum(dmix_ref[t, :, at] * out, axis=0, keepdims=True)
                d_gate = prob_ref[j, t : t + 1, at] * (d_prob - centre_ref[t : t + 1, at])
                gates[pl.ds(t * experts + slot, 1), at] = d_gate
        return 0

    lax.fori_loop(0, x_ref.shape[0] // chunk, step, 0)
    low = gates[...].astype(BF16)
    dgate_ref[...] = low
    shared_ref[...] = jnp.zeros_like(shared_ref)
    shared_ref[:48, :] = tower_ref[...]
    shared_ref[48 : 48 + 2 * experts, :] = dot(low, x_ref[...], NN)
    bias = jnp.sum(low.astype(F32), axis=1, keepdims=True)
    fold(shared_ref, 48 + 2 * experts, side_by_side([bias], 2 * experts))
    deep = keep_ref.shape[0]
    keep_ref[...] = shared_ref[pl.ds(pl.multiple_of(spot_ref[0] * deep, 8), deep), :]
    give_ref[...] = shared_ref[pl.ds(pl.multiple_of((1 - spot_ref[0]) * deep, 8), deep), :]


def backward_kernel(bundles, add, block, x_ref, pay_a, pay_b, low_ref, dmix_ref, *refs):
    kept, refs = (refs[:3], refs[3:6]), refs[6:]
    if add:
        come, refs = refs[:2], refs[2:]
    grads, dones, d_two, sums = refs[:2], refs[2:4], refs[4], refs[5]
    depth = pay_a.shape[0]
    for k in range(depth):
        weights = [second_weight(pay[k]) for pay in (pay_a, pay_b)]
        sums[...] = jnp.zeros_like(sums)

        def step(i, _, k=k, weights=weights):
            at = pl.ds(pl.multiple_of(i * block, block), block)
            for n in range(2):
                _, g1_ref, g2_ref = kept[n]
                j = bundles[n] * depth + k
                d_out = low_ref[j, 0:1, at] * dmix_ref[0, :, at] + low_ref[j, 1:2, at] * dmix_ref[1, :, at]
                two = d_out.astype(BF16).astype(F32) * g2_ref[k, :, at].astype(F32)
                two_low = two.astype(BF16)
                d_two[n, :, at] = two_low
                one = dot(weights[n], two_low, TN) * g1_ref[k, :, at].astype(F32)
                dones[n][k, :, at] = one.astype(BF16)
                add_one, add_two = one[:, :128], two[:, :128]
                for m in range(128, block, 128):
                    add_one = add_one + one[:, m : m + 128]
                    add_two = add_two + two[:, m : m + 128]
                sums[n, :256] += add_one
                sums[n, 256:] += add_two
            return 0

        lax.fori_loop(0, x_ref.shape[0] // block, step, 0)
        for n in range(2):
            h_ref = kept[n][0]
            first = dot(dones[n][k], x_ref[...], NN)
            second = dot(d_two[n], h_ref[k], NT)
            second = jnp.concatenate([second[:64], second[64:]], axis=1)
            row = jnp.concatenate(
                [
                    jnp.sum(sums[n].T, axis=0, keepdims=True),
                    jnp.zeros((1, 128), F32),
                ],
                axis=1,
            )
            high = row.astype(BF16).astype(F32)
            index = lax.broadcasted_iota(jnp.int32, (BIAS_ROWS, 512), 0)
            both = jnp.where(index == 0, high, jnp.where(index == 1, row - high, 0.0))
            if add:
                first = first + come[n][k, :256, :].astype(F32)
                second = second + come[n][k, 256:320, :].astype(F32)
                both = both + come[n][k, 320:, :].astype(F32)
            grads[n][k, :256, :] = first.astype(grads[n].dtype)
            grads[n][k, 256:320, :] = second.astype(grads[n].dtype)
            grads[n][k, 320:, :] = both.astype(grads[n].dtype)


def input_kernel(bundles, chunk, dgate_ref, gw_ref, *refs):
    experts = gw_ref.shape[1]
    count = len(bundles)
    ones, pays, outs = refs[:count], refs[count : 2 * count], refs[2 * count :]
    for side, out_ref in enumerate(outs):
        rows = out_ref.shape[0]

        def step(i, _, side=side, rows=rows, out_ref=out_ref):
            at = pl.ds(pl.multiple_of(side * rows + i * chunk, chunk), chunk)
            total = dot(dgate_ref[:experts, at], gw_ref[0], TN) + dot(dgate_ref[experts:, at], gw_ref[1], TN)
            for one, pay in zip(ones, pays):
                for k in range(one.shape[0]):
                    total = total + dot(one[k, :, at], pay[k, :256, :], TN)
            out_ref[pl.ds(pl.multiple_of(i * chunk, chunk), chunk), :] = total
            return 0

        lax.fori_loop(0, rows // chunk, step, 0)


def input_rest_kernel(bundles, chunk, *refs):
    count = len(bundles)
    ones, pays, befores, outs = refs[:count], refs[count : 2 * count], refs[2 * count : 2 * count + 2], refs[-2:]
    for side, (before, out_ref) in enumerate(zip(befores, outs)):
        rows = out_ref.shape[0]

        def step(i, _, side=side, rows=rows, before=before, out_ref=out_ref):
            at = pl.ds(pl.multiple_of(side * rows + i * chunk, chunk), chunk)
            here = pl.ds(pl.multiple_of(i * chunk, chunk), chunk)
            total = before[here, :]
            for one, pay in zip(ones, pays):
                for k in range(one.shape[0]):
                    total = total + dot(one[k, :, at], pay[k, :256, :], TN)
            out_ref[here, :] = total.astype(out_ref.dtype)
            return 0

        lax.fori_loop(0, rows // chunk, step, 0)


def add_kernel(count, *refs):
    total = refs[0][...].astype(F32)
    for ref in refs[1:count]:
        total = total + ref[...].astype(F32)
    for ref in refs[count:]:
        ref[...] = total.astype(ref.dtype)


def finish_kernel(owner_ref, mine_ref, come_ref, w1_ref, b1_ref, w2_ref, b2_ref):
    owner = owner_ref[2] == 1
    mine_ref, come_ref = mine_ref.at[0], come_ref.at[0]
    w1_ref[0] = jnp.where(owner, mine_ref[:256, :], come_ref[:256, :]).T
    second = jnp.where(owner, mine_ref[256:320, :], come_ref[256:320, :])
    w2_ref[0] = jnp.concatenate([second[:, :256], second[:, 256:]], axis=0).T
    bias = jnp.where(owner, mine_ref[320:328, :], come_ref[320:328, :])
    bias = bias[0:1] + bias[1:2]
    b1_ref[...] = bias[:, :256]
    b2_ref[...] = bias[:, 256:384]


def close_kernel(
    experts, spot_ref, keep_ref, give_ref,
    gate_ref, gate_bias_ref, first_ref, tb_ref, tl_ref, tob_ref, done_ref, shared_ref,
):

    base = 48 + 2 * experts
    deep = keep_ref.shape[0]
    shared_ref[pl.ds(pl.multiple_of(spot_ref[0] * deep, 8), deep), :] = keep_ref[...]
    shared_ref[pl.ds(pl.multiple_of((1 - spot_ref[0]) * deep, 8), deep), :] = give_ref[...]
    for t in range(2):
        gate_ref[t] = shared_ref[48 + t * experts : 48 + (t + 1) * experts, :]
        first_ref[t] = unfold(shared_ref, 16 * t, 16)
    small = unfold(shared_ref, 32, 16).T
    tl_ref[...] = small[0:2, :]
    tb_ref[...] = small[2:4, :]
    tob_ref[:, 0:1] = small[4:5, 0:1]
    tob_ref[:, 1:2] = small[5:6, 0:1]
    bias = unfold(shared_ref, base, experts // 2).T
    gate_bias_ref[0:1, :] = bias[0:1, :experts]
    gate_bias_ref[1:2, :] = bias[0:1, experts:]
    done_ref[...] = jnp.zeros_like(done_ref)


def per_device(
    inputs,
    w_first,
    b_first,
    w_second,
    b_second,
    gate_weight,
    gate_bias,
    tower_first_weight,
    tower_first_bias,
    tower_last,
    tower_out_bias,
    labels,
    group_len,
    group_shard,
):
    rows = inputs.shape[0]
    experts = lax.axis_size("expert")
    half = experts // 2
    bits = experts.bit_length() - 1
    depth = half // 8
    pin = True if depth == 1 else None
    chunk = 256 if pin else 512
    core = lax.axis_index("dp")
    place = lax.axis_index("expert")
    owner = core == place // half
    near_bit, mid_bit, end_bit = (2, 2), (1, 0), (0, 1)
    extra = [(b, b) for b in range(bits - 2, 2, -1)]

    def pairs(bit_of_core, want=None, also=0):
        return [
            (c * experts + q, c * experts + (q ^ (1 << bit_of_core[c]) ^ also))
            for c in range(2)
            for q in range(experts)
            if want is None or (c == q // half) == want
        ]

    def send(name, value, bit_of_core, want=None, also=0):
        with jax.named_scope(name):
            return lax.ppermute(value, ("dp", "expert"), pairs(bit_of_core, want, also))

    def swap(name, value):
        with jax.named_scope(name):
            return lax.ppermute(value, "dp", [(0, 1), (1, 0)])

    def deal(value):
        route = []
        for c in range(2):
            for q in range(experts):
                target = c * experts + (q ^ half) if c == q // half else (1 - c) * experts + q
                route.append((c * experts + q, target))
        with jax.named_scope("deal"):
            return lax.ppermute(value, ("dp", "expert"), route)

    def expert_mask(c, j):
        bundle, inner = j // depth, j % depth
        found = sum(1 << extra[e][c] for e in range(len(extra)) if (inner >> e) & 1)
        for n, at in enumerate((near_bit, mid_bit, end_bit)):
            found |= ((bundle >> n) & 1) << at[c]
        return found

    masks = [[expert_mask(c, j) for j in range(half)] for c in range(2)]
    spot = jnp.stack([core, place, owner.astype(jnp.int32)]).astype(jnp.int32)

    pay = pack(w_first, w_second, b_first, b_second)
    zero = deal(pay)
    for at in extra:
        zero = jnp.concatenate([zero, send("pay_extra", zero, at)], axis=0)
    labels_there = swap("labels", labels)
    inputs_there = swap("inputs", inputs)
    gate_rows = jnp.transpose(gate_weight, (0, 2, 1))
    ints = jnp.concatenate([spot, group_shard, group_len])
    outs = [((half, 2, 2 * rows), F32)] * 2 + [((1, 2 * rows), F32), ((2 * rows, 512), BF16), ((2, 2 * rows), F32)]
    kept = pltpu.VMEM if pin else jax.ShapeDtypeStruct
    prob, low, weights, x, both_labels = pl.pallas_call(
        functools.partial(gate_kernel, masks, group_len.shape[0]),
        name="gate",
        in_specs=[SMEM] + [VMEM] * 4 + [ANY] * 2,
        out_specs=[VMEM] * 5,
        out_shape=[kept(shape, dtype) for shape, dtype in outs],
        scratch_shapes=[pltpu.VMEM((2 * experts, 2 * rows), F32), pltpu.SemaphoreType.DMA((2,))],
        compiler_params=pltpu.CompilerParams(vmem_limit_bytes=(8 if pin else 60) * 2**20),
        cost_estimate=pl.CostEstimate(flops=0, bytes_accessed=0, transcendentals=0),
    )(ints, labels, labels_there, gate_rows, gate_bias, inputs, inputs_there)

    pays = [hold(zero, [low])] + [None] * 7
    pays[1] = send("pay_1", pays[0], near_bit)
    pays[2] = send("pay_2", pays[0], mid_bit)
    pays[4] = send("pay_4", pays[0], end_bit)
    held = hold(pays[1], [pays[2], pays[4]])
    pays[3] = send("pay_3", held, mid_bit)
    pays[5] = send("pay_5", held, end_bit)
    pays[6] = send("pay_6", pays[2], end_bit)

    mixed = None
    saved = [None] * 8
    slope_type = F32 if pin else BF16
    for a, b in PAIRS:
        shape = lambda deep, dtype: ((depth, deep, 2 * rows), dtype, True)
        *kept, mixed = call(
            f"forward_{a}{b}",
            functools.partial(forward_kernel, (a, b), mixed is None, 4 * chunk, chunk),
            [x, pays[a], pays[b], low] + ([] if mixed is None else [mixed]),
            [shape(256, BF16), shape(256, BF16), shape(128, BF16), shape(128, slope_type)] * 2
            + [((2, 128, 2 * rows), BF16 if (a, b) == PAIRS[-1] else F32, True)],
            pin,
            4.5 * depth,
        )
        saved[a], saved[b] = kept[:4], kept[4:]
        if pays[7] is None:
            pays[7] = send("pay_7", hold(pays[3], [mixed]), end_bit)

    predictions, dmix, centre, tower_sums = call(
        "tower",
        functools.partial(tower_kernel, 512),
        [mixed, swap("mixed", mixed), both_labels, weights, tower_out_bias[None]]
        + [jnp.transpose(tower_first_weight, (0, 2, 1)), tower_first_bias, tower_last],
        [
            ((2, rows), F32, False),
            ((2, 128, 2 * rows), F32, True),
            ((2, 2 * rows), F32, True),
            ((48, 512), F32, True),
        ],
        pin,
        4,
        [pltpu.VMEM((2, 64, 128), F32), pltpu.VMEM((64, 128), F32)],
    )

    def back(a, b, come, dtype, cost, after=()):
        grad = ((depth, PAY_ROWS, 512), dtype, False)
        done = ((depth, 256, 2 * rows), BF16, True)
        return call(
            f"backward_{a}{b}",
            functools.partial(backward_kernel, (a, b), come is not None, BACK_CHUNK),
            [x, pays[a], pays[b], low, dmix]
            + [saved[n][m] for n in (a, b) for m in (0, 1, 3)]
            + list(come or ()),
            [grad, grad, done, done],
            pin,
            cost,
            [pltpu.VMEM((2, 128, 2 * rows), BF16), pltpu.VMEM((2, 384, 128), F32)],
            after=after,
        )

    ones = [None] * 8
    grad_six, grad_seven, ones[6], ones[7] = back(6, 7, None, BF16, 5)
    six, seven = send("grad_six", grad_six, end_bit), send("grad_seven", grad_seven, end_bit)
    grad_four, grad_five, ones[4], ones[5] = back(4, 5, None, BF16, 1, [ones[7]])
    five, four = send("grad_five", grad_five, end_bit), send("grad_four", grad_four, end_bit)
    deep = shared_rows(experts) // 2
    dgate, keep, give = call(
        "gate_back",
        functools.partial(gate_back_kernel, masks, 512),
        [ints, x, dmix, centre, prob, tower_sums] + [kept[2] for kept in saved],
        [((2 * experts, 2 * rows), BF16, True)] + [((deep, 512), F32, True)] * 2,
        pin,
        1,
        [pltpu.VMEM((2 * experts, 2 * rows), F32), pltpu.VMEM((2 * deep, 512), F32)],
        1,
        after=[ones[5]],
    )
    grad_two, grad_three, ones[2], ones[3] = back(2, 3, (six, seven), BF16, 1, [dgate])
    three, two = send("grad_three", grad_three, mid_bit), send("grad_two", grad_two, mid_bit)
    halves = [((rows, 512), F32, True)] * 2
    early, late = (2, 3, 4, 5, 6, 7), (0, 1)
    parts = call(
        "input_early",
        functools.partial(input_kernel, early, 512),
        [dgate, gate_rows] + [ones[n] for n in early] + [pays[n] for n in early],
        halves,
        pin,
        EARLY * depth,
    )
    def add(values, dtypes, after=()):
        shape = values[0].shape
        outs = [(shape, dtype, True) for dtype in dtypes]
        return call("add", functools.partial(add_kernel, len(values)), values, outs, pin, 0, after=after)

    (keep,) = add([keep, swap("give", give)], [F32], [ones[3]])
    stages = []
    for b in range(2, bits):
        (keep,) = add([keep, send(f"shared_{b}", keep, (b, b))], [F32])
        stages.append(keep)

    grad_zero, grad_one, ones[0], ones[1] = back(0, 1, (four, five), F32, 5, [parts[0], stages[0]])
    own, over = call(
        "input_late",
        functools.partial(input_rest_kernel, late, 512),
        [ones[n] for n in late] + [pays[n] for n in late] + list(parts),
        [((rows, 512), F32, True), ((rows, 512), BF16, True)],
        pin,
        2.5 * depth,
        after=[stages[0]],
    )

    top = bits - 1
    (one,) = add([grad_one, three], [BF16])
    if extra:
        (zero,) = add([grad_zero, two, send("near", one, near_bit)], [F32])
        for at in reversed(extra):
            count = zero.shape[0] // 2
            zero = zero[:count] + send("extra", zero[count:].astype(BF16), at).astype(F32)
        low_zero = zero.astype(BF16)
        pieces = []
    else:
        pieces = [send("cross", one, (top, top), False, 1 << near_bit[0]), send("near", one, near_bit, True)]
        zero, low_zero = add([grad_zero, two], [F32, BF16], [own])
    pieces = [zero, *pieces, send("far", low_zero, (top, top), False)]
    (keep,) = add([keep, send("shared_1", keep, (1, 1))], [F32], [low_zero])
    (keep,) = add([keep, send("shared_0", keep, (0, 0))], [F32])
    give = swap("keep", keep)
    grad_gate, grad_gate_bias, tower_first, tower_bias, last, out_bias, done = call(
        "close",
        functools.partial(close_kernel, experts),
        [ints, keep, give],
        [
            ((2, experts, 512), F32, False),
            ((2, experts), F32, False),
            ((2, 64, 128), F32, False),
            ((2, 64), F32, False),
            ((2, 64), F32, False),
            ((1, 2), F32, False),
            ((8, 128), F32, True),
        ],
        pin,
        1,
        [pltpu.VMEM((2 * deep, 512), F32)],
        1,
    )
    (final,) = add(pieces, [F32], [done])

    (input_grad,) = call(
        "input_sum",
        functools.partial(add_kernel, 2),
        [own, swap("over", over)],
        [((rows, 512), F32, False)],
        pin,
        1.5,
        after=[final],
    )
    grad_w_first, grad_b_first, grad_w_second, grad_b_second = call(
        "finish",
        finish_kernel,
        [ints, final, swap("final", final)],
        [
            ((1, 512, 256), F32, False),
            ((1, 256), F32, False),
            ((1, 256, 128), F32, False),
            ((1, 128), F32, False),
        ],
        pin,
        TAIL,
        scalars=1,
    )
    return (
        predictions,
        input_grad,
        grad_w_first,
        grad_b_first,
        grad_w_second,
        grad_b_second,
        jnp.transpose(grad_gate, (0, 2, 1)),
        grad_gate_bias,
        jnp.transpose(tower_first, (0, 2, 1)),
        tower_bias,
        last,
        out_bias[0],
    )


def solution(mesh):
    in_specs = (
        P(("dp", "expert"), None),
        P("expert", None, None),
        P("expert", None),
        P("expert", None, None),
        P("expert", None),
        P(),
        P(),
        P(),
        P(),
        P(),
        P(),
        P(None, ("dp", "expert")),
        P(),
        P(),
    )
    out_specs = (
        P(None, ("dp", "expert")),
        P(("dp", "expert"), None),
        P("expert", None, None),
        P("expert", None),
        P("expert", None, None),
        P("expert", None),
        P(),
        P(),
        P(),
        P(),
        P(),
        P(),
    )
    return jax.shard_map(
        per_device, mesh=mesh, in_specs=in_specs, out_specs=out_specs, check_vma=False
    )
```

profile of v0, /device:TPU:0, one launch (start us, length us, event | category | flops | bytes accessed | tf_op | source)
XLA Modules:
  0.0 115.2 jit_solution(17223549490161544184)
XLA Ops:
  0.6 0.5 collective-permute-start.1
  1.2 1.2 %pack.1 = bf16[1,336,512]{2,1,0:T(8,128)(2,1)S(1)} custom-call(bf16[1,512,256]{2,1,0:T(8,128)(2,1)} %w1_ref.1, bf16[1,256,128]{2,1,0:T(8,128)(2,1)} %w2_ref.1, bf16[1,256]{1,0:T(2,128)(2,1)} %b1_ref.1, bf16[1,128]{1,0:T(2,128)(2,1)} %b2_ref.1), custom_call_target="tpu_custom_call" | custom-call | tf_op jit(solution)/shard_map/pack/pallas_call | solution.py:133
  2.4 3.7 %collective-permute-start.2 = (bf16[1,336,512]{2,1,0:T(8,128)(2,1)S(1)}, bf16[1,336,512]{2,1,0:T(8,128)(2,1)S(1)}, u32[]{:S(2)}, u32[]{:S(2)}) collective-permute-start(bf16[1,336,512]{2,1,0:T(8,128)(2,1)S(1)} %pack.1), channel_id=1, source_target_pairs={{0,8},{1,9},{2,10},{3,11},{4,12},{5,13},{6,14},{7,15},{8,24},{9,25... | collective-permute-start | bytes 1032200 | tf_op jit(solution)/shard_map/deal/ppermute | solution.py:515
  6.0 0.7 concatenate.3.int_ref.refs_0_.spot_ref.owner_ref
  6.8 0.6 collective-permute-done.there_ref
  7.4 1.2 %copy-done = bf16[1024,512]{1,0:T(8,128)(2,1)S(1)} copy-done((bf16[1024,512]{1,0:T(8,128)(2,1)S(1)}, bf16[1024,512]{1,0:T(8,128)(2,1)}, u32[]{:S(2)}) %copy-start) | copy-done | bytes 1048600
  8.6 0.8 copy-done.1
  9.4 0.7 copy-done.3
  10.1 0.7 copy-done.4
  10.8 2.3 %gate.1 = (f32[8,2,2048]{2,1,0:T(2,128)S(1)}, f32[8,2,2048]{2,1,0:T(2,128)S(1)}, f32[1,2048]{1,0:T(1,128)S(1)}, bf16[2048,512]{1,0:T(8,128)(2,1)S(1)}, f32[2,2048]{1,0:T(2,128)S(1)}) custom-call(s32[35]{0:T(128)S(1)} %concatenate.3.int_ref.refs_0_.spot_ref.owner_ref, s32[2,1024]{1,0:T(2,128)S(1)} %copy-done.3, s32[2,1024]{1,0:T(2,128)S(1)} %collective-permute-done.there_ref, ...), custom_call_target="tpu_custom_call" | custom-call | tf_op jit(solution)/shard_map/gate/pallas_call | solution.py:537
  13.1 2.9 %collective-permute-start.3 = (bf16[1,336,512]{2,1,0:T(8,128)(2,1)S(1)}, bf16[1,336,512]{2,1,0:T(8,128)(2,1)S(1)}, u32[]{:S(2)}, u32[]{:S(2)}) collective-permute-start(bf16[1,336,512]{2,1,0:T(8,128)(2,1)S(1)} %hold.3.pay_a.refs_1_.refs_2_), channel_id=1, source_target_pairs={{0,4},{1,5},{2,6},{3,7},{4,0},{5,1},{6,2},{7,3},{8,12},{9,13},{10,... | collective-permute-start | bytes 1032200 | tf_op jit(solution)/shard_map/pay_1/ppermute | solution.py:502
  16.0 1.5 %collective-permute-start.5 = (bf16[1,336,512]{2,1,0:T(8,128)(2,1)S(1)}, bf16[1,336,512]{2,1,0:T(8,128)(2,1)S(1)}, u32[]{:S(2)}, u32[]{:S(2)}) collective-permute-start(bf16[1,336,512]{2,1,0:T(8,128)(2,1)S(1)} %hold.3.pay_a.refs_1_.refs_2_), channel_id=1, source_target_pairs={{0,1},{1,0},{2,3},{3,2},{4,5},{5,4},{6,7},{7,6},{8,9},{9,8},{10,11... | collective-permute-start | bytes 1032200 | tf_op jit(solution)/shard_map/pay_4/ppermute | solution.py:502
  17.4 1.5 %collective-permute-start.4 = (bf16[1,336,512]{2,1,0:T(8,128)(2,1)S(1)}, bf16[1,336,512]{2,1,0:T(8,128)(2,1)S(1)}, u32[]{:S(2)}, u32[]{:S(2)}) collective-permute-start(bf16[1,336,512]{2,1,0:T(8,128)(2,1)S(1)} %hold.3.pay_a.refs_1_.refs_2_), channel_id=1, source_target_pairs={{0,2},{1,3},{2,0},{3,1},{4,6},{5,7},{6,4},{7,5},{8,10},{9,11},{10,... | collective-permute-start | bytes 1032200 | tf_op jit(solution)/shard_map/pay_2/ppermute | solution.py:502
  19.0 5.6 %collective-permute-done.3.pay_a.refs_2_.refs_3_ = bf16[1,336,512]{2,1,0:T(8,128)(2,1)S(1)} collective-permute-done((bf16[1,336,512]{2,1,0:T(8,128)(2,1)S(1)}, bf16[1,336,512]{2,1,0:T(8,128)(2,1)S(1)}, u32[]{:S(2)}, u32[]{:S(2)}) %collective-permute-start.3) | collective-permute-done | bytes 344096 | tf_op jit(solution)/shard_map/pay_1/ppermute | solution.py:502
  24.6 1.3 %collective-permute-done.5.refs_2_.pay_b.refs_1_.refs_8_ = bf16[1,336,512]{2,1,0:T(8,128)(2,1)S(1)} collective-permute-done((bf16[1,336,512]{2,1,0:T(8,128)(2,1)S(1)}, bf16[1,336,512]{2,1,0:T(8,128)(2,1)S(1)}, u32[]{:S(2)}, u32[]{:S(2)}) %collective-permute-start.5) | collective-permute-done | bytes 344096 | tf_op jit(solution)/shard_map/pay_4/ppermute | solution.py:502
  26.3 1.5 %collective-permute-start.8 = (bf16[1,336,512]{2,1,0:T(8,128)(2,1)S(1)}, bf16[1,336,512]{2,1,0:T(8,128)(2,1)S(1)}, u32[]{:S(2)}, u32[]{:S(2)}) collective-permute-start(bf16[1,336,512]{2,1,0:T(8,128)(2,1)S(1)} %hold.4), channel_id=1, source_target_pairs={{0,1},{1,0},{2,3},{3,2},{4,5},{5,4},{6,7},{7,6},{8,9},{9,8},{10,11... | collective-permute-start | bytes 1032200 | tf_op jit(solution)/shard_map/pay_5/ppermute | solution.py:502
  28.3 5.1 %forward_04.1 = (bf16[1,256,2048]{2,1,0:T(8,128)(2,1)S(1)}, bf16[1,256,2048]{2,1,0:T(8,128)(2,1)S(1)}, bf16[1,128,2048]{2,1,0:T(8,128)(2,1)S(1)}, f32[1,128,2048...) custom-call(bf16[2048,512]{1,0:T(8,128)(2,1)S(1)} %get-tuple-element, ...), custom_call_target="tpu_custom_call" | custom-call | flops 1350000000 | tf_op jit(solution)/shard_map/forward_04/pallas_call | solution.py:55
  33.4 3.3 %collective-permute-done.6.pay_a.refs_2_.refs_7_ = bf16[1,336,512]{2,1,0:T(8,128)(2,1)S(1)} collective-permute-done((bf16[1,336,512]{2,1,0:T(8,128)(2,1)S(1)}, bf16[1,336,512]{2,1,0:T(8,128)(2,1)S(1)}, u32[]{:S(2)}, u32[]{:S(2)}) %collective-permute-start.6) | collective-permute-done | bytes 344096 | tf_op jit(solution)/shard_map/pay_3/ppermute | solution.py:502
  36.8 1.7 %collective-permute-start.7 = (bf16[1,336,512]{2,1,0:T(8,128)(2,1)S(1)}, bf16[1,336,512]{2,1,0:T(8,128)(2,1)S(1)}, u32[]{:S(2)}, u32[]{:S(2)}) collective-permute-start(bf16[1,336,512]{2,1,0:T(8,128)(2,1)S(1)} %hold.5), channel_id=1, source_target_pairs={{0,1},{1,0},{2,3},{3,2},{4,5},{5,4},{6,7},{7,6},{8,9},{9,8},{10,11... | collective-permute-start | bytes 1032200 | tf_op jit(solution)/shard_map/pay_7/ppermute | solution.py:502
  38.4 4.9 %forward_12.1 = (bf16[1,256,2048]{2,1,0:T(8,128)(2,1)S(1)}, bf16[1,256,2048]{2,1,0:T(8,128)(2,1)S(1)}, bf16[1,128,2048]{2,1,0:T(8,128)(2,1)S(1)}, f32[1,128,2048...) custom-call(bf16[2048,512]{1,0:T(8,128)(2,1)S(1)} %get-tuple-element, ...), custom_call_target="tpu_custom_call" | custom-call | flops 1350000000 | tf_op jit(solution)/shard_map/forward_12/pallas_call | solution.py:55
  43.3 4.9 %forward_56.1 = (bf16[1,256,2048]{2,1,0:T(8,128)(2,1)S(1)}, bf16[1,256,2048]{2,1,0:T(8,128)(2,1)S(1)}, bf16[1,128,2048]{2,1,0:T(8,128)(2,1)S(1)}, f32[1,128,2048...) custom-call(bf16[2048,512]{1,0:T(8,128)(2,1)S(1)} %get-tuple-element, ...), custom_call_target="tpu_custom_call" | custom-call | flops 1350000000 | tf_op jit(solution)/shard_map/forward_56/pallas_call | solution.py:55
  48.3 4.9 %forward_37.1 = (bf16[1,256,2048]{2,1,0:T(8,128)(2,1)S(1)}, bf16[1,256,2048]{2,1,0:T(8,128)(2,1)S(1)}, bf16[1,128,2048]{2,1,0:T(8,128)(2,1)S(1)}, f32[1,128,2048...) custom-call(bf16[2048,512]{1,0:T(8,128)(2,1)S(1)} %get-tuple-element, ...), custom_call_target="tpu_custom_call" | custom-call | flops 1350000000 | tf_op jit(solution)/shard_map/forward_37/pallas_call | solution.py:55
  53.3 2.6 %collective-permute-done.10.come_ref = bf16[2,128,2048]{2,1,0:T(8,128)(2,1)S(1)} collective-permute-done((bf16[2,128,2048]{2,1,0:T(8,128)(2,1)S(1)}, bf16[2,128,2048]{2,1,0:T(8,128)(2,1)S(1)}, u32[]{:S(2)}, u32[]{:S(2)}) %collective-permute-start.10) | collective-permute-done | bytes 1048608 | tf_op jit(solution)/shard_map/mixed/ppermute | solution.py:506
  56.0 3.5 %tower.1 = (f32[2,1024]{1,0:T(2,128)}, f32[2,128,2048]{2,1,0:T(8,128)S(1)}, f32[2,2048]{1,0:T(2,128)S(1)}, f32[48,512]{1,0:T(8,128)S(1)}) custom-call(bf16[2,128,2048]{2,1,0:T(8,128)(2,1)S(1)} %get-tuple-element.98.mix_ref, bf16[2,128,2048]{2,1,0:T(8,128)(2,1)S(1)} %collective-permute-done.10.come_ref, f32[2,2048]{1,0:T(2,128)S(1)} %get-tuple-element.99.label_ref, ...), custom_call_target="tpu_custom_call" | custom-call | flops 1200000000 | tf_op jit(solution)/shard_map/tower/pallas_call | solution.py:55
  59.4 2.8 %backward_67.1 = (bf16[1,336,512]{2,1,0:T(8,128)(2,1)S(1)}, bf16[1,336,512]{2,1,0:T(8,128)(2,1)S(1)}, bf16[1,256,2048]{2,1,0:T(8,128)(2,1)S(1)}, bf16[1,256,2048]{2,1,0:T(8,128)(2,1)S(1)}) custom-call(bf16[2048,512]{1,0:T(8,128)(2,1)S(1)} %get-tuple-element.93.x_ref.refs_0_.refs_1_, bf16[1,336,512]{2,1,0:T(8,128)(2,1)S(1)} %collective-permute-done.9.pay_b.pay_a.refs_10_, ...), custom_call_target="tpu_custom_call" | custom-call | flops 1500000000 | tf_op jit(solution)/shard_map/backward_67/pallas_call | solution.py:55
  62.7 1.6 %collective-permute-start.14 = (bf16[1,336,512]{2,1,0:T(8,128)(2,1)S(1)}, bf16[1,336,512]{2,1,0:T(8,128)(2,1)S(1)}, u32[]{:S(2)}, u32[]{:S(2)}) collective-permute-start(bf16[1,336,512]{2,1,0:T(8,128)(2,1)S(1)} %get-tuple-element.144), channel_id=1, source_target_pairs={{0,1},{1,0},{2,3},{3,2},{4,5},{5,4},{6,7},{7,6},{8,9},{9,8},{10,11... | collective-permute-start | bytes 1032200 | tf_op jit(solution)/shard_map/grad_seven/ppermute | solution.py:502
  64.4 2.8 %backward_45.1 = (bf16[1,336,512]{2,1,0:T(8,128)(2,1)S(1)}, bf16[1,336,512]{2,1,0:T(8,128)(2,1)S(1)}, bf16[1,256,2048]{2,1,0:T(8,128)(2,1)S(1)}, bf16[1,256,2048]{2,1,0:T(8,128)(2,1)S(1)}) custom-call(bf16[2048,512]{1,0:T(8,128)(2,1)S(1)} %get-tuple-element.93.x_ref.refs_0_.refs_1_, ...), custom_call_target="tpu_custom_call" | custom-call | flops 300000000 | tf_op jit(solution)/shard_map/backward_45/pallas_call | solution.py:55
  67.6 1.6 %collective-permute-start.12 = (bf16[1,336,512]{2,1,0:T(8,128)(2,1)S(1)}, bf16[1,336,512]{2,1,0:T(8,128)(2,1)S(1)}, u32[]{:S(2)}, u32[]{:S(2)}) collective-permute-start(bf16[1,336,512]{2,1,0:T(8,128)(2,1)S(1)} %get-tuple-element.123), channel_id=1, source_target_pairs={{0,1},{1,0},{2,3},{3,2},{4,5},{5,4},{6,7},{7,6},{8,9},{9,8},{10,11... | collective-permute-start | bytes 1032200 | tf_op jit(solution)/shard_map/grad_five/ppermute | solution.py:502
  69.2 3.3 %gate_back.1 = (bf16[32,2048]{1,0:T(8,128)(2,1)S(1)}, f32[48,512]{1,0:T(8,128)S(1)}, f32[48,512]{1,0:T(8,128)S(1)}) custom-call(s32[35]{0:T(128)S(1)} %concatenate.3.int_ref.refs_0_.spot_ref.owner_ref, bf16[2048,512]{1,0:T(8,128)(2,1)S(1)} %get-tuple-element.93.x_ref.refs_0_.refs_1_, f32[2,128,2048]{2,1,0:T(8,128)S(1)} %get-tuple-element.102.dmix_ref.refs_4_.refs_2_, ...), custom_call_target="tpu_custom_call" | custom-call | flops 300000000 | tf_op jit(solution)/shard_map/gate_back/pallas_call | solution.py:55
  72.6 0.6 collective-permute-done.14.refs_12_
  73.3 2.8 %backward_23.1 = (bf16[1,336,512]{2,1,0:T(8,128)(2,1)S(1)}, bf16[1,336,512]{2,1,0:T(8,128)(2,1)S(1)}, bf16[1,256,2048]{2,1,0:T(8,128)(2,1)S(1)}, bf16[1,256,2048]{2,1,0:T(8,128)(2,1)S(1)}) custom-call(bf16[2048,512]{1,0:T(8,128)(2,1)S(1)} %get-tuple-element.93.x_ref.refs_0_.refs_1_, bf16[1,336,512]{2,1,0:T(8,128)(2,1)S(1)} %collective-permute-done.4.refs_1_.pay_b.refs_6_, ...), custom_call_target="tpu_custom_call" | custom-call | flops 300000000 | tf_op jit(solution)/shard_map/backward_23/pallas_call | solution.py:55
  76.1 0.5 collective-permute-start.16
  76.6 1.7 %collective-permute-start.18 = (bf16[1,336,512]{2,1,0:T(8,128)(2,1)S(1)}, bf16[1,336,512]{2,1,0:T(8,128)(2,1)S(1)}, u32[]{:S(2)}, u32[]{:S(2)}) collective-permute-start(bf16[1,336,512]{2,1,0:T(8,128)(2,1)S(1)} %get-tuple-element.158), channel_id=1, source_target_pairs={{0,2},{1,3},{2,0},{3,1},{4,6},{5,7},{6,4},{7,5},{8,10},{9,11},{10,... | collective-permute-start | bytes 1032200 | tf_op jit(solution)/shard_map/grad_two/ppermute | solution.py:502
  78.7 5.3 %input_early.1 = (f32[1024,512]{1,0:T(8,128)S(1)}, f32[1024,512]{1,0:T(8,128)S(1)}) custom-call(bf16[32,2048]{1,0:T(8,128)(2,1)S(1)} %get-tuple-element.136.refs_13_.dgate_ref, bf16[2,16,512]{2,1,0:T(8,128)(2,1)S(1)} %bitcast.10, bf16[1,256,2048]{2,1,0:T(8,128)(2,1)S(1)} %get-tuple-element.145.refs_0_, ...), custom_call_target="tpu_custom_call" | custom-call | flops 1800000000 | tf_op jit(solution)/shard_map/input_early/pallas_call | solution.py:55
  84.0 3.0 %collective-permute-start.23 = (f32[48,512]{1,0:T(8,128)S(1)}, f32[48,512]{1,0:T(8,128)S(1)}, u32[]{:S(2)}, u32[]{:S(2)}) collective-permute-start(f32[48,512]{1,0:T(8,128)S(1)} %add.10.refs_14_.refs_6_.refs_0_), channel_id=1, source_target_pairs={{0,8},{1,9},{2,10},{3,11},{4,12},{5,13},{6,14},{7,15},{8,0},{9,1},... | collective-permute-start | bytes 294920 | tf_op jit(solution)/shard_map/shared_3/ppermute | solution.py:502
  87.0 2.8 %backward_01.1 = (f32[1,336,512]{2,1,0:T(8,128)S(1)}, f32[1,336,512]{2,1,0:T(8,128)S(1)}, bf16[1,256,2048]{2,1,0:T(8,128)(2,1)S(1)}, bf16[1,256,2048]{2,1,0:T(8,128)(2,1)S(1)}) custom-call(bf16[2048,512]{1,0:T(8,128)(2,1)S(1)} %get-tuple-element.93.x_ref.refs_0_.refs_1_, bf16[1,336,512]{2,1,0:T(8,128)(2,1)S(1)} %hold.3.pay_a.refs_1_.refs_2_, ...), custom_call_target="tpu_custom_call" | custom-call | flops 1500000000 | tf_op jit(solution)/shard_map/backward_01/pallas_call | solution.py:55
  89.8 1.9 %input_late.1 = (f32[1024,512]{1,0:T(8,128)S(1)}, bf16[1024,512]{1,0:T(8,128)(2,1)S(1)}) custom-call(bf16[1,256,2048]{2,1,0:T(8,128)(2,1)S(1)} %get-tuple-element.152.refs_0_, bf16[1,256,2048]{2,1,0:T(8,128)(2,1)S(1)} %get-tuple-element.153.refs_1_, bf16[1,336,512]{2,1,0:T(8,128)(2,1)S(1)} %hold.3.pay_a.refs_1_.refs_2_, ...), custom_call_target="tpu_custom_call" | custom-call | flops 750000000 | tf_op jit(solution)/shard_map/input_late/pallas_call | solution.py:55
  91.9 1.3 %collective-permute-start.22 = (bf16[1,336,512]{2,1,0:T(8,128)(2,1)S(1)}, bf16[1,336,512]{2,1,0:T(8,128)(2,1)S(1)}, u32[]{:S(2)}, u32[]{:S(2)}) collective-permute-start(bf16[1,336,512]{2,1,0:T(8,128)(2,1)S(1)} %get-tuple-element.162.refs_2_), channel_id=1, source_target_pairs={{8,0},{9,1},{10,2},{11,3},{12,4},{13,5},{14,6},{15,7},{16,24},{17,... | collective-permute-start | bytes 1032200 | tf_op jit(solution)/shard_map/far/ppermute | solution.py:502
  93.3 3.8 %collective-permute-start.21 = (bf16[1,336,512]{2,1,0:T(8,128)(2,1)S(1)}, bf16[1,336,512]{2,1,0:T(8,128)(2,1)S(1)}, u32[]{:S(2)}, u32[]{:S(2)}) collective-permute-start(bf16[1,336,512]{2,1,0:T(8,128)(2,1)S(1)} %add.12), channel_id=1, source_target_pairs={{0,4},{1,5},{2,6},{3,7},{4,0},{5,1},{6,2},{7,3},{24,28},{25,29},{2... | collective-permute-start | bytes 1032200 | tf_op jit(solution)/shard_map/near/ppermute | solution.py:502
  97.1 1.3 %collective-permute-start.20 = (bf16[1,336,512]{2,1,0:T(8,128)(2,1)S(1)}, bf16[1,336,512]{2,1,0:T(8,128)(2,1)S(1)}, u32[]{:S(2)}, u32[]{:S(2)}) collective-permute-start(bf16[1,336,512]{2,1,0:T(8,128)(2,1)S(1)} %add.12), channel_id=1, source_target_pairs={{8,4},{9,5},{10,6},{11,7},{12,0},{13,1},{14,2},{15,3},{16,28},{17,... | collective-permute-start | bytes 1032200 | tf_op jit(solution)/shard_map/cross/ppermute | solution.py:502
  98.5 2.1 %collective-permute-start.24 = (f32[48,512]{1,0:T(8,128)S(1)}, f32[48,512]{1,0:T(8,128)S(1)}, u32[]{:S(2)}, u32[]{:S(2)}) collective-permute-start(f32[48,512]{1,0:T(8,128)S(1)} %add.13.refs_0_), channel_id=1, source_target_pairs={{0,2},{1,3},{2,0},{3,1},{4,6},{5,7},{6,4},{7,5},{8,10},{9,11},{10,... | collective-permute-start | bytes 294920 | tf_op jit(solution)/shard_map/shared_1/ppermute | solution.py:502
  100.5 3.3 %collective-permute-done.24.refs_1_ = f32[48,512]{1,0:T(8,128)S(1)} collective-permute-done((f32[48,512]{1,0:T(8,128)S(1)}, f32[48,512]{1,0:T(8,128)S(1)}, u32[]{:S(2)}, u32[]{:S(2)}) %collective-permute-start.24) | collective-permute-done | bytes 98336 | tf_op jit(solution)/shard_map/shared_1/ppermute | solution.py:502
  103.8 1.6 %collective-permute-start.25 = (f32[48,512]{1,0:T(8,128)S(1)}, f32[48,512]{1,0:T(8,128)S(1)}, u32[]{:S(2)}, u32[]{:S(2)}) collective-permute-start(f32[48,512]{1,0:T(8,128)S(1)} %add.14.refs_0_), channel_id=1, source_target_pairs={{0,1},{1,0},{2,3},{3,2},{4,5},{5,4},{6,7},{7,6},{8,9},{9,8},{10,11... | collective-permute-start | bytes 294920 | tf_op jit(solution)/shard_map/shared_0/ppermute | solution.py:502
  105.4 3.1 %collective-permute-done.25.refs_1_ = f32[48,512]{1,0:T(8,128)S(1)} collective-permute-done((f32[48,512]{1,0:T(8,128)S(1)}, f32[48,512]{1,0:T(8,128)S(1)}, u32[]{:S(2)}, u32[]{:S(2)}) %collective-permute-start.25) | collective-permute-done | bytes 98336 | tf_op jit(solution)/shard_map/shared_0/ppermute | solution.py:502
  108.6 1.3 %collective-permute-done.26.give_ref = f32[48,512]{1,0:T(8,128)S(1)} collective-permute-done((f32[48,512]{1,0:T(8,128)S(1)}, f32[48,512]{1,0:T(8,128)S(1)}, u32[]{:S(2)}, u32[]{:S(2)}) %collective-permute-start.26) | collective-permute-done | bytes 98336 | tf_op jit(solution)/shard_map/keep/ppermute | solution.py:506
  109.9 1.3 %close.1 = (f32[2,16,512]{2,1,0:T(8,128)}, f32[2,16]{1,0:T(2,128)}, f32[2,64,128]{2,1,0:T(8,128)}, f32[2,64]{1,0:T(2,128)}, f32[2,64]{1,0:T(2,128)}, /*index=5*/f32[1,2]{1,0:T(1,128)}, f32[8,128]{1,0:T(8,128)S(1)}) custom-call(s32[35]{0:T(128)S(1)} %concatenate.3.int_ref.refs_0_.spot_ref.owner_ref, f32[48,512]{1,0:T(8,128)S(1)} %add.15.keep_ref, ...), custom_call_target="tpu_custom_call" | custom-call | flops 300000000 | tf_op jit(solution)/shard_map/close/pallas_call | solution.py:55
  111.6 1.5 %input_sum.1 = f32[1024,512]{1,0:T(8,128)} custom-call(f32[1024,512]{1,0:T(8,128)S(1)} %get-tuple-element.155.refs_2_.refs_0_, bf16[1024,512]{1,0:T(8,128)(2,1)S(1)} %collective-permute-done.17.refs_1_, f32[1,336,512]{2,1,0:T(8,128)S(1)} %add.16.refs_2_.mine_ref), custom_call_target="tpu_custom_call" | custom-call | flops 450000000 | tf_op jit(solution)/shard_map/input_sum/pallas_call | solution.py:55
  113.6 1.6 %finish.1 = (f32[1,512,256]{2,1,0:T(8,128)}, f32[1,256]{1,0:T(1,128)}, f32[1,256,128]{2,1,0:T(8,128)}, f32[1,128]{1,0:T(1,128)}) custom-call(s32[35]{0:T(128)S(1)} %concatenate.3.int_ref.refs_0_.spot_ref.owner_ref, f32[1,336,512]{2,1,0:T(8,128)S(1)} %add.16.refs_2_.mine_ref, f32[1,336,512]{2,1,0:T(8,128)S(1)} %collective-permute-done.27.come_ref), custom_call_target="tpu_custom_call" | custom-call | flops 3000000000 | tf_op jit(solution)/shard_map/finish/pallas_call | solution.py:55
  (57 shorter events, 3.7 us)
Async XLA Ops:
  0.6 6.8 %collective-permute-start.1 = (bf16[1024,512]{1,0:T(8,128)(2,1)}, bf16[1024,512]{1,0:T(8,128)(2,1)S(1)}, u32[]{:S(2)}, u32[]{:S(2)}) collective-permute-start(bf16[1024,512]{1,0:T(8,128)(2,1)} %mine_ref.1), channel_id=1, source_target_pairs={{0,16},{16,0},{1,17},{17,1},{2,18},{18,2},{3,19},{19,3},{4,20},{20... | collective-permute-start | bytes 3145736 | tf_op jit(solution)/shard_map/inputs/ppermute | solution.py:506
  2.4 10.7 %collective-permute-start.2 = (bf16[1,336,512]{2,1,0:T(8,128)(2,1)S(1)}, bf16[1,336,512]{2,1,0:T(8,128)(2,1)S(1)}, u32[]{:S(2)}, u32[]{:S(2)}) collective-permute-start(bf16[1,336,512]{2,1,0:T(8,128)(2,1)S(1)} %pack.1), channel_id=1, source_target_pairs={{0,8},{1,9},{2,10},{3,11},{4,12},{5,13},{6,14},{7,15},{8,24},{9,25... | collective-permute-start | bytes 1032200 | tf_op jit(solution)/shard_map/deal/ppermute | solution.py:515
  6.0 1.4 %collective-permute-start = (s32[2,1024]{1,0:T(2,128)}, s32[2,1024]{1,0:T(2,128)S(1)}, u32[]{:S(2)}, u32[]{:S(2)}) collective-permute-start(s32[2,1024]{1,0:T(2,128)} %label_ref.1), channel_id=1, source_target_pairs={{0,16},{16,0},{1,17},{17,1},{2,18},{18,2},{3,19},{19,3},{4,20},{20... | collective-permute-start | bytes 24584 | tf_op jit(solution)/shard_map/labels/ppermute | solution.py:506
  7.4 1.2 %copy-start = (bf16[1024,512]{1,0:T(8,128)(2,1)S(1)}, bf16[1024,512]{1,0:T(8,128)(2,1)}, u32[]{:S(2)}) copy-start(bf16[1024,512]{1,0:T(8,128)(2,1)} %mine_ref.1) | copy-start | bytes 3145732
  8.6 0.8 copy-start.1
  9.4 0.7 copy-start.3
  10.1 0.7 copy-start.4
  13.1 11.5 %collective-permute-start.3 = (bf16[1,336,512]{2,1,0:T(8,128)(2,1)S(1)}, bf16[1,336,512]{2,1,0:T(8,128)(2,1)S(1)}, u32[]{:S(2)}, u32[]{:S(2)}) collective-permute-start(bf16[1,336,512]{2,1,0:T(8,128)(2,1)S(1)} %hold.3.pay_a.refs_1_.refs_2_), channel_id=1, source_target_pairs={{0,4},{1,5},{2,6},{3,7},{4,0},{5,1},{6,2},{7,3},{8,12},{9,13},{10,... | collective-permute-start | bytes 1032200 | tf_op jit(solution)/shard_map/pay_1/ppermute | solution.py:502
  16.0 9.9 %collective-permute-start.5 = (bf16[1,336,512]{2,1,0:T(8,128)(2,1)S(1)}, bf16[1,336,512]{2,1,0:T(8,128)(2,1)S(1)}, u32[]{:S(2)}, u32[]{:S(2)}) collective-permute-start(bf16[1,336,512]{2,1,0:T(8,128)(2,1)S(1)} %hold.3.pay_a.refs_1_.refs_2_), channel_id=1, source_target_pairs={{0,1},{1,0},{2,3},{3,2},{4,5},{5,4},{6,7},{7,6},{8,9},{9,8},{10,11... | collective-permute-start | bytes 1032200 | tf_op jit(solution)/shard_map/pay_4/ppermute | solution.py:502
  17.4 8.4 %collective-permute-start.4 = (bf16[1,336,512]{2,1,0:T(8,128)(2,1)S(1)}, bf16[1,336,512]{2,1,0:T(8,128)(2,1)S(1)}, u32[]{:S(2)}, u32[]{:S(2)}) collective-permute-start(bf16[1,336,512]{2,1,0:T(8,128)(2,1)S(1)} %hold.3.pay_a.refs_1_.refs_2_), channel_id=1, source_target_pairs={{0,2},{1,3},{2,0},{3,1},{4,6},{5,7},{6,4},{7,5},{8,10},{9,11},{10,... | collective-permute-start | bytes 1032200 | tf_op jit(solution)/shard_map/pay_2/ppermute | solution.py:502
  25.8 10.9 %collective-permute-start.6 = (bf16[1,336,512]{2,1,0:T(8,128)(2,1)S(1)}, bf16[1,336,512]{2,1,0:T(8,128)(2,1)S(1)}, u32[]{:S(2)}, u32[]{:S(2)}) collective-permute-start(bf16[1,336,512]{2,1,0:T(8,128)(2,1)S(1)} %hold.4), channel_id=1, source_target_pairs={{0,2},{1,3},{2,0},{3,1},{4,6},{5,7},{6,4},{7,5},{8,10},{9,11},{10,... | collective-permute-start | bytes 1032200 | tf_op jit(solution)/shard_map/pay_3/ppermute | solution.py:502
  26.3 17.0 %collective-permute-start.8 = (bf16[1,336,512]{2,1,0:T(8,128)(2,1)S(1)}, bf16[1,336,512]{2,1,0:T(8,128)(2,1)S(1)}, u32[]{:S(2)}, u32[]{:S(2)}) collective-permute-start(bf16[1,336,512]{2,1,0:T(8,128)(2,1)S(1)} %hold.4), channel_id=1, source_target_pairs={{0,1},{1,0},{2,3},{3,2},{4,5},{5,4},{6,7},{7,6},{8,9},{9,8},{10,11... | collective-permute-start | bytes 1032200 | tf_op jit(solution)/shard_map/pay_5/ppermute | solution.py:502
  27.8 15.5 %collective-permute-start.9 = (bf16[1,336,512]{2,1,0:T(8,128)(2,1)S(1)}, bf16[1,336,512]{2,1,0:T(8,128)(2,1)S(1)}, u32[]{:S(2)}, u32[]{:S(2)}) collective-permute-start(bf16[1,336,512]{2,1,0:T(8,128)(2,1)S(1)} %collective-permute-done.4.refs_1_.pay_b.refs_6_), channel_id=1, source_target_pairs={{0,1},{1,0},{2,3},{3,2},{4,5},{5,4},{6,7},{7,6},{8,9},{9,8},{10,11... | collective-permute-start | bytes 1032200 | tf_op jit(solution)/shard_map/pay_6/ppermute | solution.py:502
  36.8 11.5 %collective-permute-start.7 = (bf16[1,336,512]{2,1,0:T(8,128)(2,1)S(1)}, bf16[1,336,512]{2,1,0:T(8,128)(2,1)S(1)}, u32[]{:S(2)}, u32[]{:S(2)}) collective-permute-start(bf16[1,336,512]{2,1,0:T(8,128)(2,1)S(1)} %hold.5), channel_id=1, source_target_pairs={{0,1},{1,0},{2,3},{3,2},{4,5},{5,4},{6,7},{7,6},{8,9},{9,8},{10,11... | collective-permute-start | bytes 1032200 | tf_op jit(solution)/shard_map/pay_7/ppermute | solution.py:502
  48.3 7.7 %copy-start.5 = (bf16[2,128,64]{1,2,0:T(8,128)(2,1)S(1)}, bf16[2,128,64]{1,2,0:T(8,128)(2,1)}, u32[]{:S(2)}) copy-start(bf16[2,128,64]{1,2,0:T(8,128)(2,1)} %param.21) | copy-start | bytes 98308
  48.3 7.7 %copy-start.6 = (bf16[2]{0:T(256)(128)(2,1)S(1)}, bf16[2]{0:T(256)(128)(2,1)}, u32[]{:S(2)}) copy-start(bf16[2]{0:T(256)(128)(2,1)} %param.24) | copy-start | bytes 16
  48.3 7.7 %copy-start.7 = (bf16[2,64]{1,0:T(2,128)(2,1)S(1)}, bf16[2,64]{1,0:T(2,128)(2,1)}, u32[]{:S(2)}) copy-start(bf16[2,64]{1,0:T(2,128)(2,1)} %tb_ref.1) | copy-start | bytes 772
  48.3 7.7 %copy-start.8 = (bf16[2,64]{1,0:T(2,128)(2,1)S(1)}, bf16[2,64]{1,0:T(2,128)(2,1)}, u32[]{:S(2)}) copy-start(bf16[2,64]{1,0:T(2,128)(2,1)} %tl_ref.1) | copy-start | bytes 772
  53.2 2.7 %collective-permute-start.10 = (bf16[2,128,2048]{2,1,0:T(8,128)(2,1)S(1)}, bf16[2,128,2048]{2,1,0:T(8,128)(2,1)S(1)}, u32[]{:S(2)}, u32[]{:S(2)}) collective-permute-start(bf16[2,128,2048]{2,1,0:T(8,128)(2,1)S(1)} %get-tuple-element.98.mix_ref), channel_id=1, source_target_pairs={{0,16},{16,0},{1,17},{17,1},{2,18},{18,2},{3,19},{19,3},{4,20},{20... | collective-permute-start | bytes 3145736 | tf_op jit(solution)/shard_map/mixed/ppermute | solution.py:506
  62.3 10.4 %collective-permute-start.13 = (bf16[1,336,512]{2,1,0:T(8,128)(2,1)S(1)}, bf16[1,336,512]{2,1,0:T(8,128)(2,1)S(1)}, u32[]{:S(2)}, u32[]{:S(2)}) collective-permute-start(bf16[1,336,512]{2,1,0:T(8,128)(2,1)S(1)} %get-tuple-element.143), channel_id=1, source_target_pairs={{0,1},{1,0},{2,3},{3,2},{4,5},{5,4},{6,7},{7,6},{8,9},{9,8},{10,11... | collective-permute-start | bytes 1032200 | tf_op jit(solution)/shard_map/grad_six/ppermute | solution.py:502
  62.7 10.5 %collective-permute-start.14 = (bf16[1,336,512]{2,1,0:T(8,128)(2,1)S(1)}, bf16[1,336,512]{2,1,0:T(8,128)(2,1)S(1)}, u32[]{:S(2)}, u32[]{:S(2)}) collective-permute-start(bf16[1,336,512]{2,1,0:T(8,128)(2,1)S(1)} %get-tuple-element.144), channel_id=1, source_target_pairs={{0,1},{1,0},{2,3},{3,2},{4,5},{5,4},{6,7},{7,6},{8,9},{9,8},{10,11... | collective-permute-start | bytes 1032200 | tf_op jit(solution)/shard_map/grad_seven/ppermute | solution.py:502
  67.1 19.9 %collective-permute-start.11 = (bf16[1,336,512]{2,1,0:T(8,128)(2,1)S(1)}, bf16[1,336,512]{2,1,0:T(8,128)(2,1)S(1)}, u32[]{:S(2)}, u32[]{:S(2)}) collective-permute-start(bf16[1,336,512]{2,1,0:T(8,128)(2,1)S(1)} %get-tuple-element.122), channel_id=1, source_target_pairs={{0,1},{1,0},{2,3},{3,2},{4,5},{5,4},{6,7},{7,6},{8,9},{9,8},{10,11... | collective-permute-start | bytes 1032200 | tf_op jit(solution)/shard_map/grad_four/ppermute | solution.py:502
  67.6 19.4 %collective-permute-start.12 = (bf16[1,336,512]{2,1,0:T(8,128)(2,1)S(1)}, bf16[1,336,512]{2,1,0:T(8,128)(2,1)S(1)}, u32[]{:S(2)}, u32[]{:S(2)}) collective-permute-start(bf16[1,336,512]{2,1,0:T(8,128)(2,1)S(1)} %get-tuple-element.123), channel_id=1, source_target_pairs={{0,1},{1,0},{2,3},{3,2},{4,5},{5,4},{6,7},{7,6},{8,9},{9,8},{10,11... | collective-permute-start | bytes 1032200 | tf_op jit(solution)/shard_map/grad_five/ppermute | solution.py:502
  72.5 3.6 %collective-permute-start.15 = (f32[48,512]{1,0:T(8,128)S(1)}, f32[48,512]{1,0:T(8,128)S(1)}, u32[]{:S(2)}, u32[]{:S(2)}) collective-permute-start(f32[48,512]{1,0:T(8,128)S(1)} %get-tuple-element.151), channel_id=1, source_target_pairs={{0,16},{16,0},{1,17},{17,1},{2,18},{18,2},{3,19},{19,3},{4,20},{20... | collective-permute-start | bytes 294920 | tf_op jit(solution)/shard_map/give/ppermute | solution.py:506
  73.3 5.4 %copy-start.2 = (bf16[2,512,16]{1,2,0:T(8,128)(2,1)S(1)}, bf16[2,512,16]{1,2,0:T(8,128)(2,1)}, u32[]{:S(2)}) copy-start(bf16[2,512,16]{1,2,0:T(8,128)(2,1)} %param.19) | copy-start | bytes 98308
  76.1 7.8 %collective-permute-start.16 = (f32[48,512]{1,0:T(8,128)S(1)}, f32[48,512]{1,0:T(8,128)S(1)}, u32[]{:S(2)}, u32[]{:S(2)}) collective-permute-start(f32[48,512]{1,0:T(8,128)S(1)} %add.9.refs_0_), channel_id=1, source_target_pairs={{0,4},{1,5},{2,6},{3,7},{4,0},{5,1},{6,2},{7,3},{8,12},{9,13},{10,... | collective-permute-start | bytes 294920 | tf_op jit(solution)/shard_map/shared_2/ppermute | solution.py:502
  76.6 15.2 %collective-permute-start.18 = (bf16[1,336,512]{2,1,0:T(8,128)(2,1)S(1)}, bf16[1,336,512]{2,1,0:T(8,128)(2,1)S(1)}, u32[]{:S(2)}, u32[]{:S(2)}) collective-permute-start(bf16[1,336,512]{2,1,0:T(8,128)(2,1)S(1)} %get-tuple-element.158), channel_id=1, source_target_pairs={{0,2},{1,3},{2,0},{3,1},{4,6},{5,7},{6,4},{7,5},{8,10},{9,11},{10,... | collective-permute-start | bytes 1032200 | tf_op jit(solution)/shard_map/grad_two/ppermute | solution.py:502
  78.4 14.9 %collective-permute-start.19 = (bf16[1,336,512]{2,1,0:T(8,128)(2,1)S(1)}, bf16[1,336,512]{2,1,0:T(8,128)(2,1)S(1)}, u32[]{:S(2)}, u32[]{:S(2)}) collective-permute-start(bf16[1,336,512]{2,1,0:T(8,128)(2,1)S(1)} %get-tuple-element.161), channel_id=1, source_target_pairs={{0,2},{1,3},{2,0},{3,1},{4,6},{5,7},{6,4},{7,5},{8,10},{9,11},{10,... | collective-permute-start | bytes 1032200 | tf_op jit(solution)/shard_map/grad_three/ppermute | solution.py:502
  84.0 14.4 %collective-permute-start.23 = (f32[48,512]{1,0:T(8,128)S(1)}, f32[48,512]{1,0:T(8,128)S(1)}, u32[]{:S(2)}, u32[]{:S(2)}) collective-permute-start(f32[48,512]{1,0:T(8,128)S(1)} %add.10.refs_14_.refs_6_.refs_0_), channel_id=1, source_target_pairs={{0,8},{1,9},{2,10},{3,11},{4,12},{5,13},{6,14},{7,15},{8,0},{9,1},... | collective-permute-start | bytes 294920 | tf_op jit(solution)/shard_map/shared_3/ppermute | solution.py:502
  91.7 19.9 %collective-permute-start.17 = (bf16[1024,512]{1,0:T(8,128)(2,1)S(1)}, bf16[1024,512]{1,0:T(8,128)(2,1)S(1)}, u32[]{:S(2)}, u32[]{:S(2)}) collective-permute-start(bf16[1024,512]{1,0:T(8,128)(2,1)S(1)} %get-tuple-element.156), channel_id=1, source_target_pairs={{0,16},{16,0},{1,17},{17,1},{2,18},{18,2},{3,19},{19,3},{4,20},{20... | collective-permute-start | bytes 3145736 | tf_op jit(solution)/shard_map/over/ppermute | solution.py:506
  91.9 19.3 %collective-permute-start.22 = (bf16[1,336,512]{2,1,0:T(8,128)(2,1)S(1)}, bf16[1,336,512]{2,1,0:T(8,128)(2,1)S(1)}, u32[]{:S(2)}, u32[]{:S(2)}) collective-permute-start(bf16[1,336,512]{2,1,0:T(8,128)(2,1)S(1)} %get-tuple-element.162.refs_2_), channel_id=1, source_target_pairs={{8,0},{9,1},{10,2},{11,3},{12,4},{13,5},{14,6},{15,7},{16,24},{17,... | collective-permute-start | bytes 1032200 | tf_op jit(solution)/shard_map/far/ppermute | solution.py:502
  93.3 17.9 %collective-permute-start.21 = (bf16[1,336,512]{2,1,0:T(8,128)(2,1)S(1)}, bf16[1,336,512]{2,1,0:T(8,128)(2,1)S(1)}, u32[]{:S(2)}, u32[]{:S(2)}) collective-permute-start(bf16[1,336,512]{2,1,0:T(8,128)(2,1)S(1)} %add.12), channel_id=1, source_target_pairs={{0,4},{1,5},{2,6},{3,7},{4,0},{5,1},{6,2},{7,3},{24,28},{25,29},{2... | collective-permute-start | bytes 1032200 | tf_op jit(solution)/shard_map/near/ppermute | solution.py:502
  97.1 14.1 %collective-permute-start.20 = (bf16[1,336,512]{2,1,0:T(8,128)(2,1)S(1)}, bf16[1,336,512]{2,1,0:T(8,128)(2,1)S(1)}, u32[]{:S(2)}, u32[]{:S(2)}) collective-permute-start(bf16[1,336,512]{2,1,0:T(8,128)(2,1)S(1)} %add.12), channel_id=1, source_target_pairs={{8,4},{9,5},{10,6},{11,7},{12,0},{13,1},{14,2},{15,3},{16,28},{17,... | collective-permute-start | bytes 1032200 | tf_op jit(solution)/shard_map/cross/ppermute | solution.py:502
  98.5 5.3 %collective-permute-start.24 = (f32[48,512]{1,0:T(8,128)S(1)}, f32[48,512]{1,0:T(8,128)S(1)}, u32[]{:S(2)}, u32[]{:S(2)}) collective-permute-start(f32[48,512]{1,0:T(8,128)S(1)} %add.13.refs_0_), channel_id=1, source_target_pairs={{0,2},{1,3},{2,0},{3,1},{4,6},{5,7},{6,4},{7,5},{8,10},{9,11},{10,... | collective-permute-start | bytes 294920 | tf_op jit(solution)/shard_map/shared_1/ppermute | solution.py:502
  103.8 4.7 %collective-permute-start.25 = (f32[48,512]{1,0:T(8,128)S(1)}, f32[48,512]{1,0:T(8,128)S(1)}, u32[]{:S(2)}, u32[]{:S(2)}) collective-permute-start(f32[48,512]{1,0:T(8,128)S(1)} %add.14.refs_0_), channel_id=1, source_target_pairs={{0,1},{1,0},{2,3},{3,2},{4,5},{5,4},{6,7},{7,6},{8,9},{9,8},{10,11... | collective-permute-start | bytes 294920 | tf_op jit(solution)/shard_map/shared_0/ppermute | solution.py:502
  108.5 1.4 %collective-permute-start.26 = (f32[48,512]{1,0:T(8,128)S(1)}, f32[48,512]{1,0:T(8,128)S(1)}, u32[]{:S(2)}, u32[]{:S(2)}) collective-permute-start(f32[48,512]{1,0:T(8,128)S(1)} %add.15.keep_ref), channel_id=1, source_target_pairs={{0,16},{16,0},{1,17},{17,1},{2,18},{18,2},{3,19},{19,3},{4,20},{20... | collective-permute-start | bytes 294920 | tf_op jit(solution)/shard_map/keep/ppermute | solution.py:506
  111.4 2.2 %collective-permute-start.27 = (f32[1,336,512]{2,1,0:T(8,128)S(1)}, f32[1,336,512]{2,1,0:T(8,128)S(1)}, u32[]{:S(2)}, u32[]{:S(2)}) collective-permute-start(f32[1,336,512]{2,1,0:T(8,128)S(1)} %add.16.refs_2_.mine_ref), channel_id=1, source_target_pairs={{0,16},{16,0},{1,17},{17,1},{2,18},{18,2},{3,19},{19,3},{4,20},{20... | collective-permute-start | bytes 2064392 | tf_op jit(solution)/shard_map/final/ppermute | solution.py:506
where the time goes:
time: 116 us; the launch traced here: 115 us
  Pallas kernels  53.3 us (46%)
  starting transfers between devices  34.4 us (30%)
  waiting for transfers between devices  22.3 us (19%)
  local copies, waits for them, and re-layouts  4.15 us (4%)
    pallas_call x23, Pallas kernels, call(): pl.pallas_call(body, name=name, in_specs=[SMEM] * scalars + [VMEM] * (cou...  49.8 us
    ppermute x20, starting transfers between devices, send(): return lax.ppermute(value, ('dp', 'expert'), pairs(bit_of_core, want, also))  29.7 us
    ppermute x20, waiting for transfers between devices, send(): return lax.ppermute(value, ('dp', 'expert'), pairs(bit_of_core, want, also))  17.2 us
    ppermute x7, waiting for transfers between devices, swap(): return lax.ppermute(value, 'dp', [(0, 1), (1, 0)])  5.07 us
    ppermute x1, starting transfers between devices, deal(): return lax.ppermute(value, ('dp', 'expert'), route)  3.66 us
    unnamed x20, local copies, waits for them, and re-layouts  3.41 us
  transfers between devices with their start and end apart: 28, of which 10 were waited for; matrix products, arithmetic and copies ran while one was open for 1% of the time, Pallas kernels for 35%

commit v1 on v0

--- a/solution.py
+++ b/solution.py
@@ -20,7 +20,8 @@
 EARLY = 6
 BACK_CHUNK = 2048
 TAIL = 10
-PAIRS = ((0, 4), (1, 2), (5, 6), (3, 7))
+GROUPS = ((0,), (1, 4), (2,), (3, 5), (6, 7))
+LAST_ASK = 2
 PAY_ROWS = 320 + BIAS_ROWS
 VMEM = pl.BlockSpec(memory_space=pltpu.VMEM)
 SMEM = pl.BlockSpec(memory_space=pltpu.SMEM)
@@ -190,17 +191,19 @@
             low_ref[j, t : t + 1, :] = row.astype(BF16).astype(F32)
 
 
-def forward_kernel(bundles, first, block, chunk, x_ref, pay_a, pay_b, low_ref, *refs):
+def forward_kernel(bundles, first, block, chunk, x_ref, low_ref, *refs):
+    count = len(bundles)
+    pays, refs = refs[:count], refs[count:]
     if not first:
         mix_in, *refs = refs
-    kept, mix_ref = (refs[:4], refs[4:8]), refs[8]
-    depth = pay_a.shape[0]
+    kept, mix_ref = [refs[4 * n : 4 * n + 4] for n in range(count)], refs[4 * count]
+    depth = pays[0].shape[0]
     weights = {}
     for k in range(depth):
-        for n, pay_ref in enumerate((pay_a, pay_b)):
+        for n, pay_ref in enumerate(pays):
             pay = pay_ref[k]
             weights[k, n] = (pay[:256], second_weight(pay), *biases(pay))
-    work = [(c, k, n) for c in range(0, block, chunk) for k in range(depth) for n in range(2)]
+    work = [(c, k, n) for c in range(0, block, chunk) for k in range(depth) for n in range(count)]
 
     def step(i, _):
         base = pl.multiple_of(i * block, block)
@@ -229,7 +232,7 @@
                     totals[t] = term if first else mix_in[t, :, at] + term
                 else:
                     totals[t] = totals[t] + term
-                if k == depth - 1 and n == 1:
+                if k == depth - 1 and n == count - 1:
                     mix_ref[t, :, at] = totals[t].astype(mix_ref.dtype)
 
         ones, twos = {0: layer_one(*work[0])}, {}
@@ -379,42 +382,21 @@
             grads[n][k, 320:, :] = both.astype(grads[n].dtype)
 
 
-def input_kernel(bundles, chunk, dgate_ref, gw_ref, *refs):
+def input_kernel(side, chunk, dgate_ref, gw_ref, *refs):
     experts = gw_ref.shape[1]
-    count = len(bundles)
-    ones, pays, outs = refs[:count], refs[count : 2 * count], refs[2 * count :]
-    for side, out_ref in enumerate(outs):
-        rows = out_ref.shape[0]
-
-        def step(i, _, side=side, rows=rows, out_ref=out_ref):
-            at = pl.ds(pl.multiple_of(side * rows + i * chunk, chunk), chunk)
-            total = dot(dgate_ref[:experts, at], gw_ref[0], TN) + dot(dgate_ref[experts:, at], gw_ref[1], TN)
-            for one, pay in zip(ones, pays):
-                for k in range(one.shape[0]):
-                    total = total + dot(one[k, :, at], pay[k, :256, :], TN)
-            out_ref[pl.ds(pl.multiple_of(i * chunk, chunk), chunk), :] = total
-            return 0
-
-        lax.fori_loop(0, rows // chunk, step, 0)
-
-
-def input_rest_kernel(bundles, chunk, *refs):
-    count = len(bundles)
-    ones, pays, befores, outs = refs[:count], refs[count : 2 * count], refs[2 * count : 2 * count + 2], refs[-2:]
-    for side, (before, out_ref) in enumerate(zip(befores, outs)):
-        rows = out_ref.shape[0]
-
-        def step(i, _, side=side, rows=rows, before=before, out_ref=out_ref):
-            at = pl.ds(pl.multiple_of(side * rows + i * chunk, chunk), chunk)
-            here = pl.ds(pl.multiple_of(i * chunk, chunk), chunk)
-            total = before[here, :]
-            for one, pay in zip(ones, pays):
-                for k in range(one.shape[0]):
-                    total = total + dot(one[k, :, at], pay[k, :256, :], TN)
-            out_ref[here, :] = total.astype(out_ref.dtype)
-            return 0
-
-        lax.fori_loop(0, rows // chunk, step, 0)
+    ones, pays, out_ref = refs[:8], refs[8:16], refs[16]
+    rows = out_ref.shape[0]
+
+    def step(i, _):
+        at = pl.ds(pl.multiple_of(side * rows + i * chunk, chunk), chunk)
+        total = dot(dgate_ref[:experts, at], gw_ref[0], TN) + dot(dgate_ref[experts:, at], gw_ref[1], TN)
+        for one, pay in zip(ones, pays):
+            for k in range(one.shape[0]):
+                total = total + dot(one[k, :, at], pay[k, :256, :], TN)
+        out_ref[pl.ds(pl.multiple_of(i * chunk, chunk), chunk), :] = total.astype(out_ref.dtype)
+        return 0
+
+    lax.fori_loop(0, rows // chunk, step, 0)
 
 
 def add_kernel(count, *refs):
@@ -423,6 +405,11 @@
         total = total + ref[...].astype(F32)
     for ref in refs[count:]:
         ref[...] = total.astype(ref.dtype)
+
+
+def input_sum_kernel(own_ref, come_ref, out_ref, done_ref):
+    out_ref[...] = own_ref[...] + come_ref[...].astype(F32)
+    done_ref[...] = jnp.zeros_like(done_ref)
 
 
 def finish_kernel(owner_ref, mine_ref, come_ref, w1_ref, b1_ref, w2_ref, b2_ref):
@@ -524,8 +511,15 @@
     masks = [[expert_mask(c, j) for j in range(half)] for c in range(2)]
     spot = jnp.stack([core, place, owner.astype(jnp.int32)]).astype(jnp.int32)
 
+    def add(values, dtypes, after=()):
+        shape = values[0].shape
+        outs = [(shape, dtype, True) for dtype in dtypes]
+        return call("add", functools.partial(add_kernel, len(values)), values, outs, pin, 0, after=after)
+
     pay = pack(w_first, w_second, b_first, b_second)
     zero = deal(pay)
+    if not extra:
+        owners_near = send("owners_near", pay, near_bit, True)
     for at in extra:
         zero = jnp.concatenate([zero, send("pay_extra", zero, at)], axis=0)
     labels_there = swap("labels", labels)
@@ -546,30 +540,36 @@
     )(ints, labels, labels_there, gate_rows, gate_bias, inputs, inputs_there)
 
     pays = [hold(zero, [low])] + [None] * 7
-    pays[1] = send("pay_1", pays[0], near_bit)
+    pays[1] = send("pay_1", pays[0], near_bit, None if extra else False)
     pays[2] = send("pay_2", pays[0], mid_bit)
     pays[4] = send("pay_4", pays[0], end_bit)
-    held = hold(pays[1], [pays[2], pays[4]])
-    pays[3] = send("pay_3", held, mid_bit)
-    pays[5] = send("pay_5", held, end_bit)
-    pays[6] = send("pay_6", pays[2], end_bit)
-
     mixed = None
     saved = [None] * 8
     slope_type = F32 if pin else BF16
-    for a, b in PAIRS:
+    for group in GROUPS:
         shape = lambda deep, dtype: ((depth, deep, 2 * rows), dtype, True)
         *kept, mixed = call(
-            f"forward_{a}{b}",
-            functools.partial(forward_kernel, (a, b), mixed is None, 4 * chunk, chunk),
-            [x, pays[a], pays[b], low] + ([] if mixed is None else [mixed]),
-            [shape(256, BF16), shape(256, BF16), shape(128, BF16), shape(128, slope_type)] * 2
-            + [((2, 128, 2 * rows), BF16 if (a, b) == PAIRS[-1] else F32, True)],
+            "forward_" + "".join(str(n) for n in group),
+            functools.partial(forward_kernel, group, mixed is None, 4 * chunk, chunk),
+            [x, low] + [pays[n] for n in group] + ([] if mixed is None else [mixed]),
+            [shape(256, BF16), shape(256, BF16), shape(128, BF16), shape(128, slope_type)] * len(group)
+            + [((2, 128, 2 * rows), BF16 if group == GROUPS[-1] else F32, True)],
             pin,
-            4.5 * depth,
+            2.25 * len(group) * depth,
         )
-        saved[a], saved[b] = kept[:4], kept[4:]
-        if pays[7] is None:
+        for n, bundle in enumerate(group):
+            saved[bundle] = kept[4 * n : 4 * n + 4]
+        if group == GROUPS[0]:
+            if extra:
+                held = hold(pays[1], [pays[2], pays[4], mixed])
+            else:
+                pays[2] = hold(pays[2], [pays[4], owners_near, mixed])
+                (pays[1],) = add([owners_near, pays[1]], [BF16], [pays[2]])
+                held = pays[1]
+            pays[3] = send("pay_3", held, mid_bit)
+            pays[5] = send("pay_5", held, end_bit)
+            pays[6] = send("pay_6", pays[2], end_bit)
+        if group == GROUPS[LAST_ASK]:
             pays[7] = send("pay_7", hold(pays[3], [mixed]), end_bit)
 
     predictions, dmix, centre, tower_sums = call(
@@ -621,42 +621,31 @@
         1,
         after=[ones[5]],
     )
-    grad_two, grad_three, ones[2], ones[3] = back(2, 3, (six, seven), BF16, 1, [dgate])
+    (keep,) = add([keep, swap("give", give)], [F32])
+    grad_two, grad_three, ones[2], ones[3] = back(2, 3, (six, seven), BF16, 1, [keep])
     three, two = send("grad_three", grad_three, mid_bit), send("grad_two", grad_two, mid_bit)
-    halves = [((rows, 512), F32, True)] * 2
-    early, late = (2, 3, 4, 5, 6, 7), (0, 1)
-    parts = call(
-        "input_early",
-        functools.partial(input_kernel, early, 512),
-        [dgate, gate_rows] + [ones[n] for n in early] + [pays[n] for n in early],
-        halves,
-        pin,
-        EARLY * depth,
-    )
-    def add(values, dtypes, after=()):
-        shape = values[0].shape
-        outs = [(shape, dtype, True) for dtype in dtypes]
-        return call("add", functools.partial(add_kernel, len(values)), values, outs, pin, 0, after=after)
-
-    (keep,) = add([keep, swap("give", give)], [F32], [ones[3]])
     stages = []
     for b in range(2, bits):
-        (keep,) = add([keep, send(f"shared_{b}", keep, (b, b))], [F32])
+        (keep,) = add([keep, send(f"shared_{b}", keep, (b, b))], [F32], [ones[3]])
         stages.append(keep)
 
-    grad_zero, grad_one, ones[0], ones[1] = back(0, 1, (four, five), F32, 5, [parts[0], stages[0]])
-    own, over = call(
-        "input_late",
-        functools.partial(input_rest_kernel, late, 512),
-        [ones[n] for n in late] + [pays[n] for n in late] + list(parts),
-        [((rows, 512), F32, True), ((rows, 512), BF16, True)],
-        pin,
-        2.5 * depth,
-        after=[stages[0]],
-    )
-
+    grad_zero, grad_one, ones[0], ones[1] = back(0, 1, (four, five), F32, 1, [ones[3], stages[0]])
+    def input_gradient(side, dtype, after=()):
+        (out,) = call(
+            f"input_{side}",
+            functools.partial(input_kernel, side, 512),
+            [dgate, gate_rows, *ones, *pays],
+            [((rows, 512), dtype, True)],
+            pin,
+            3.5 * depth,
+            after=after,
+        )
+        return out
+
+    over = input_gradient(1, BF16, [stages[1]])
+    own = input_gradient(0, F32)
     top = bits - 1
-    (one,) = add([grad_one, three], [BF16])
+    (one,) = add([grad_one, three], [BF16], [over])
     if extra:
         (zero,) = add([grad_zero, two, send("near", one, near_bit)], [F32])
         for at in reversed(extra):
@@ -665,10 +654,10 @@
         low_zero = zero.astype(BF16)
         pieces = []
     else:
-        pieces = [send("cross", one, (top, top), False, 1 << near_bit[0]), send("near", one, near_bit, True)]
-        zero, low_zero = add([grad_zero, two], [F32, BF16], [own])
+        pieces = [send("near", one, near_bit, True), send("cross", one, (top, top), False, 1 << near_bit[0])]
+        zero, low_zero = add([grad_zero, two], [F32, BF16])
     pieces = [zero, *pieces, send("far", low_zero, (top, top), False)]
-    (keep,) = add([keep, send("shared_1", keep, (1, 1))], [F32], [low_zero])
+    (keep,) = add([keep, send("shared_1", keep, (1, 1))], [F32], [low_zero, own])
     (keep,) = add([keep, send("shared_0", keep, (0, 0))], [F32])
     give = swap("keep", keep)
     grad_gate, grad_gate_bias, tower_first, tower_bias, last, out_bias, done = call(
@@ -689,13 +678,13 @@
         [pltpu.VMEM((2 * deep, 512), F32)],
         1,
     )
-    (final,) = add(pieces, [F32], [done])
-
-    (input_grad,) = call(
+    (final,) = add(pieces, [F32], [done, own])
+
+    input_grad, summed = call(
         "input_sum",
-        functools.partial(add_kernel, 2),
+        input_sum_kernel,
         [own, swap("over", over)],
-        [((rows, 512), F32, False)],
+        [((rows, 512), F32, False), ((8, 128), F32, True)],
         pin,
         1.5,
         after=[final],
@@ -713,6 +702,7 @@
         pin,
         TAIL,
         scalars=1,
+        after=[summed],
     )
     return (
         predictions,

time: 116 us -> 112 us (0.966)
  waiting for transfers between devices: 22.3 us -> 18.5 us
    ppermute x20 -> x21, waiting for transfers between devices: 17.2 us -> 13 us  [send(): return lax.ppermute(value, ('dp', 'expert'), pairs(bit_of_core, want, also))]
    pallas_call x23 -> x25, Pallas kernels: 49.8 us -> 49.6 us  [call(): pl.pallas_call(body, name=name, in_specs=[SMEM] * scalars + [VMEM] * (cou...]
    ppermute x20 -> x21, starting transfers between devices: 29.7 us -> 29.6 us  [send(): return lax.ppermute(value, ('dp', 'expert'), pairs(bit_of_core, want, also))]
    unnamed x20 -> x19, local copies, waits for them, and re-layouts: 3.41 us -> 3.37 us
  transfers between devices with their start and end apart: 28 -> 29, of which waited for: 10 -> 11; matrix products, arithmetic and copies ran while one was open for 1% -> 1% of each run, Pallas kernels for 35% -> 36%
where the time goes in v1:
time: 112 us; the launch traced here: 111 us
  Pallas kernels  53.1 us (47%)
  starting transfers between devices  34.7 us (31%)
  waiting for transfers between devices  18.5 us (17%)
  local copies, waits for them, and re-layouts  4.12 us (4%)
    pallas_call x25, Pallas kernels, call(): pl.pallas_call(body, name=name, in_specs=[SMEM] * scalars + [VMEM] * (cou...  49.6 us
    ppermute x21, starting transfers between devices, send(): return lax.ppermute(value, ('dp', 'expert'), pairs(bit_of_core, want, also))  29.6 us
    ppermute x21, waiting for transfers between devices, send(): return lax.ppermute(value, ('dp', 'expert'), pairs(bit_of_core, want, also))  13 us
    ppermute x7, waiting for transfers between devices, swap(): return lax.ppermute(value, 'dp', [(0, 1), (1, 0)])  5.52 us
    ppermute x1, starting transfers between devices, deal(): return lax.ppermute(value, ('dp', 'expert'), route)  3.66 us
    unnamed x19, local copies, waits for them, and re-layouts  3.37 us
    pallas_call x1, Pallas kernels, per_device(): pl.pallas_call(functools.partial(gate_kernel, masks, group_len.shape[0]),...  2.26 us
  transfers between devices with their start and end apart: 29, of which 11 were waited for; matrix products, arithmetic and copies ran while one was open for 1% of the time, Pallas kernels for 36%

profile of v1, /device:TPU:0, one launch (start us, length us, event | category | flops | bytes accessed | tf_op | source)
XLA Modules:
  0.0 111.4 jit_solution(12085043096551549962)
XLA Ops:
  1.2 1.2 %pack.1 = bf16[1,336,512]{2,1,0:T(8,128)(2,1)S(1)} custom-call(bf16[1,512,256]{2,1,0:T(8,128)(2,1)} %w1_ref.1, bf16[1,256,128]{2,1,0:T(8,128)(2,1)} %w2_ref.1, bf16[1,256]{1,0:T(2,128)(2,1)} %b1_ref.1, bf16[1,128]{1,0:T(2,128)(2,1)} %b2_ref.1), custom_call_target="tpu_custom_call" | custom-call | tf_op jit(solution)/shard_map/pack/pallas_call | solution.py:134
  2.4 3.7 %collective-permute-start.2 = (bf16[1,336,512]{2,1,0:T(8,128)(2,1)S(1)}, bf16[1,336,512]{2,1,0:T(8,128)(2,1)S(1)}, u32[]{:S(2)}, u32[]{:S(2)}) collective-permute-start(bf16[1,336,512]{2,1,0:T(8,128)(2,1)S(1)} %pack.1), channel_id=1, source_target_pairs={{0,8},{1,9},{2,10},{3,11},{4,12},{5,13},{6,14},{7,15},{8,24},{9,25... | collective-permute-start | bytes 1032200 | tf_op jit(solution)/shard_map/deal/ppermute | solution.py:502
  6.0 3.5 %collective-permute-start.5 = (bf16[1,336,512]{2,1,0:T(8,128)(2,1)S(1)}, bf16[1,336,512]{2,1,0:T(8,128)(2,1)S(1)}, u32[]{:S(2)}, u32[]{:S(2)}) collective-permute-start(bf16[1,336,512]{2,1,0:T(8,128)(2,1)S(1)} %pack.1), channel_id=1, source_target_pairs={{0,4},{1,5},{2,6},{3,7},{4,0},{5,1},{6,2},{7,3},{24,28},{25,29},{2... | collective-permute-start | bytes 1032200 | tf_op jit(solution)/shard_map/owners_near/ppermute | solution.py:489
  9.5 0.7 concatenate.3.int_ref.refs_0_.spot_ref
  10.3 1.2 %copy-done = bf16[1024,512]{1,0:T(8,128)(2,1)S(1)} copy-done((bf16[1024,512]{1,0:T(8,128)(2,1)S(1)}, bf16[1024,512]{1,0:T(8,128)(2,1)}, u32[]{:S(2)}) %copy-start) | copy-done | bytes 1048600
  11.5 0.8 copy-done.1
  12.3 0.7 copy-done.3
  13.0 0.7 copy-done.4
  13.6 2.3 %gate.1 = (f32[8,2,2048]{2,1,0:T(2,128)S(1)}, f32[8,2,2048]{2,1,0:T(2,128)S(1)}, f32[1,2048]{1,0:T(1,128)S(1)}, bf16[2048,512]{1,0:T(8,128)(2,1)S(1)}, f32[2,2048]{1,0:T(2,128)S(1)}) custom-call(s32[35]{0:T(128)S(1)} %concatenate.3.int_ref.refs_0_.spot_ref, s32[2,1024]{1,0:T(2,128)S(1)} %copy-done.3, s32[2,1024]{1,0:T(2,128)S(1)} %collective-permute-done.there_ref, ...), custom_call_target="tpu_custom_call" | custom-call | tf_op jit(solution)/shard_map/gate/pallas_call | solution.py:531
  15.9 1.6 %collective-permute-start.4 = (bf16[1,336,512]{2,1,0:T(8,128)(2,1)S(1)}, bf16[1,336,512]{2,1,0:T(8,128)(2,1)S(1)}, u32[]{:S(2)}, u32[]{:S(2)}) collective-permute-start(bf16[1,336,512]{2,1,0:T(8,128)(2,1)S(1)} %hold.3.refs_0_.refs_1_.refs_8_.refs_10_), channel_id=1, source_target_pairs={{0,1},{1,0},{2,3},{3,2},{4,5},{5,4},{6,7},{7,6},{8,9},{9,8},{10,11... | collective-permute-start | bytes 1032200 | tf_op jit(solution)/shard_map/pay_4/ppermute | solution.py:489
  17.5 1.5 %collective-permute-start.3 = (bf16[1,336,512]{2,1,0:T(8,128)(2,1)S(1)}, bf16[1,336,512]{2,1,0:T(8,128)(2,1)S(1)}, u32[]{:S(2)}, u32[]{:S(2)}) collective-permute-start(bf16[1,336,512]{2,1,0:T(8,128)(2,1)S(1)} %hold.3.refs_0_.refs_1_.refs_8_.refs_10_), channel_id=1, source_target_pairs={{0,2},{1,3},{2,0},{3,1},{4,6},{5,7},{6,4},{7,5},{8,10},{9,11},{10,... | collective-permute-start | bytes 1032200 | tf_op jit(solution)/shard_map/pay_2/ppermute | solution.py:489
  19.0 0.7 collective-permute-start.7
  19.7 2.9 %forward_0.1 = (bf16[1,256,2048]{2,1,0:T(8,128)(2,1)S(1)}, bf16[1,256,2048]{2,1,0:T(8,128)(2,1)S(1)}, bf16[1,128,2048]{2,1,0:T(8,128)(2,1)S(1)}, f32[1,128,2048]{2,1,0:T(8,128)S(1)}, f32[2,128,2048]{2,1,0:T(8,128)S(1)}) custom-call(bf16[2048,512]{1,0:T(8,128)(2,1)S(1)} %get-tuple-element.92.x_ref.refs_0_.refs_1_, ...), custom_call_target="tpu_custom_call" | custom-call | flops 675000000 | tf_op jit(solution)/shard_map/forward_0/pallas_call | solution.py:56
  22.6 3.3 %collective-permute-done.4.refs_1_.refs_12_.refs_14_ = bf16[1,336,512]{2,1,0:T(8,128)(2,1)S(1)} collective-permute-done((bf16[1,336,512]{2,1,0:T(8,128)(2,1)S(1)}, bf16[1,336,512]{2,1,0:T(8,128)(2,1)S(1)}, u32[]{:S(2)}, u32[]{:S(2)}) %collective-permute-start.4) | collective-permute-done | bytes 344096 | tf_op jit(solution)/shard_map/pay_4/ppermute | solution.py:489
  26.6 1.5 %collective-permute-start.10 = (bf16[1,336,512]{2,1,0:T(8,128)(2,1)S(1)}, bf16[1,336,512]{2,1,0:T(8,128)(2,1)S(1)}, u32[]{:S(2)}, u32[]{:S(2)}) collective-permute-start(bf16[1,336,512]{2,1,0:T(8,128)(2,1)S(1)} %add.10.refs_0_.refs_2_.refs_9_.refs_11_), channel_id=1, source_target_pairs={{0,1},{1,0},{2,3},{3,2},{4,5},{5,4},{6,7},{7,6},{8,9},{9,8},{10,11... | collective-permute-start | bytes 1032200 | tf_op jit(solution)/shard_map/pay_5/ppermute | solution.py:489
  28.6 4.9 %forward_14.1 = (bf16[1,256,2048]{2,1,0:T(8,128)(2,1)S(1)}, bf16[1,256,2048]{2,1,0:T(8,128)(2,1)S(1)}, bf16[1,128,2048]{2,1,0:T(8,128)(2,1)S(1)}, f32[1,128,2048...) custom-call(bf16[2048,512]{1,0:T(8,128)(2,1)S(1)} %get-tuple-element, ...), custom_call_target="tpu_custom_call" | custom-call | flops 1350000000 | tf_op jit(solution)/shard_map/forward_14/pallas_call | solution.py:56
  33.5 2.9 %forward_2.1 = (bf16[1,256,2048]{2,1,0:T(8,128)(2,1)S(1)}, bf16[1,256,2048]{2,1,0:T(8,128)(2,1)S(1)}, bf16[1,128,2048]{2,1,0:T(8,128)(2,1)S(1)}, f32[1,128,2048]{2,1,0:T(8,128)S(1)}, f32[2,128,2048]{2,1,0:T(8,128)S(1)}) custom-call(bf16[2048,512]{1,0:T(8,128)(2,1)S(1)} %get-tuple-element.92.x_ref.refs_0_.refs_1_, ...), custom_call_target="tpu_custom_call" | custom-call | flops 675000000 | tf_op jit(solution)/shard_map/forward_2/pallas_call | solution.py:56
  37.0 1.6 %collective-permute-start.9 = (bf16[1,336,512]{2,1,0:T(8,128)(2,1)S(1)}, bf16[1,336,512]{2,1,0:T(8,128)(2,1)S(1)}, u32[]{:S(2)}, u32[]{:S(2)}) collective-permute-start(bf16[1,336,512]{2,1,0:T(8,128)(2,1)S(1)} %hold.5), channel_id=1, source_target_pairs={{0,1},{1,0},{2,3},{3,2},{4,5},{5,4},{6,7},{7,6},{8,9},{9,8},{10,11... | collective-permute-start | bytes 1032200 | tf_op jit(solution)/shard_map/pay_7/ppermute | solution.py:489
  38.7 4.9 %forward_35.1 = (bf16[1,256,2048]{2,1,0:T(8,128)(2,1)S(1)}, bf16[1,256,2048]{2,1,0:T(8,128)(2,1)S(1)}, bf16[1,128,2048]{2,1,0:T(8,128)(2,1)S(1)}, f32[1,128,2048...) custom-call(bf16[2048,512]{1,0:T(8,128)(2,1)S(1)} %get-tuple-element, ...), custom_call_target="tpu_custom_call" | custom-call | flops 1350000000 | tf_op jit(solution)/shard_map/forward_35/pallas_call | solution.py:56
  43.6 0.8 collective-permute-done.9.refs_1_.pay_b.refs_15_.refs_17_
  44.4 4.9 %forward_67.1 = (bf16[1,256,2048]{2,1,0:T(8,128)(2,1)S(1)}, bf16[1,256,2048]{2,1,0:T(8,128)(2,1)S(1)}, bf16[1,128,2048]{2,1,0:T(8,128)(2,1)S(1)}, f32[1,128,2048...) custom-call(bf16[2048,512]{1,0:T(8,128)(2,1)S(1)} %get-tuple-element, ...), custom_call_target="tpu_custom_call" | custom-call | flops 1350000000 | tf_op jit(solution)/shard_map/forward_67/pallas_call | solution.py:56
  49.4 2.6 %collective-permute-done.11.come_ref = bf16[2,128,2048]{2,1,0:T(8,128)(2,1)S(1)} collective-permute-done((bf16[2,128,2048]{2,1,0:T(8,128)(2,1)S(1)}, bf16[2,128,2048]{2,1,0:T(8,128)(2,1)S(1)}, u32[]{:S(2)}, u32[]{:S(2)}) %collective-permute-start.11) | collective-permute-done | bytes 1048608 | tf_op jit(solution)/shard_map/mixed/ppermute | solution.py:493
  52.0 3.3 %tower.1 = (f32[2,1024]{1,0:T(2,128)}, f32[2,128,2048]{2,1,0:T(8,128)S(1)}, f32[2,2048]{1,0:T(2,128)S(1)}, f32[48,512]{1,0:T(8,128)S(1)}) custom-call(bf16[2,128,2048]{2,1,0:T(8,128)(2,1)S(1)} %get-tuple-element.98.mix_ref, bf16[2,128,2048]{2,1,0:T(8,128)(2,1)S(1)} %collective-permute-done.11.come_ref, f32[2,2048]{1,0:T(2,128)S(1)} %get-tuple-element.99.label_ref, ...), custom_call_target="tpu_custom_call" | custom-call | flops 1200000000 | tf_op jit(solution)/shard_map/tower/pallas_call | solution.py:56
  55.4 2.8 %backward_67.1 = (bf16[1,336,512]{2,1,0:T(8,128)(2,1)S(1)}, bf16[1,336,512]{2,1,0:T(8,128)(2,1)S(1)}, bf16[1,256,2048]{2,1,0:T(8,128)(2,1)S(1)}, bf16[1,256,2048]{2,1,0:T(8,128)(2,1)S(1)}) custom-call(bf16[2048,512]{1,0:T(8,128)(2,1)S(1)} %get-tuple-element.92.x_ref.refs_0_.refs_1_, ...), custom_call_target="tpu_custom_call" | custom-call | flops 1500000000 | tf_op jit(solution)/shard_map/backward_67/pallas_call | solution.py:56
  58.2 1.6 %collective-permute-start.14 = (bf16[1,336,512]{2,1,0:T(8,128)(2,1)S(1)}, bf16[1,336,512]{2,1,0:T(8,128)(2,1)S(1)}, u32[]{:S(2)}, u32[]{:S(2)}) collective-permute-start(bf16[1,336,512]{2,1,0:T(8,128)(2,1)S(1)} %get-tuple-element.143), channel_id=1, source_target_pairs={{0,1},{1,0},{2,3},{3,2},{4,5},{5,4},{6,7},{7,6},{8,9},{9,8},{10,11... | collective-permute-start | bytes 1032200 | tf_op jit(solution)/shard_map/grad_six/ppermute | solution.py:489
  60.3 2.8 %backward_45.1 = (bf16[1,336,512]{2,1,0:T(8,128)(2,1)S(1)}, bf16[1,336,512]{2,1,0:T(8,128)(2,1)S(1)}, bf16[1,256,2048]{2,1,0:T(8,128)(2,1)S(1)}, bf16[1,256,2048]{2,1,0:T(8,128)(2,1)S(1)}) custom-call(bf16[2048,512]{1,0:T(8,128)(2,1)S(1)} %get-tuple-element.92.x_ref.refs_0_.refs_1_, ...), custom_call_target="tpu_custom_call" | custom-call | flops 300000000 | tf_op jit(solution)/shard_map/backward_45/pallas_call | solution.py:56
  63.0 1.6 %collective-permute-start.12 = (bf16[1,336,512]{2,1,0:T(8,128)(2,1)S(1)}, bf16[1,336,512]{2,1,0:T(8,128)(2,1)S(1)}, u32[]{:S(2)}, u32[]{:S(2)}) collective-permute-start(bf16[1,336,512]{2,1,0:T(8,128)(2,1)S(1)} %get-tuple-element.135), channel_id=1, source_target_pairs={{0,1},{1,0},{2,3},{3,2},{4,5},{5,4},{6,7},{7,6},{8,9},{9,8},{10,11... | collective-permute-start | bytes 1032200 | tf_op jit(solution)/shard_map/grad_four/ppermute | solution.py:489
  65.1 3.3 %gate_back.1 = (bf16[32,2048]{1,0:T(8,128)(2,1)S(1)}, f32[48,512]{1,0:T(8,128)S(1)}, f32[48,512]{1,0:T(8,128)S(1)}) custom-call(s32[35]{0:T(128)S(1)} %concatenate.3.int_ref.refs_0_.spot_ref, bf16[2048,512]{1,0:T(8,128)(2,1)S(1)} %get-tuple-element.92.x_ref.refs_0_.refs_1_, f32[2,128,2048]{2,1,0:T(8,128)S(1)} %get-tuple-element.102.dmix_ref.refs_4_.refs_2_, ...), custom_call_target="tpu_custom_call" | custom-call | flops 300000000 | tf_op jit(solution)/shard_map/gate_back/pallas_call | solution.py:56
  68.5 1.3 %collective-permute-done.16.refs_1_ = f32[48,512]{1,0:T(8,128)S(1)} collective-permute-done((f32[48,512]{1,0:T(8,128)S(1)}, f32[48,512]{1,0:T(8,128)S(1)}, u32[]{:S(2)}, u32[]{:S(2)}) %collective-permute-start.16) | collective-permute-done | bytes 98336 | tf_op jit(solution)/shard_map/give/ppermute | solution.py:493
  70.4 2.8 %backward_23.1 = (bf16[1,336,512]{2,1,0:T(8,128)(2,1)S(1)}, bf16[1,336,512]{2,1,0:T(8,128)(2,1)S(1)}, bf16[1,256,2048]{2,1,0:T(8,128)(2,1)S(1)}, bf16[1,256,2048]{2,1,0:T(8,128)(2,1)S(1)}) custom-call(bf16[2048,512]{1,0:T(8,128)(2,1)S(1)} %get-tuple-element.92.x_ref.refs_0_.refs_1_, bf16[1,336,512]{2,1,0:T(8,128)(2,1)S(1)} %hold.4.refs_2_.refs_0_.refs_1_.refs_10_.refs_12_, ...), custom_call_target="tpu_custom_call" | custom-call | flops 300000000 | tf_op jit(solution)/shard_map/backward_23/pallas_call | solution.py:56
  73.2 1.1 collective-permute-start.20
  74.3 1.0 collective-permute-start.21
  75.4 5.3 %collective-permute-start.18 = (f32[48,512]{1,0:T(8,128)S(1)}, f32[48,512]{1,0:T(8,128)S(1)}, u32[]{:S(2)}, u32[]{:S(2)}) collective-permute-start(f32[48,512]{1,0:T(8,128)S(1)} %add.12.refs_14_.refs_0_), channel_id=1, source_target_pairs={{0,8},{1,9},{2,10},{3,11},{4,12},{5,13},{6,14},{7,15},{8,0},{9,1},... | collective-permute-start | bytes 294920 | tf_op jit(solution)/shard_map/shared_3/ppermute | solution.py:489
  80.7 2.8 %backward_01.1 = (f32[1,336,512]{2,1,0:T(8,128)S(1)}, f32[1,336,512]{2,1,0:T(8,128)S(1)}, bf16[1,256,2048]{2,1,0:T(8,128)(2,1)S(1)}, bf16[1,256,2048]{2,1,0:T(8,128)(2,1)S(1)}) custom-call(bf16[2048,512]{1,0:T(8,128)(2,1)S(1)} %get-tuple-element.92.x_ref.refs_0_.refs_1_, bf16[1,336,512]{2,1,0:T(8,128)(2,1)S(1)} %hold.3.refs_0_.refs_1_.refs_8_.refs_10_, ...), custom_call_target="tpu_custom_call" | custom-call | flops 300000000 | tf_op jit(solution)/shard_map/backward_01/pallas_call | solution.py:56
  83.5 1.3 %collective-permute-done.18.refs_1_ = f32[48,512]{1,0:T(8,128)S(1)} collective-permute-done((f32[48,512]{1,0:T(8,128)S(1)}, f32[48,512]{1,0:T(8,128)S(1)}, u32[]{:S(2)}, u32[]{:S(2)}) %collective-permute-start.18) | collective-permute-done | bytes 98336 | tf_op jit(solution)/shard_map/shared_3/ppermute | solution.py:489
  84.8 3.3 %input_1.1.refs_2_ = bf16[1024,512]{1,0:T(8,128)(2,1)S(1)} custom-call(bf16[32,2048]{1,0:T(8,128)(2,1)S(1)} %get-tuple-element.128.dgate_ref.refs_0_, bf16[2,16,512]{2,1,0:T(8,128)(2,1)S(1)} %bitcast.10, bf16[1,256,2048]{2,1,0:T(8,128)(2,1)S(1)} %get-tuple-element.148.refs_0_.refs_2_, bf16[1,256,2048]{2,1,0:T(8,128)(2,1)S(1)} %get-tuple-element.149.refs_1_.refs_3_, ...), custom_call_target="tpu_custom_call" | custom-call | flops 1050000000 | tf_op jit(solution)/shard_map/input_1/pallas_call | solution.py:56
  88.3 1.3 %collective-permute-start.24 = (bf16[1,336,512]{2,1,0:T(8,128)(2,1)S(1)}, bf16[1,336,512]{2,1,0:T(8,128)(2,1)S(1)}, u32[]{:S(2)}, u32[]{:S(2)}) collective-permute-start(bf16[1,336,512]{2,1,0:T(8,128)(2,1)S(1)} %get-tuple-element.158.refs_2_), channel_id=1, source_target_pairs={{8,0},{9,1},{10,2},{11,3},{12,4},{13,5},{14,6},{15,7},{16,24},{17,... | collective-permute-start | bytes 1032200 | tf_op jit(solution)/shard_map/far/ppermute | solution.py:489
  89.7 1.3 %collective-permute-start.23 = (bf16[1,336,512]{2,1,0:T(8,128)(2,1)S(1)}, bf16[1,336,512]{2,1,0:T(8,128)(2,1)S(1)}, u32[]{:S(2)}, u32[]{:S(2)}) collective-permute-start(bf16[1,336,512]{2,1,0:T(8,128)(2,1)S(1)} %add.15), channel_id=1, source_target_pairs={{8,4},{9,5},{10,6},{11,7},{12,0},{13,1},{14,2},{15,3},{16,28},{17,... | collective-permute-start | bytes 1032200 | tf_op jit(solution)/shard_map/cross/ppermute | solution.py:489
  91.0 1.9 %collective-permute-start.22 = (bf16[1,336,512]{2,1,0:T(8,128)(2,1)S(1)}, bf16[1,336,512]{2,1,0:T(8,128)(2,1)S(1)}, u32[]{:S(2)}, u32[]{:S(2)}) collective-permute-start(bf16[1,336,512]{2,1,0:T(8,128)(2,1)S(1)} %add.15), channel_id=1, source_target_pairs={{0,4},{1,5},{2,6},{3,7},{4,0},{5,1},{6,2},{7,3},{24,28},{25,29},{2... | collective-permute-start | bytes 1032200 | tf_op jit(solution)/shard_map/near/ppermute | solution.py:489
  92.9 0.9 collective-permute-start.25
  93.8 3.1 %input_0.1.refs_3_.refs_5_.refs_0_ = f32[1024,512]{1,0:T(8,128)S(1)} custom-call(bf16[32,2048]{1,0:T(8,128)(2,1)S(1)} %get-tuple-element.128.dgate_ref.refs_0_, bf16[2,16,512]{2,1,0:T(8,128)(2,1)S(1)} %bitcast.11, bf16[1,256,2048]{2,1,0:T(8,128)(2,1)S(1)} %get-tuple-element.148.refs_0_.refs_2_, bf16[1,256,2048]{2,1,0:T(8,128)(2,1)S(1)} %get-tuple-element.149.refs_1_.refs_3_, ...), custom_call_target="tpu_custom_call" | custom-call | flops 1050000000 | tf_op jit(solution)/shard_map/input_0/pallas_call | solution.py:56
  96.9 0.7 collective-permute-done.25.refs_1_
  98.2 4.7 %collective-permute-done.26.refs_1_ = f32[48,512]{1,0:T(8,128)S(1)} collective-permute-done((f32[48,512]{1,0:T(8,128)S(1)}, f32[48,512]{1,0:T(8,128)S(1)}, u32[]{:S(2)}, u32[]{:S(2)}) %collective-permute-start.26) | collective-permute-done | bytes 98336 | tf_op jit(solution)/shard_map/shared_0/ppermute | solution.py:489
  103.5 0.9 collective-permute-done.27.give_ref
  104.5 1.3 %close.1 = (f32[2,16,512]{2,1,0:T(8,128)}, f32[2,16]{1,0:T(2,128)}, f32[2,64,128]{2,1,0:T(8,128)}, f32[2,64]{1,0:T(2,128)}, f32[2,64]{1,0:T(2,128)}, /*index=5*/f32[1,2]{1,0:T(1,128)}, f32[8,128]{1,0:T(8,128)S(1)}) custom-call(s32[35]{0:T(128)S(1)} %concatenate.3.int_ref.refs_0_.spot_ref, f32[48,512]{1,0:T(8,128)S(1)} %add.17.keep_ref, ...), custom_call_target="tpu_custom_call" | custom-call | flops 300000000 | tf_op jit(solution)/shard_map/close/pallas_call | solution.py:56
  105.8 1.6 %collective-permute-done.22.refs_1_ = bf16[1,336,512]{2,1,0:T(8,128)(2,1)S(1)} collective-permute-done((bf16[1,336,512]{2,1,0:T(8,128)(2,1)S(1)}, bf16[1,336,512]{2,1,0:T(8,128)(2,1)S(1)}, u32[]{:S(2)}, u32[]{:S(2)}) %collective-permute-start.22) | collective-permute-done | bytes 344096 | tf_op jit(solution)/shard_map/near/ppermute | solution.py:489
  107.6 1.5 %input_sum.1 = (f32[1024,512]{1,0:T(8,128)}, f32[8,128]{1,0:T(8,128)S(1)}) custom-call(f32[1024,512]{1,0:T(8,128)S(1)} %input_0.1.refs_3_.refs_5_.refs_0_, bf16[1024,512]{1,0:T(8,128)(2,1)S(1)} %collective-permute-done.19.refs_1_, f32[1,336,512]{2,1,0:T(8,128)S(1)} %add.18.refs_2_.refs_1_), custom_call_target="tpu_custom_call" | custom-call | flops 450000000 | tf_op jit(solution)/shard_map/input_sum/pallas_call | solution.py:56
  109.8 1.6 %finish.1 = (f32[1,512,256]{2,1,0:T(8,128)}, f32[1,256]{1,0:T(1,128)}, f32[1,256,128]{2,1,0:T(8,128)}, f32[1,128]{1,0:T(1,128)}) custom-call(s32[35]{0:T(128)S(1)} %concatenate.3.int_ref.refs_0_.spot_ref, f32[1,336,512]{2,1,0:T(8,128)S(1)} %add.18.refs_2_.refs_1_, f32[1,336,512]{2,1,0:T(8,128)S(1)} %collective-permute-done.28.refs_2_, ...), custom_call_target="tpu_custom_call" | custom-call | flops 3000000000 | tf_op jit(solution)/shard_map/finish/pallas_call | solution.py:56
  (60 shorter events, 6.4 us)
Async XLA Ops:
  0.6 9.6 %collective-permute-start.1 = (bf16[1024,512]{1,0:T(8,128)(2,1)}, bf16[1024,512]{1,0:T(8,128)(2,1)S(1)}, u32[]{:S(2)}, u32[]{:S(2)}) collective-permute-start(bf16[1024,512]{1,0:T(8,128)(2,1)} %mine_ref.1), channel_id=1, source_target_pairs={{0,16},{16,0},{1,17},{17,1},{2,18},{18,2},{3,19},{19,3},{4,20},{20... | collective-permute-start | bytes 3145736 | tf_op jit(solution)/shard_map/inputs/ppermute | solution.py:493
  2.4 13.5 %collective-permute-start.2 = (bf16[1,336,512]{2,1,0:T(8,128)(2,1)S(1)}, bf16[1,336,512]{2,1,0:T(8,128)(2,1)S(1)}, u32[]{:S(2)}, u32[]{:S(2)}) collective-permute-start(bf16[1,336,512]{2,1,0:T(8,128)(2,1)S(1)} %pack.1), channel_id=1, source_target_pairs={{0,8},{1,9},{2,10},{3,11},{4,12},{5,13},{6,14},{7,15},{8,24},{9,25... | collective-permute-start | bytes 1032200 | tf_op jit(solution)/shard_map/deal/ppermute | solution.py:502
  6.0 4.3 %collective-permute-start = (s32[2,1024]{1,0:T(2,128)}, s32[2,1024]{1,0:T(2,128)S(1)}, u32[]{:S(2)}, u32[]{:S(2)}) collective-permute-start(s32[2,1024]{1,0:T(2,128)} %label_ref.1), channel_id=1, source_target_pairs={{0,16},{16,0},{1,17},{17,1},{2,18},{18,2},{3,19},{19,3},{4,20},{20... | collective-permute-start | bytes 24584 | tf_op jit(solution)/shard_map/labels/ppermute | solution.py:493
  6.0 16.5 %collective-permute-start.5 = (bf16[1,336,512]{2,1,0:T(8,128)(2,1)S(1)}, bf16[1,336,512]{2,1,0:T(8,128)(2,1)S(1)}, u32[]{:S(2)}, u32[]{:S(2)}) collective-permute-start(bf16[1,336,512]{2,1,0:T(8,128)(2,1)S(1)} %pack.1), channel_id=1, source_target_pairs={{0,4},{1,5},{2,6},{3,7},{4,0},{5,1},{6,2},{7,3},{24,28},{25,29},{2... | collective-permute-start | bytes 1032200 | tf_op jit(solution)/shard_map/owners_near/ppermute | solution.py:489
  10.3 1.2 %copy-start = (bf16[1024,512]{1,0:T(8,128)(2,1)S(1)}, bf16[1024,512]{1,0:T(8,128)(2,1)}, u32[]{:S(2)}) copy-start(bf16[1024,512]{1,0:T(8,128)(2,1)} %mine_ref.1) | copy-start | bytes 3145732
  11.5 0.8 copy-start.1
  12.3 0.7 copy-start.3
  13.0 0.7 copy-start.4
  15.9 10.0 %collective-permute-start.4 = (bf16[1,336,512]{2,1,0:T(8,128)(2,1)S(1)}, bf16[1,336,512]{2,1,0:T(8,128)(2,1)S(1)}, u32[]{:S(2)}, u32[]{:S(2)}) collective-permute-start(bf16[1,336,512]{2,1,0:T(8,128)(2,1)S(1)} %hold.3.refs_0_.refs_1_.refs_8_.refs_10_), channel_id=1, source_target_pairs={{0,1},{1,0},{2,3},{3,2},{4,5},{5,4},{6,7},{7,6},{8,9},{9,8},{10,11... | collective-permute-start | bytes 1032200 | tf_op jit(solution)/shard_map/pay_4/ppermute | solution.py:489
  17.5 8.5 %collective-permute-start.3 = (bf16[1,336,512]{2,1,0:T(8,128)(2,1)S(1)}, bf16[1,336,512]{2,1,0:T(8,128)(2,1)S(1)}, u32[]{:S(2)}, u32[]{:S(2)}) collective-permute-start(bf16[1,336,512]{2,1,0:T(8,128)(2,1)S(1)} %hold.3.refs_0_.refs_1_.refs_8_.refs_10_), channel_id=1, source_target_pairs={{0,2},{1,3},{2,0},{3,1},{4,6},{5,7},{6,4},{7,5},{8,10},{9,11},{10,... | collective-permute-start | bytes 1032200 | tf_op jit(solution)/shard_map/pay_2/ppermute | solution.py:489
  19.0 6.9 %collective-permute-start.7 = (bf16[1,336,512]{2,1,0:T(8,128)(2,1)S(1)}, bf16[1,336,512]{2,1,0:T(8,128)(2,1)S(1)}, u32[]{:S(2)}, u32[]{:S(2)}) collective-permute-start(bf16[1,336,512]{2,1,0:T(8,128)(2,1)S(1)} %hold.3.refs_0_.refs_1_.refs_8_.refs_10_), channel_id=1, source_target_pairs={{8,12},{9,13},{10,14},{11,15},{12,8},{13,9},{14,10},{15,11},{16,20... | collective-permute-start | bytes 1032200 | tf_op jit(solution)/shard_map/pay_1/ppermute | solution.py:489
  26.0 11.0 %collective-permute-start.8 = (bf16[1,336,512]{2,1,0:T(8,128)(2,1)S(1)}, bf16[1,336,512]{2,1,0:T(8,128)(2,1)S(1)}, u32[]{:S(2)}, u32[]{:S(2)}) collective-permute-start(bf16[1,336,512]{2,1,0:T(8,128)(2,1)S(1)} %add.10.refs_0_.refs_2_.refs_9_.refs_11_), channel_id=1, source_target_pairs={{0,2},{1,3},{2,0},{3,1},{4,6},{5,7},{6,4},{7,5},{8,10},{9,11},{10,... | collective-permute-start | bytes 1032200 | tf_op jit(solution)/shard_map/pay_3/ppermute | solution.py:489
  26.6 12.1 %collective-permute-start.10 = (bf16[1,336,512]{2,1,0:T(8,128)(2,1)S(1)}, bf16[1,336,512]{2,1,0:T(8,128)(2,1)S(1)}, u32[]{:S(2)}, u32[]{:S(2)}) collective-permute-start(bf16[1,336,512]{2,1,0:T(8,128)(2,1)S(1)} %add.10.refs_0_.refs_2_.refs_9_.refs_11_), channel_id=1, source_target_pairs={{0,1},{1,0},{2,3},{3,2},{4,5},{5,4},{6,7},{7,6},{8,9},{9,8},{10,11... | collective-permute-start | bytes 1032200 | tf_op jit(solution)/shard_map/pay_5/ppermute | solution.py:489
  28.1 15.5 %collective-permute-start.6 = (bf16[1,336,512]{2,1,0:T(8,128)(2,1)S(1)}, bf16[1,336,512]{2,1,0:T(8,128)(2,1)S(1)}, u32[]{:S(2)}, u32[]{:S(2)}) collective-permute-start(bf16[1,336,512]{2,1,0:T(8,128)(2,1)S(1)} %hold.4.refs_2_.refs_0_.refs_1_.refs_10_.refs_12_), channel_id=1, source_target_pairs={{0,1},{1,0},{2,3},{3,2},{4,5},{5,4},{6,7},{7,6},{8,9},{9,8},{10,11... | collective-permute-start | bytes 1032200 | tf_op jit(solution)/shard_map/pay_6/ppermute | solution.py:489
  37.0 7.3 %collective-permute-start.9 = (bf16[1,336,512]{2,1,0:T(8,128)(2,1)S(1)}, bf16[1,336,512]{2,1,0:T(8,128)(2,1)S(1)}, u32[]{:S(2)}, u32[]{:S(2)}) collective-permute-start(bf16[1,336,512]{2,1,0:T(8,128)(2,1)S(1)} %hold.5), channel_id=1, source_target_pairs={{0,1},{1,0},{2,3},{3,2},{4,5},{5,4},{6,7},{7,6},{8,9},{9,8},{10,11... | collective-permute-start | bytes 1032200 | tf_op jit(solution)/shard_map/pay_7/ppermute | solution.py:489
  44.3 7.7 %copy-start.5 = (bf16[2,128,64]{1,2,0:T(8,128)(2,1)S(1)}, bf16[2,128,64]{1,2,0:T(8,128)(2,1)}, u32[]{:S(2)}) copy-start(bf16[2,128,64]{1,2,0:T(8,128)(2,1)} %param.21) | copy-start | bytes 98308
  44.3 7.7 %copy-start.6 = (bf16[2]{0:T(256)(128)(2,1)S(1)}, bf16[2]{0:T(256)(128)(2,1)}, u32[]{:S(2)}) copy-start(bf16[2]{0:T(256)(128)(2,1)} %param.24) | copy-start | bytes 16
  44.4 7.7 %copy-start.7 = (bf16[2,64]{1,0:T(2,128)(2,1)S(1)}, bf16[2,64]{1,0:T(2,128)(2,1)}, u32[]{:S(2)}) copy-start(bf16[2,64]{1,0:T(2,128)(2,1)} %tb_ref.1) | copy-start | bytes 772
  44.4 7.7 %copy-start.8 = (bf16[2,64]{1,0:T(2,128)(2,1)S(1)}, bf16[2,64]{1,0:T(2,128)(2,1)}, u32[]{:S(2)}) copy-start(bf16[2,64]{1,0:T(2,128)(2,1)} %tl_ref.1) | copy-start | bytes 772
  49.3 2.7 %collective-permute-start.11 = (bf16[2,128,2048]{2,1,0:T(8,128)(2,1)S(1)}, bf16[2,128,2048]{2,1,0:T(8,128)(2,1)S(1)}, u32[]{:S(2)}, u32[]{:S(2)}) collective-permute-start(bf16[2,128,2048]{2,1,0:T(8,128)(2,1)S(1)} %get-tuple-element.98.mix_ref), channel_id=1, source_target_pairs={{0,16},{16,0},{1,17},{17,1},{2,18},{18,2},{3,19},{19,3},{4,20},{20... | collective-permute-start | bytes 3145736 | tf_op jit(solution)/shard_map/mixed/ppermute | solution.py:493
  58.2 12.2 %collective-permute-start.14 = (bf16[1,336,512]{2,1,0:T(8,128)(2,1)S(1)}, bf16[1,336,512]{2,1,0:T(8,128)(2,1)S(1)}, u32[]{:S(2)}, u32[]{:S(2)}) collective-permute-start(bf16[1,336,512]{2,1,0:T(8,128)(2,1)S(1)} %get-tuple-element.143), channel_id=1, source_target_pairs={{0,1},{1,0},{2,3},{3,2},{4,5},{5,4},{6,7},{7,6},{8,9},{9,8},{10,11... | collective-permute-start | bytes 1032200 | tf_op jit(solution)/shard_map/grad_six/ppermute | solution.py:489
  59.8 10.6 %collective-permute-start.15 = (bf16[1,336,512]{2,1,0:T(8,128)(2,1)S(1)}, bf16[1,336,512]{2,1,0:T(8,128)(2,1)S(1)}, u32[]{:S(2)}, u32[]{:S(2)}) collective-permute-start(bf16[1,336,512]{2,1,0:T(8,128)(2,1)S(1)} %get-tuple-element.144), channel_id=1, source_target_pairs={{0,1},{1,0},{2,3},{3,2},{4,5},{5,4},{6,7},{7,6},{8,9},{9,8},{10,11... | collective-permute-start | bytes 1032200 | tf_op jit(solution)/shard_map/grad_seven/ppermute | solution.py:489
  63.0 17.6 %collective-permute-start.12 = (bf16[1,336,512]{2,1,0:T(8,128)(2,1)S(1)}, bf16[1,336,512]{2,1,0:T(8,128)(2,1)S(1)}, u32[]{:S(2)}, u32[]{:S(2)}) collective-permute-start(bf16[1,336,512]{2,1,0:T(8,128)(2,1)S(1)} %get-tuple-element.135), channel_id=1, source_target_pairs={{0,1},{1,0},{2,3},{3,2},{4,5},{5,4},{6,7},{7,6},{8,9},{9,8},{10,11... | collective-permute-start | bytes 1032200 | tf_op jit(solution)/shard_map/grad_four/ppermute | solution.py:489
  64.7 16.0 %collective-permute-start.13 = (bf16[1,336,512]{2,1,0:T(8,128)(2,1)S(1)}, bf16[1,336,512]{2,1,0:T(8,128)(2,1)S(1)}, u32[]{:S(2)}, u32[]{:S(2)}) collective-permute-start(bf16[1,336,512]{2,1,0:T(8,128)(2,1)S(1)} %get-tuple-element.136), channel_id=1, source_target_pairs={{0,1},{1,0},{2,3},{3,2},{4,5},{5,4},{6,7},{7,6},{8,9},{9,8},{10,11... | collective-permute-start | bytes 1032200 | tf_op jit(solution)/shard_map/grad_five/ppermute | solution.py:489
  68.5 1.4 %collective-permute-start.16 = (f32[48,512]{1,0:T(8,128)S(1)}, f32[48,512]{1,0:T(8,128)S(1)}, u32[]{:S(2)}, u32[]{:S(2)}) collective-permute-start(f32[48,512]{1,0:T(8,128)S(1)} %get-tuple-element.146), channel_id=1, source_target_pairs={{0,16},{16,0},{1,17},{17,1},{2,18},{18,2},{3,19},{19,3},{4,20},{20... | collective-permute-start | bytes 294920 | tf_op jit(solution)/shard_map/give/ppermute | solution.py:493
  69.8 5.5 %collective-permute-start.17 = (f32[48,512]{1,0:T(8,128)S(1)}, f32[48,512]{1,0:T(8,128)S(1)}, u32[]{:S(2)}, u32[]{:S(2)}) collective-permute-start(f32[48,512]{1,0:T(8,128)S(1)} %add.11.refs_13_.refs_0_), channel_id=1, source_target_pairs={{0,4},{1,5},{2,6},{3,7},{4,0},{5,1},{6,2},{7,3},{8,12},{9,13},{10,... | collective-permute-start | bytes 294920 | tf_op jit(solution)/shard_map/shared_2/ppermute | solution.py:489
  73.2 14.9 %collective-permute-start.20 = (bf16[1,336,512]{2,1,0:T(8,128)(2,1)S(1)}, bf16[1,336,512]{2,1,0:T(8,128)(2,1)S(1)}, u32[]{:S(2)}, u32[]{:S(2)}) collective-permute-start(bf16[1,336,512]{2,1,0:T(8,128)(2,1)S(1)} %get-tuple-element.154), channel_id=1, source_target_pairs={{0,2},{1,3},{2,0},{3,1},{4,6},{5,7},{6,4},{7,5},{8,10},{9,11},{10,... | collective-permute-start | bytes 1032200 | tf_op jit(solution)/shard_map/grad_two/ppermute | solution.py:489
  74.3 15.3 %collective-permute-start.21 = (bf16[1,336,512]{2,1,0:T(8,128)(2,1)S(1)}, bf16[1,336,512]{2,1,0:T(8,128)(2,1)S(1)}, u32[]{:S(2)}, u32[]{:S(2)}) collective-permute-start(bf16[1,336,512]{2,1,0:T(8,128)(2,1)S(1)} %get-tuple-element.157), channel_id=1, source_target_pairs={{0,2},{1,3},{2,0},{3,1},{4,6},{5,7},{6,4},{7,5},{8,10},{9,11},{10,... | collective-permute-start | bytes 1032200 | tf_op jit(solution)/shard_map/grad_three/ppermute | solution.py:489
  75.4 9.4 %collective-permute-start.18 = (f32[48,512]{1,0:T(8,128)S(1)}, f32[48,512]{1,0:T(8,128)S(1)}, u32[]{:S(2)}, u32[]{:S(2)}) collective-permute-start(f32[48,512]{1,0:T(8,128)S(1)} %add.12.refs_14_.refs_0_), channel_id=1, source_target_pairs={{0,8},{1,9},{2,10},{3,11},{4,12},{5,13},{6,14},{7,15},{8,0},{9,1},... | collective-permute-start | bytes 294920 | tf_op jit(solution)/shard_map/shared_3/ppermute | solution.py:489
  80.7 4.1 %copy-start.2 = (bf16[2,512,16]{1,2,0:T(8,128)(2,1)S(1)}, bf16[2,512,16]{1,2,0:T(8,128)(2,1)}, u32[]{:S(2)}) copy-start(bf16[2,512,16]{1,2,0:T(8,128)(2,1)} %param.19) | copy-start | bytes 98308
  88.1 19.5 %collective-permute-start.19 = (bf16[1024,512]{1,0:T(8,128)(2,1)S(1)}, bf16[1024,512]{1,0:T(8,128)(2,1)S(1)}, u32[]{:S(2)}, u32[]{:S(2)}) collective-permute-start(bf16[1024,512]{1,0:T(8,128)(2,1)S(1)} %input_1.1.refs_2_), channel_id=1, source_target_pairs={{0,16},{16,0},{1,17},{17,1},{2,18},{18,2},{3,19},{19,3},{4,20},{20... | collective-permute-start | bytes 3145736 | tf_op jit(solution)/shard_map/over/ppermute | solution.py:493
  88.3 17.5 %collective-permute-start.24 = (bf16[1,336,512]{2,1,0:T(8,128)(2,1)S(1)}, bf16[1,336,512]{2,1,0:T(8,128)(2,1)S(1)}, u32[]{:S(2)}, u32[]{:S(2)}) collective-permute-start(bf16[1,336,512]{2,1,0:T(8,128)(2,1)S(1)} %get-tuple-element.158.refs_2_), channel_id=1, source_target_pairs={{8,0},{9,1},{10,2},{11,3},{12,4},{13,5},{14,6},{15,7},{16,24},{17,... | collective-permute-start | bytes 1032200 | tf_op jit(solution)/shard_map/far/ppermute | solution.py:489
  89.7 16.1 %collective-permute-start.23 = (bf16[1,336,512]{2,1,0:T(8,128)(2,1)S(1)}, bf16[1,336,512]{2,1,0:T(8,128)(2,1)S(1)}, u32[]{:S(2)}, u32[]{:S(2)}) collective-permute-start(bf16[1,336,512]{2,1,0:T(8,128)(2,1)S(1)} %add.15), channel_id=1, source_target_pairs={{8,4},{9,5},{10,6},{11,7},{12,0},{13,1},{14,2},{15,3},{16,28},{17,... | collective-permute-start | bytes 1032200 | tf_op jit(solution)/shard_map/cross/ppermute | solution.py:489
  91.0 16.4 %collective-permute-start.22 = (bf16[1,336,512]{2,1,0:T(8,128)(2,1)S(1)}, bf16[1,336,512]{2,1,0:T(8,128)(2,1)S(1)}, u32[]{:S(2)}, u32[]{:S(2)}) collective-permute-start(bf16[1,336,512]{2,1,0:T(8,128)(2,1)S(1)} %add.15), channel_id=1, source_target_pairs={{0,4},{1,5},{2,6},{3,7},{4,0},{5,1},{6,2},{7,3},{24,28},{25,29},{2... | collective-permute-start | bytes 1032200 | tf_op jit(solution)/shard_map/near/ppermute | solution.py:489
  92.9 4.7 %collective-permute-start.25 = (f32[48,512]{1,0:T(8,128)S(1)}, f32[48,512]{1,0:T(8,128)S(1)}, u32[]{:S(2)}, u32[]{:S(2)}) collective-permute-start(f32[48,512]{1,0:T(8,128)S(1)} %add.13.refs_18_.refs_0_), channel_id=1, source_target_pairs={{0,2},{1,3},{2,0},{3,1},{4,6},{5,7},{6,4},{7,5},{8,10},{9,11},{10,... | collective-permute-start | bytes 294920 | tf_op jit(solution)/shard_map/shared_1/ppermute | solution.py:489
  97.6 5.3 %collective-permute-start.26 = (f32[48,512]{1,0:T(8,128)S(1)}, f32[48,512]{1,0:T(8,128)S(1)}, u32[]{:S(2)}, u32[]{:S(2)}) collective-permute-start(f32[48,512]{1,0:T(8,128)S(1)} %add.16.refs_0_), channel_id=1, source_target_pairs={{0,1},{1,0},{2,3},{3,2},{4,5},{5,4},{6,7},{7,6},{8,9},{9,8},{10,11... | collective-permute-start | bytes 294920 | tf_op jit(solution)/shard_map/shared_0/ppermute | solution.py:489
  102.9 1.6 %collective-permute-start.27 = (f32[48,512]{1,0:T(8,128)S(1)}, f32[48,512]{1,0:T(8,128)S(1)}, u32[]{:S(2)}, u32[]{:S(2)}) collective-permute-start(f32[48,512]{1,0:T(8,128)S(1)} %add.17.keep_ref), channel_id=1, source_target_pairs={{0,16},{16,0},{1,17},{17,1},{2,18},{18,2},{3,19},{19,3},{4,20},{20... | collective-permute-start | bytes 294920 | tf_op jit(solution)/shard_map/keep/ppermute | solution.py:493
  107.6 2.2 %collective-permute-start.28 = (f32[1,336,512]{2,1,0:T(8,128)S(1)}, f32[1,336,512]{2,1,0:T(8,128)S(1)}, u32[]{:S(2)}, u32[]{:S(2)}) collective-permute-start(f32[1,336,512]{2,1,0:T(8,128)S(1)} %add.18.refs_2_.refs_1_), channel_id=1, source_target_pairs={{0,16},{16,0},{1,17},{17,1},{2,18},{18,2},{3,19},{19,3},{4,20},{20... | collective-permute-start | bytes 2064392 | tf_op jit(solution)/shard_map/final/ppermute | solution.py:493

commit v2 on v1

--- a/solution.py
+++ b/solution.py
@@ -40,23 +40,24 @@
     return value, slope
 
 
-def call(name, kernel, ins, outs, pin, micros, scratch=(), scalars=0, limit=8, after=()):
+def call(name, kernel, ins, outs, pin, micros, scratch=(), scalars=0, limit=8, after=(), alias=()):
     limit = limit if pin is not None else 60
     pinned = lambda a: pltpu.with_memory_space_constraint(a, pltpu.VMEM) if pin else a
-    args = [a if n < scalars else pinned(a) for n, a in enumerate(ins)] + list(after)
-    count = len(ins)
+    args = [a if n < scalars else pinned(a) for n, a in enumerate(ins)] + [pinned(a) for a in alias] + list(after)
+    count, skip = len(ins), len(alias) + len(after)
     body = kernel
-    if after:
+    if skip:
 
         def body(*refs):
-            return kernel(*refs[:count], *refs[count + len(after) :])
+            return kernel(*refs[:count], *refs[count + skip :])
 
     kept = pltpu.VMEM if pin else jax.ShapeDtypeStruct
     shapes = [(kept if stay else jax.ShapeDtypeStruct)(shape, dtype) for shape, dtype, stay in outs]
     return pl.pallas_call(
         body,
         name=name,
-        in_specs=[SMEM] * scalars + [VMEM] * (count - scalars) + [ANY] * len(after),
+        in_specs=[SMEM] * scalars + [VMEM] * (count - scalars + len(alias)) + [ANY] * len(after),
+        input_output_aliases={count + n: n for n in range(len(alias))},
         out_specs=[VMEM] * len(outs),
         out_shape=shapes,
         scratch_shapes=list(scratch),
@@ -191,7 +192,7 @@
             low_ref[j, t : t + 1, :] = row.astype(BF16).astype(F32)
 
 
-def forward_kernel(bundles, first, block, chunk, x_ref, low_ref, *refs):
+def forward_kernel(bundles, first, block, chunk, span, x_ref, low_ref, *refs):
     count = len(bundles)
     pays, refs = refs[:count], refs[count:]
     if not first:
@@ -203,6 +204,7 @@
         for n, pay_ref in enumerate(pays):
             pay = pay_ref[k]
             weights[k, n] = (pay[:256], second_weight(pay), *biases(pay))
+    out_from = 0 if mix_ref.shape[2] == x_ref.shape[0] else span[0]
     work = [(c, k, n) for c in range(0, block, chunk) for k in range(depth) for n in range(count)]
 
     def step(i, _):
@@ -233,7 +235,7 @@
                 else:
                     totals[t] = totals[t] + term
                 if k == depth - 1 and n == count - 1:
-                    mix_ref[t, :, at] = totals[t].astype(mix_ref.dtype)
+                    mix_ref[t, :, pl.ds(base + c - out_from, chunk)] = totals[t].astype(mix_ref.dtype)
 
         ones, twos = {0: layer_one(*work[0])}, {}
         for i in range(len(work) + 1):
@@ -247,25 +249,26 @@
                 twos[i] = dot(weights[work[i][1:]][1], hidden, NN)
         return 0
 
-    lax.fori_loop(0, x_ref.shape[0] // block, step, 0)
+    lax.fori_loop(span[0] // block, span[1] // block, step, 0)
 
 
 def tower_kernel(
-    chunk, mix_ref, come_ref, label_ref, weight_ref, tob_ref, tw_ref, tb_ref, tl_ref,
-    pred_ref, dmix_ref, centre_ref, shared_ref, first, sums,
+    side, chunk, mix_ref, come_ref, label_ref, weight_ref, tob_ref, tw_ref, tb_ref, tl_ref, dmix_ref, centre_ref, *refs
 ):
-    rows = pred_ref.shape[1]
-    first[...] = jnp.zeros_like(first)
-    sums[...] = jnp.zeros_like(sums)
+    rows = mix_ref.shape[2]
+    if side == 0:
+        pred_ref, shared_ref, first, sums = refs
+        first[...] = jnp.zeros_like(first)
+        sums[...] = jnp.zeros_like(sums)
     tb = [to_column(tb_ref[t : t + 1, :].astype(F32)) for t in range(2)]
     tl = [to_column(tl_ref[t : t + 1, :].astype(F32)) for t in range(2)]
 
-    def step(side, i, _):
+    def step(i, _):
+        here = pl.ds(pl.multiple_of(i * chunk, chunk), chunk)
         at = pl.ds(pl.multiple_of(side * rows + i * chunk, chunk), chunk)
-        there = pl.ds(pl.multiple_of((1 - side) * rows + i * chunk, chunk), chunk)
         cols = []
         for t in range(2):
-            mixed = mix_ref[t, :, at].astype(F32) + come_ref[t, :, there].astype(F32)
+            mixed = mix_ref[t, :, here].astype(F32) + come_ref[t, :, here].astype(F32)
             low = mixed.astype(BF16)
             act, slope = gelu_pair(dot(tw_ref[t], low, NN) + tb[t])
             score = jnp.sum(act * tl[t], axis=0, keepdims=True) + tob_ref[0:1, t : t + 1].astype(F32)
@@ -276,7 +279,7 @@
             dmix_ref[t, :, at] = d_mixed
             centre_ref[t : t + 1, at] = jnp.sum(d_mixed * mixed, axis=0, keepdims=True)
             if side == 0:
-                pred_ref[t : t + 1, at] = pred
+                pred_ref[t : t + 1, here] = pred
                 first[t] += dot(d_low, low, NT)
                 cols.append(jnp.sum(act * d_score, axis=1, keepdims=True))
                 cols.append(jnp.sum(d_low.astype(F32), axis=1, keepdims=True))
@@ -286,11 +289,17 @@
             sums[...] += side_by_side([cols[3 * t + n] for n in range(3) for t in range(2)], 64)
         return 0
 
-    lax.fori_loop(0, rows // chunk, functools.partial(step, 0), 0)
-    lax.fori_loop(0, rows // chunk, functools.partial(step, 1), 0)
-    for t in range(2):
-        fold(shared_ref, 16 * t, first[t])
-    fold(shared_ref, 32, sums[...])
+    lax.fori_loop(0, rows // chunk, step, 0)
+    if side == 0:
+        for t in range(2):
+            fold(shared_ref, 16 * t, first[t])
+        fold(shared_ref, 32, sums[...])
+
+
+def tower_whole_kernel(chunk, mix_ref, come_ref, mix_there, come_there, *refs):
+    ins, (dmix_ref, centre_ref, pred_ref, shared_ref, first, sums) = refs[:6], refs[6:]
+    tower_kernel(0, chunk, mix_ref, come_ref, *ins, dmix_ref, centre_ref, pred_ref, shared_ref, first, sums)
+    tower_kernel(1, chunk, mix_there, come_there, *ins, dmix_ref, centre_ref)
 
 
 def shared_rows(experts):
@@ -548,15 +557,26 @@
     slope_type = F32 if pin else BF16
     for group in GROUPS:
         shape = lambda deep, dtype: ((depth, deep, 2 * rows), dtype, True)
-        *kept, mixed = call(
-            "forward_" + "".join(str(n) for n in group),
-            functools.partial(forward_kernel, group, mixed is None, 4 * chunk, chunk),
-            [x, low] + [pays[n] for n in group] + ([] if mixed is None else [mixed]),
-            [shape(256, BF16), shape(256, BF16), shape(128, BF16), shape(128, slope_type)] * len(group)
-            + [((2, 128, 2 * rows), BF16 if group == GROUPS[-1] else F32, True)],
-            pin,
-            2.25 * len(group) * depth,
-        )
+        name = "forward_" + "".join(str(n) for n in group)
+        ins = [x, low] + [pays[n] for n in group] + ([] if mixed is None else [mixed])
+        kernel = functools.partial(forward_kernel, group, mixed is None, 4 * chunk, chunk)
+        outs = [shape(256, BF16), shape(256, BF16), shape(128, BF16), shape(128, slope_type)] * len(group)
+        cost = 2.25 * len(group) * depth
+        if group != GROUPS[-1]:
+            outs.append(((2, 128, 2 * rows), F32, True))
+            *kept, mixed = call(name, functools.partial(kernel, (0, 2 * rows)), ins, outs, pin, cost)
+        elif extra:
+            outs.append(((2, 128, 2 * rows), BF16, True))
+            *kept, mixed = call(name, functools.partial(kernel, (0, 2 * rows)), ins, outs, pin, cost)
+            mixed_own, mixed_other = mixed[:, :, :rows], mixed[:, :, rows:]
+        else:
+            outs.append(((2, 128, rows), BF16, True))
+            *kept, mixed_other = call(
+                name + "_other", functools.partial(kernel, (rows, 2 * rows)), ins, outs, pin, cost / 2
+            )
+            *kept, mixed_own = call(
+                name + "_own", functools.partial(kernel, (0, rows)), ins, outs, pin, cost / 2, alias=kept
+            )
         for n, bundle in enumerate(group):
             saved[bundle] = kept[4 * n : 4 * n + 4]
         if group == GROUPS[0]:
@@ -572,21 +592,23 @@
         if group == GROUPS[LAST_ASK]:
             pays[7] = send("pay_7", hold(pays[3], [mixed]), end_bit)
 
-    predictions, dmix, centre, tower_sums = call(
-        "tower",
-        functools.partial(tower_kernel, 512),
-        [mixed, swap("mixed", mixed), both_labels, weights, tower_out_bias[None]]
-        + [jnp.transpose(tower_first_weight, (0, 2, 1)), tower_first_bias, tower_last],
-        [
-            ((2, rows), F32, False),
-            ((2, 128, 2 * rows), F32, True),
-            ((2, 2 * rows), F32, True),
-            ((48, 512), F32, True),
-        ],
-        pin,
-        4,
-        [pltpu.VMEM((2, 64, 128), F32), pltpu.VMEM((64, 128), F32)],
-    )
+    tower_ins = [both_labels, weights, tower_out_bias[None], jnp.transpose(tower_first_weight, (0, 2, 1))]
+    tower_ins += [tower_first_bias, tower_last]
+    tower_outs = [((2, 128, 2 * rows), F32, True), ((2, 2 * rows), F32, True)]
+    own_outs = tower_outs + [((2, rows), F32, False), ((48, 512), F32, True)]
+    scratch = [pltpu.VMEM((2, 64, 128), F32), pltpu.VMEM((64, 128), F32)]
+    come_own, come_other = swap("mixed_other", mixed_other), swap("mixed_own", mixed_own)
+    if extra:
+        ins = [mixed_own, come_own, mixed_other, come_other, *tower_ins]
+        kernel = functools.partial(tower_whole_kernel, 512)
+        dmix, centre, predictions, tower_sums = call("tower", kernel, ins, own_outs, pin, 4, scratch)
+    else:
+        ins = [mixed_own, come_own, *tower_ins]
+        kernel = functools.partial(tower_kernel, 0, 512)
+        *begun, predictions, tower_sums = call("tower_own", kernel, ins, own_outs, pin, 2, scratch)
+        ins = [mixed_other, come_other, *tower_ins]
+        kernel = functools.partial(tower_kernel, 1, 512)
+        dmix, centre = call("tower_other", kernel, ins, tower_outs, pin, 2, alias=begun)
 
     def back(a, b, come, dtype, cost, after=()):
         grad = ((depth, PAY_ROWS, 512), dtype, False)

time: 112 us -> 110 us (0.982)
  waiting for transfers between devices: 18.5 us -> 15.7 us
    ppermute x7 -> x8, waiting for transfers between devices: 5.52 us -> 2.87 us  [swap(): return lax.ppermute(value, 'dp', [(0, 1), (1, 0)])]
    pallas_call x25 -> x27, Pallas kernels: 49.6 us -> 50 us  [call(): pl.pallas_call(body, name=name, in_specs=[SMEM] * scalars + [VMEM] * (cou...]
  transfers between devices with their start and end apart: 29 -> 30, of which waited for: 11 -> 10; matrix products, arithmetic and copies ran while one was open for 1% -> 1% of each run, Pallas kernels for 36% -> 41%
where the time goes in v2:
time: 110 us; the launch traced here: 109 us
  Pallas kernels  53.4 us (49%)
  starting transfers between devices  35.2 us (32%)
  waiting for transfers between devices  15.7 us (14%)
  local copies, waits for them, and re-layouts  4.13 us (4%)
    pallas_call x27, Pallas kernels, call(): pl.pallas_call(body, name=name, in_specs=[SMEM] * scalars + [VMEM] * (cou...  50 us
    ppermute x21, starting transfers between devices, send(): return lax.ppermute(value, ('dp', 'expert'), pairs(bit_of_core, want, also))  29.6 us
    ppermute x21, waiting for transfers between devices, send(): return lax.ppermute(value, ('dp', 'expert'), pairs(bit_of_core, want, also))  12.8 us
    ppermute x1, starting transfers between devices, deal(): return lax.ppermute(value, ('dp', 'expert'), route)  3.66 us
    unnamed x19, local copies, waits for them, and re-layouts  3.38 us
    ppermute x8, waiting for transfers between devices, swap(): return lax.ppermute(value, 'dp', [(0, 1), (1, 0)])  2.87 us
    pallas_call x1, Pallas kernels, per_device(): pl.pallas_call(functools.partial(gate_kernel, masks, group_len.shape[0]),...  2.26 us
  transfers between devices with their start and end apart: 30, of which 10 were waited for; matrix products, arithmetic and copies ran while one was open for 1% of the time, Pallas kernels for 41%

profile of v2, /device:TPU:0, one launch (start us, length us, event | category | flops | bytes accessed | tf_op | source)
XLA Modules:
  0.0 109.5 jit_solution(2263988542571925271)
XLA Ops:
  1.2 1.2 %pack.1 = bf16[1,336,512]{2,1,0:T(8,128)(2,1)S(1)} custom-call(bf16[1,512,256]{2,1,0:T(8,128)(2,1)} %w1_ref.1, bf16[1,256,128]{2,1,0:T(8,128)(2,1)} %w2_ref.1, bf16[1,256]{1,0:T(2,128)(2,1)} %b1_ref.1, bf16[1,128]{1,0:T(2,128)(2,1)} %b2_ref.1), custom_call_target="tpu_custom_call" | custom-call | tf_op jit(solution)/shard_map/pack/pallas_call | solution.py:135
  2.4 3.7 %collective-permute-start.2 = (bf16[1,336,512]{2,1,0:T(8,128)(2,1)S(1)}, bf16[1,336,512]{2,1,0:T(8,128)(2,1)S(1)}, u32[]{:S(2)}, u32[]{:S(2)}) collective-permute-start(bf16[1,336,512]{2,1,0:T(8,128)(2,1)S(1)} %pack.1), channel_id=1, source_target_pairs={{0,8},{1,9},{2,10},{3,11},{4,12},{5,13},{6,14},{7,15},{8,24},{9,25... | collective-permute-start | bytes 1032200 | tf_op jit(solution)/shard_map/deal/ppermute | solution.py:511
  6.0 3.5 %collective-permute-start.5 = (bf16[1,336,512]{2,1,0:T(8,128)(2,1)S(1)}, bf16[1,336,512]{2,1,0:T(8,128)(2,1)S(1)}, u32[]{:S(2)}, u32[]{:S(2)}) collective-permute-start(bf16[1,336,512]{2,1,0:T(8,128)(2,1)S(1)} %pack.1), channel_id=1, source_target_pairs={{0,4},{1,5},{2,6},{3,7},{4,0},{5,1},{6,2},{7,3},{24,28},{25,29},{2... | collective-permute-start | bytes 1032200 | tf_op jit(solution)/shard_map/owners_near/ppermute | solution.py:498
  9.5 0.7 concatenate.3.int_ref.refs_0_.spot_ref
  10.3 1.2 %copy-done = bf16[1024,512]{1,0:T(8,128)(2,1)S(1)} copy-done((bf16[1024,512]{1,0:T(8,128)(2,1)S(1)}, bf16[1024,512]{1,0:T(8,128)(2,1)}, u32[]{:S(2)}) %copy-start) | copy-done | bytes 1048600
  11.5 0.8 copy-done.1
  12.3 0.7 copy-done.4
  13.0 0.7 copy-done.8
  13.6 2.3 %gate.1 = (f32[8,2,2048]{2,1,0:T(2,128)S(1)}, f32[8,2,2048]{2,1,0:T(2,128)S(1)}, f32[1,2048]{1,0:T(1,128)S(1)}, bf16[2048,512]{1,0:T(8,128)(2,1)S(1)}, f32[2,2048]{1,0:T(2,128)S(1)}) custom-call(s32[35]{0:T(128)S(1)} %concatenate.3.int_ref.refs_0_.spot_ref, s32[2,1024]{1,0:T(2,128)S(1)} %copy-done.4, s32[2,1024]{1,0:T(2,128)S(1)} %collective-permute-done.there_ref, ...), custom_call_target="tpu_custom_call" | custom-call | tf_op jit(solution)/shard_map/gate/pallas_call | solution.py:540
  15.9 1.6 %collective-permute-start.4 = (bf16[1,336,512]{2,1,0:T(8,128)(2,1)S(1)}, bf16[1,336,512]{2,1,0:T(8,128)(2,1)S(1)}, u32[]{:S(2)}, u32[]{:S(2)}) collective-permute-start(bf16[1,336,512]{2,1,0:T(8,128)(2,1)S(1)} %hold.3.refs_0_.refs_1_.refs_8_.refs_10_), channel_id=1, source_target_pairs={{0,1},{1,0},{2,3},{3,2},{4,5},{5,4},{6,7},{7,6},{8,9},{9,8},{10,11... | collective-permute-start | bytes 1032200 | tf_op jit(solution)/shard_map/pay_4/ppermute | solution.py:498
  17.5 1.5 %collective-permute-start.3 = (bf16[1,336,512]{2,1,0:T(8,128)(2,1)S(1)}, bf16[1,336,512]{2,1,0:T(8,128)(2,1)S(1)}, u32[]{:S(2)}, u32[]{:S(2)}) collective-permute-start(bf16[1,336,512]{2,1,0:T(8,128)(2,1)S(1)} %hold.3.refs_0_.refs_1_.refs_8_.refs_10_), channel_id=1, source_target_pairs={{0,2},{1,3},{2,0},{3,1},{4,6},{5,7},{6,4},{7,5},{8,10},{9,11},{10,... | collective-permute-start | bytes 1032200 | tf_op jit(solution)/shard_map/pay_2/ppermute | solution.py:498
  19.0 0.7 collective-permute-start.7
  19.7 2.9 %forward_0.1 = (bf16[1,256,2048]{2,1,0:T(8,128)(2,1)S(1)}, bf16[1,256,2048]{2,1,0:T(8,128)(2,1)S(1)}, bf16[1,128,2048]{2,1,0:T(8,128)(2,1)S(1)}, f32[1,128,2048]{2,1,0:T(8,128)S(1)}, f32[2,128,2048]{2,1,0:T(8,128)S(1)}) custom-call(bf16[2048,512]{1,0:T(8,128)(2,1)S(1)} %get-tuple-element.103.x_ref.refs_0_.refs_1_, ...), custom_call_target="tpu_custom_call" | custom-call | flops 675000000 | tf_op jit(solution)/shard_map/forward_0/pallas_call | solution.py:56
  22.6 3.3 %collective-permute-done.4.refs_1_.refs_12_.refs_14_ = bf16[1,336,512]{2,1,0:T(8,128)(2,1)S(1)} collective-permute-done((bf16[1,336,512]{2,1,0:T(8,128)(2,1)S(1)}, bf16[1,336,512]{2,1,0:T(8,128)(2,1)S(1)}, u32[]{:S(2)}, u32[]{:S(2)}) %collective-permute-start.4) | collective-permute-done | bytes 344096 | tf_op jit(solution)/shard_map/pay_4/ppermute | solution.py:498
  26.6 1.5 %collective-permute-start.10 = (bf16[1,336,512]{2,1,0:T(8,128)(2,1)S(1)}, bf16[1,336,512]{2,1,0:T(8,128)(2,1)S(1)}, u32[]{:S(2)}, u32[]{:S(2)}) collective-permute-start(bf16[1,336,512]{2,1,0:T(8,128)(2,1)S(1)} %add.10.refs_0_.refs_2_.refs_9_.refs_11_), channel_id=1, source_target_pairs={{0,1},{1,0},{2,3},{3,2},{4,5},{5,4},{6,7},{7,6},{8,9},{9,8},{10,11... | collective-permute-start | bytes 1032200 | tf_op jit(solution)/shard_map/pay_5/ppermute | solution.py:498
  28.6 4.9 %forward_14.1 = (bf16[1,256,2048]{2,1,0:T(8,128)(2,1)S(1)}, bf16[1,256,2048]{2,1,0:T(8,128)(2,1)S(1)}, bf16[1,128,2048]{2,1,0:T(8,128)(2,1)S(1)}, f32[1,128,2048...) custom-call(bf16[2048,512]{1,0:T(8,128)(2,1)S(1)} %get-tuple-element, ...), custom_call_target="tpu_custom_call" | custom-call | flops 1350000000 | tf_op jit(solution)/shard_map/forward_14/pallas_call | solution.py:56
  33.5 2.9 %forward_2.1 = (bf16[1,256,2048]{2,1,0:T(8,128)(2,1)S(1)}, bf16[1,256,2048]{2,1,0:T(8,128)(2,1)S(1)}, bf16[1,128,2048]{2,1,0:T(8,128)(2,1)S(1)}, f32[1,128,2048]{2,1,0:T(8,128)S(1)}, f32[2,128,2048]{2,1,0:T(8,128)S(1)}) custom-call(bf16[2048,512]{1,0:T(8,128)(2,1)S(1)} %get-tuple-element.103.x_ref.refs_0_.refs_1_, ...), custom_call_target="tpu_custom_call" | custom-call | flops 675000000 | tf_op jit(solution)/shard_map/forward_2/pallas_call | solution.py:56
  37.0 1.6 %collective-permute-start.9 = (bf16[1,336,512]{2,1,0:T(8,128)(2,1)S(1)}, bf16[1,336,512]{2,1,0:T(8,128)(2,1)S(1)}, u32[]{:S(2)}, u32[]{:S(2)}) collective-permute-start(bf16[1,336,512]{2,1,0:T(8,128)(2,1)S(1)} %hold.5), channel_id=1, source_target_pairs={{0,1},{1,0},{2,3},{3,2},{4,5},{5,4},{6,7},{7,6},{8,9},{9,8},{10,11... | collective-permute-start | bytes 1032200 | tf_op jit(solution)/shard_map/pay_7/ppermute | solution.py:498
  38.7 5.1 %forward_35.1 = (bf16[1,256,2048]{2,1,0:T(8,128)(2,1)S(1)}, bf16[1,256,2048]{2,1,0:T(8,128)(2,1)S(1)}, bf16[1,128,2048]{2,1,0:T(8,128)(2,1)S(1)}, f32[1,128,2048...) custom-call(bf16[2048,512]{1,0:T(8,128)(2,1)S(1)} %get-tuple-element, ...), custom_call_target="tpu_custom_call" | custom-call | flops 1350000000 | tf_op jit(solution)/shard_map/forward_35/pallas_call | solution.py:56
  44.3 2.4 %forward_67_other.1 = (bf16[1,256,2048]{2,1,0:T(8,128)(2,1)S(1)}, bf16[1,256,2048]{2,1,0:T(8,128)(2,1)S(1)}, bf16[1,128,2048]{2,1,0:T(8,128)(2,1)S(1)}, f32[1,12...) custom-call(bf16[2048,512]{1,0:T(8,128)(2,1)S(1)} %get-tuple-element, ...), custom_call_target="tpu_custom_call" | custom-call | flops 675000000 | tf_op jit(solution)/shard_map/forward_67_other/pallas_call | solution.py:56
  46.9 2.4 %forward_67_own.1 = (bf16[1,256,2048]{2,1,0:T(8,128)(2,1)S(1)}, bf16[1,256,2048]{2,1,0:T(8,128)(2,1)S(1)}, bf16[1,128,2048]{2,1,0:T(8,128)(2,1)S(1)}, f32[1,128,...) custom-call(bf16[2048,512]{1,0:T(8,128)(2,1)S(1)} %get-tuple-element, ...), custom_call_target="tpu_custom_call", output_to_operand_aliasing={{0}: (5, {}), {1}: (6, {}), {2}: (7, {}), {3}: (8, {}), {4}... | custom-call | flops 675000000 | tf_op jit(solution)/shard_map/forward_67_own/pallas_call | solution.py:56
  49.8 2.1 %tower_own.1 = (f32[2,128,2048]{2,1,0:T(8,128)S(1)}, f32[2,2048]{1,0:T(2,128)S(1)}, f32[2,1024]{1,0:T(2,128)}, f32[48,512]{1,0:T(8,128)S(1)}) custom-call(bf16[2,128,1024]{2,1,0:T(8,128)(2,1)S(1)} %get-tuple-element.117.mix_ref, bf16[2,128,1024]{2,1,0:T(8,128)(2,1)S(1)} %collective-permute-done.11.come_ref, ...), custom_call_target="tpu_custom_call" | custom-call | flops 600000000 | tf_op jit(solution)/shard_map/tower_own/pallas_call | solution.py:56
  51.9 1.6 %tower_other.1 = (f32[2,128,2048]{2,1,0:T(8,128)S(1)}, f32[2,2048]{1,0:T(2,128)S(1)}) custom-call(bf16[2,128,1024]{2,1,0:T(8,128)(2,1)S(1)} %get-tuple-element.118.refs_0_, bf16[2,128,1024]{2,1,0:T(8,128)(2,1)S(1)} %collective-permute-done.12.refs_1_, ...), custom_call_target="tpu_custom_call", output_to_operand_aliasing={{0}: (8, {}), {1}: (9, {})} | custom-call | flops 600000000 | tf_op jit(solution)/shard_map/tower_other/pallas_call | solution.py:56
  53.5 2.8 %backward_67.1 = (bf16[1,336,512]{2,1,0:T(8,128)(2,1)S(1)}, bf16[1,336,512]{2,1,0:T(8,128)(2,1)S(1)}, bf16[1,256,2048]{2,1,0:T(8,128)(2,1)S(1)}, bf16[1,256,2048]{2,1,0:T(8,128)(2,1)S(1)}) custom-call(bf16[2048,512]{1,0:T(8,128)(2,1)S(1)} %get-tuple-element.103.x_ref.refs_0_.refs_1_, ...), custom_call_target="tpu_custom_call" | custom-call | flops 1500000000 | tf_op jit(solution)/shard_map/backward_67/pallas_call | solution.py:56
  56.3 1.6 %collective-permute-start.15 = (bf16[1,336,512]{2,1,0:T(8,128)(2,1)S(1)}, bf16[1,336,512]{2,1,0:T(8,128)(2,1)S(1)}, u32[]{:S(2)}, u32[]{:S(2)}) collective-permute-start(bf16[1,336,512]{2,1,0:T(8,128)(2,1)S(1)} %get-tuple-element.165), channel_id=1, source_target_pairs={{0,1},{1,0},{2,3},{3,2},{4,5},{5,4},{6,7},{7,6},{8,9},{9,8},{10,11... | collective-permute-start | bytes 1032200 | tf_op jit(solution)/shard_map/grad_six/ppermute | solution.py:498
  58.4 2.8 %backward_45.1 = (bf16[1,336,512]{2,1,0:T(8,128)(2,1)S(1)}, bf16[1,336,512]{2,1,0:T(8,128)(2,1)S(1)}, bf16[1,256,2048]{2,1,0:T(8,128)(2,1)S(1)}, bf16[1,256,2048]{2,1,0:T(8,128)(2,1)S(1)}) custom-call(bf16[2048,512]{1,0:T(8,128)(2,1)S(1)} %get-tuple-element.103.x_ref.refs_0_.refs_1_, ...), custom_call_target="tpu_custom_call" | custom-call | flops 300000000 | tf_op jit(solution)/shard_map/backward_45/pallas_call | solution.py:56
  61.2 1.6 %collective-permute-start.13 = (bf16[1,336,512]{2,1,0:T(8,128)(2,1)S(1)}, bf16[1,336,512]{2,1,0:T(8,128)(2,1)S(1)}, u32[]{:S(2)}, u32[]{:S(2)}) collective-permute-start(bf16[1,336,512]{2,1,0:T(8,128)(2,1)S(1)} %get-tuple-element.157), channel_id=1, source_target_pairs={{0,1},{1,0},{2,3},{3,2},{4,5},{5,4},{6,7},{7,6},{8,9},{9,8},{10,11... | collective-permute-start | bytes 1032200 | tf_op jit(solution)/shard_map/grad_four/ppermute | solution.py:498
  63.3 3.5 %gate_back.1 = (bf16[32,2048]{1,0:T(8,128)(2,1)S(1)}, f32[48,512]{1,0:T(8,128)S(1)}, f32[48,512]{1,0:T(8,128)S(1)}) custom-call(s32[35]{0:T(128)S(1)} %concatenate.3.int_ref.refs_0_.spot_ref, bf16[2048,512]{1,0:T(8,128)(2,1)S(1)} %get-tuple-element.103.x_ref.refs_0_.refs_1_, f32[2,128,2048]{2,1,0:T(8,128)S(1)} %get-tuple-element.124.dmix_ref.refs_4_.refs_2_, ...), custom_call_target="tpu_custom_call" | custom-call | flops 300000000 | tf_op jit(solution)/shard_map/gate_back/pallas_call | solution.py:56
  66.9 1.3 %collective-permute-done.17.refs_1_ = f32[48,512]{1,0:T(8,128)S(1)} collective-permute-done((f32[48,512]{1,0:T(8,128)S(1)}, f32[48,512]{1,0:T(8,128)S(1)}, u32[]{:S(2)}, u32[]{:S(2)}) %collective-permute-start.17) | collective-permute-done | bytes 98336 | tf_op jit(solution)/shard_map/give/ppermute | solution.py:502
  68.8 2.8 %backward_23.1 = (bf16[1,336,512]{2,1,0:T(8,128)(2,1)S(1)}, bf16[1,336,512]{2,1,0:T(8,128)(2,1)S(1)}, bf16[1,256,2048]{2,1,0:T(8,128)(2,1)S(1)}, bf16[1,256,2048]{2,1,0:T(8,128)(2,1)S(1)}) custom-call(bf16[2048,512]{1,0:T(8,128)(2,1)S(1)} %get-tuple-element.103.x_ref.refs_0_.refs_1_, bf16[1,336,512]{2,1,0:T(8,128)(2,1)S(1)} %hold.4.refs_2_.refs_0_.refs_1_.refs_10_.refs_12_, ...), custom_call_target="tpu_custom_call" | custom-call | flops 300000000 | tf_op jit(solution)/shard_map/backward_23/pallas_call | solution.py:56
  71.6 1.1 collective-permute-start.21
  72.7 1.0 collective-permute-start.22
  73.7 5.3 %collective-permute-start.19 = (f32[48,512]{1,0:T(8,128)S(1)}, f32[48,512]{1,0:T(8,128)S(1)}, u32[]{:S(2)}, u32[]{:S(2)}) collective-permute-start(f32[48,512]{1,0:T(8,128)S(1)} %add.12.refs_14_.refs_0_), channel_id=1, source_target_pairs={{0,8},{1,9},{2,10},{3,11},{4,12},{5,13},{6,14},{7,15},{8,0},{9,1},... | collective-permute-start | bytes 294920 | tf_op jit(solution)/shard_map/shared_3/ppermute | solution.py:498
  79.0 2.8 %backward_01.1 = (f32[1,336,512]{2,1,0:T(8,128)S(1)}, f32[1,336,512]{2,1,0:T(8,128)S(1)}, bf16[1,256,2048]{2,1,0:T(8,128)(2,1)S(1)}, bf16[1,256,2048]{2,1,0:T(8,128)(2,1)S(1)}) custom-call(bf16[2048,512]{1,0:T(8,128)(2,1)S(1)} %get-tuple-element.103.x_ref.refs_0_.refs_1_, bf16[1,336,512]{2,1,0:T(8,128)(2,1)S(1)} %hold.3.refs_0_.refs_1_.refs_8_.refs_10_, ...), custom_call_target="tpu_custom_call" | custom-call | flops 300000000 | tf_op jit(solution)/shard_map/backward_01/pallas_call | solution.py:56
  81.9 1.3 %collective-permute-done.19.refs_1_ = f32[48,512]{1,0:T(8,128)S(1)} collective-permute-done((f32[48,512]{1,0:T(8,128)S(1)}, f32[48,512]{1,0:T(8,128)S(1)}, u32[]{:S(2)}, u32[]{:S(2)}) %collective-permute-start.19) | collective-permute-done | bytes 98336 | tf_op jit(solution)/shard_map/shared_3/ppermute | solution.py:498
  83.2 3.1 %input_1.1.refs_2_ = bf16[1024,512]{1,0:T(8,128)(2,1)S(1)} custom-call(bf16[32,2048]{1,0:T(8,128)(2,1)S(1)} %get-tuple-element.150.dgate_ref.refs_0_, bf16[2,16,512]{2,1,0:T(8,128)(2,1)S(1)} %bitcast.10, bf16[1,256,2048]{2,1,0:T(8,128)(2,1)S(1)} %get-tuple-element.170.refs_0_.refs_2_, bf16[1,256,2048]{2,1,0:T(8,128)(2,1)S(1)} %get-tuple-element.171.refs_1_.refs_3_, ...), custom_call_target="tpu_custom_call" | custom-call | flops 1050000000 | tf_op jit(solution)/shard_map/input_1/pallas_call | solution.py:56
  86.4 1.3 %collective-permute-start.25 = (bf16[1,336,512]{2,1,0:T(8,128)(2,1)S(1)}, bf16[1,336,512]{2,1,0:T(8,128)(2,1)S(1)}, u32[]{:S(2)}, u32[]{:S(2)}) collective-permute-start(bf16[1,336,512]{2,1,0:T(8,128)(2,1)S(1)} %get-tuple-element.180.refs_2_), channel_id=1, source_target_pairs={{8,0},{9,1},{10,2},{11,3},{12,4},{13,5},{14,6},{15,7},{16,24},{17,... | collective-permute-start | bytes 1032200 | tf_op jit(solution)/shard_map/far/ppermute | solution.py:498
  87.8 1.3 %collective-permute-start.24 = (bf16[1,336,512]{2,1,0:T(8,128)(2,1)S(1)}, bf16[1,336,512]{2,1,0:T(8,128)(2,1)S(1)}, u32[]{:S(2)}, u32[]{:S(2)}) collective-permute-start(bf16[1,336,512]{2,1,0:T(8,128)(2,1)S(1)} %add.15), channel_id=1, source_target_pairs={{8,4},{9,5},{10,6},{11,7},{12,0},{13,1},{14,2},{15,3},{16,28},{17,... | collective-permute-start | bytes 1032200 | tf_op jit(solution)/shard_map/cross/ppermute | solution.py:498
  89.1 1.9 %collective-permute-start.23 = (bf16[1,336,512]{2,1,0:T(8,128)(2,1)S(1)}, bf16[1,336,512]{2,1,0:T(8,128)(2,1)S(1)}, u32[]{:S(2)}, u32[]{:S(2)}) collective-permute-start(bf16[1,336,512]{2,1,0:T(8,128)(2,1)S(1)} %add.15), channel_id=1, source_target_pairs={{0,4},{1,5},{2,6},{3,7},{4,0},{5,1},{6,2},{7,3},{24,28},{25,29},{2... | collective-permute-start | bytes 1032200 | tf_op jit(solution)/shard_map/near/ppermute | solution.py:498
  91.0 0.9 collective-permute-start.26
  92.0 3.1 %input_0.1.refs_3_.refs_5_.refs_0_ = f32[1024,512]{1,0:T(8,128)S(1)} custom-call(bf16[32,2048]{1,0:T(8,128)(2,1)S(1)} %get-tuple-element.150.dgate_ref.refs_0_, bf16[2,16,512]{2,1,0:T(8,128)(2,1)S(1)} %bitcast.11, bf16[1,256,2048]{2,1,0:T(8,128)(2,1)S(1)} %get-tuple-element.170.refs_0_.refs_2_, bf16[1,256,2048]{2,1,0:T(8,128)(2,1)S(1)} %get-tuple-element.171.refs_1_.refs_3_, ...), custom_call_target="tpu_custom_call" | custom-call | flops 1050000000 | tf_op jit(solution)/shard_map/input_0/pallas_call | solution.py:56
  95.1 0.7 collective-permute-done.26.refs_1_
  96.3 4.7 %collective-permute-done.27.refs_1_ = f32[48,512]{1,0:T(8,128)S(1)} collective-permute-done((f32[48,512]{1,0:T(8,128)S(1)}, f32[48,512]{1,0:T(8,128)S(1)}, u32[]{:S(2)}, u32[]{:S(2)}) %collective-permute-start.27) | collective-permute-done | bytes 98336 | tf_op jit(solution)/shard_map/shared_0/ppermute | solution.py:498
  101.7 0.9 collective-permute-done.28.give_ref
  102.6 1.3 %close.1 = (f32[2,16,512]{2,1,0:T(8,128)}, f32[2,16]{1,0:T(2,128)}, f32[2,64,128]{2,1,0:T(8,128)}, f32[2,64]{1,0:T(2,128)}, f32[2,64]{1,0:T(2,128)}, /*index=5*/f32[1,2]{1,0:T(1,128)}, f32[8,128]{1,0:T(8,128)S(1)}) custom-call(s32[35]{0:T(128)S(1)} %concatenate.3.int_ref.refs_0_.spot_ref, f32[48,512]{1,0:T(8,128)S(1)} %add.17.keep_ref, ...), custom_call_target="tpu_custom_call" | custom-call | flops 300000000 | tf_op jit(solution)/shard_map/close/pallas_call | solution.py:56
  104.0 1.6 %collective-permute-done.23.refs_1_ = bf16[1,336,512]{2,1,0:T(8,128)(2,1)S(1)} collective-permute-done((bf16[1,336,512]{2,1,0:T(8,128)(2,1)S(1)}, bf16[1,336,512]{2,1,0:T(8,128)(2,1)S(1)}, u32[]{:S(2)}, u32[]{:S(2)}) %collective-permute-start.23) | collective-permute-done | bytes 344096 | tf_op jit(solution)/shard_map/near/ppermute | solution.py:498
  105.8 1.5 %input_sum.1 = (f32[1024,512]{1,0:T(8,128)}, f32[8,128]{1,0:T(8,128)S(1)}) custom-call(f32[1024,512]{1,0:T(8,128)S(1)} %input_0.1.refs_3_.refs_5_.refs_0_, bf16[1024,512]{1,0:T(8,128)(2,1)S(1)} %collective-permute-done.20.refs_1_, f32[1,336,512]{2,1,0:T(8,128)S(1)} %add.18.refs_2_.refs_1_), custom_call_target="tpu_custom_call" | custom-call | flops 450000000 | tf_op jit(solution)/shard_map/input_sum/pallas_call | solution.py:56
  107.9 1.6 %finish.1 = (f32[1,512,256]{2,1,0:T(8,128)}, f32[1,256]{1,0:T(1,128)}, f32[1,256,128]{2,1,0:T(8,128)}, f32[1,128]{1,0:T(1,128)}) custom-call(s32[35]{0:T(128)S(1)} %concatenate.3.int_ref.refs_0_.spot_ref, f32[1,336,512]{2,1,0:T(8,128)S(1)} %add.18.refs_2_.refs_1_, f32[1,336,512]{2,1,0:T(8,128)S(1)} %collective-permute-done.29.refs_2_, ...), custom_call_target="tpu_custom_call" | custom-call | flops 3000000000 | tf_op jit(solution)/shard_map/finish/pallas_call | solution.py:56
  (64 shorter events, 7.5 us)
Async XLA Ops:
  0.6 9.6 %collective-permute-start.1 = (bf16[1024,512]{1,0:T(8,128)(2,1)}, bf16[1024,512]{1,0:T(8,128)(2,1)S(1)}, u32[]{:S(2)}, u32[]{:S(2)}) collective-permute-start(bf16[1024,512]{1,0:T(8,128)(2,1)} %mine_ref.1), channel_id=1, source_target_pairs={{0,16},{16,0},{1,17},{17,1},{2,18},{18,2},{3,19},{19,3},{4,20},{20... | collective-permute-start | bytes 3145736 | tf_op jit(solution)/shard_map/inputs/ppermute | solution.py:502
  2.4 13.5 %collective-permute-start.2 = (bf16[1,336,512]{2,1,0:T(8,128)(2,1)S(1)}, bf16[1,336,512]{2,1,0:T(8,128)(2,1)S(1)}, u32[]{:S(2)}, u32[]{:S(2)}) collective-permute-start(bf16[1,336,512]{2,1,0:T(8,128)(2,1)S(1)} %pack.1), channel_id=1, source_target_pairs={{0,8},{1,9},{2,10},{3,11},{4,12},{5,13},{6,14},{7,15},{8,24},{9,25... | collective-permute-start | bytes 1032200 | tf_op jit(solution)/shard_map/deal/ppermute | solution.py:511
  6.0 4.3 %collective-permute-start = (s32[2,1024]{1,0:T(2,128)}, s32[2,1024]{1,0:T(2,128)S(1)}, u32[]{:S(2)}, u32[]{:S(2)}) collective-permute-start(s32[2,1024]{1,0:T(2,128)} %label_ref.1), channel_id=1, source_target_pairs={{0,16},{16,0},{1,17},{17,1},{2,18},{18,2},{3,19},{19,3},{4,20},{20... | collective-permute-start | bytes 24584 | tf_op jit(solution)/shard_map/labels/ppermute | solution.py:502
  6.0 16.5 %collective-permute-start.5 = (bf16[1,336,512]{2,1,0:T(8,128)(2,1)S(1)}, bf16[1,336,512]{2,1,0:T(8,128)(2,1)S(1)}, u32[]{:S(2)}, u32[]{:S(2)}) collective-permute-start(bf16[1,336,512]{2,1,0:T(8,128)(2,1)S(1)} %pack.1), channel_id=1, source_target_pairs={{0,4},{1,5},{2,6},{3,7},{4,0},{5,1},{6,2},{7,3},{24,28},{25,29},{2... | collective-permute-start | bytes 1032200 | tf_op jit(solution)/shard_map/owners_near/ppermute | solution.py:498
  10.3 1.2 %copy-start = (bf16[1024,512]{1,0:T(8,128)(2,1)S(1)}, bf16[1024,512]{1,0:T(8,128)(2,1)}, u32[]{:S(2)}) copy-start(bf16[1024,512]{1,0:T(8,128)(2,1)} %mine_ref.1) | copy-start | bytes 3145732
  11.5 0.8 copy-start.1
  12.3 0.7 copy-start.4
  13.0 0.7 copy-start.8
  15.9 10.0 %collective-permute-start.4 = (bf16[1,336,512]{2,1,0:T(8,128)(2,1)S(1)}, bf16[1,336,512]{2,1,0:T(8,128)(2,1)S(1)}, u32[]{:S(2)}, u32[]{:S(2)}) collective-permute-start(bf16[1,336,512]{2,1,0:T(8,128)(2,1)S(1)} %hold.3.refs_0_.refs_1_.refs_8_.refs_10_), channel_id=1, source_target_pairs={{0,1},{1,0},{2,3},{3,2},{4,5},{5,4},{6,7},{7,6},{8,9},{9,8},{10,11... | collective-permute-start | bytes 1032200 | tf_op jit(solution)/shard_map/pay_4/ppermute | solution.py:498
  17.5 8.5 %collective-permute-start.3 = (bf16[1,336,512]{2,1,0:T(8,128)(2,1)S(1)}, bf16[1,336,512]{2,1,0:T(8,128)(2,1)S(1)}, u32[]{:S(2)}, u32[]{:S(2)}) collective-permute-start(bf16[1,336,512]{2,1,0:T(8,128)(2,1)S(1)} %hold.3.refs_0_.refs_1_.refs_8_.refs_10_), channel_id=1, source_target_pairs={{0,2},{1,3},{2,0},{3,1},{4,6},{5,7},{6,4},{7,5},{8,10},{9,11},{10,... | collective-permute-start | bytes 1032200 | tf_op jit(solution)/shard_map/pay_2/ppermute | solution.py:498
  19.0 6.9 %collective-permute-start.7 = (bf16[1,336,512]{2,1,0:T(8,128)(2,1)S(1)}, bf16[1,336,512]{2,1,0:T(8,128)(2,1)S(1)}, u32[]{:S(2)}, u32[]{:S(2)}) collective-permute-start(bf16[1,336,512]{2,1,0:T(8,128)(2,1)S(1)} %hold.3.refs_0_.refs_1_.refs_8_.refs_10_), channel_id=1, source_target_pairs={{8,12},{9,13},{10,14},{11,15},{12,8},{13,9},{14,10},{15,11},{16,20... | collective-permute-start | bytes 1032200 | tf_op jit(solution)/shard_map/pay_1/ppermute | solution.py:498
  26.0 11.0 %collective-permute-start.8 = (bf16[1,336,512]{2,1,0:T(8,128)(2,1)S(1)}, bf16[1,336,512]{2,1,0:T(8,128)(2,1)S(1)}, u32[]{:S(2)}, u32[]{:S(2)}) collective-permute-start(bf16[1,336,512]{2,1,0:T(8,128)(2,1)S(1)} %add.10.refs_0_.refs_2_.refs_9_.refs_11_), channel_id=1, source_target_pairs={{0,2},{1,3},{2,0},{3,1},{4,6},{5,7},{6,4},{7,5},{8,10},{9,11},{10,... | collective-permute-start | bytes 1032200 | tf_op jit(solution)/shard_map/pay_3/ppermute | solution.py:498
  26.6 12.1 %collective-permute-start.10 = (bf16[1,336,512]{2,1,0:T(8,128)(2,1)S(1)}, bf16[1,336,512]{2,1,0:T(8,128)(2,1)S(1)}, u32[]{:S(2)}, u32[]{:S(2)}) collective-permute-start(bf16[1,336,512]{2,1,0:T(8,128)(2,1)S(1)} %add.10.refs_0_.refs_2_.refs_9_.refs_11_), channel_id=1, source_target_pairs={{0,1},{1,0},{2,3},{3,2},{4,5},{5,4},{6,7},{7,6},{8,9},{9,8},{10,11... | collective-permute-start | bytes 1032200 | tf_op jit(solution)/shard_map/pay_5/ppermute | solution.py:498
  28.1 15.6 %collective-permute-start.6 = (bf16[1,336,512]{2,1,0:T(8,128)(2,1)S(1)}, bf16[1,336,512]{2,1,0:T(8,128)(2,1)S(1)}, u32[]{:S(2)}, u32[]{:S(2)}) collective-permute-start(bf16[1,336,512]{2,1,0:T(8,128)(2,1)S(1)} %hold.4.refs_2_.refs_0_.refs_1_.refs_10_.refs_12_), channel_id=1, source_target_pairs={{0,1},{1,0},{2,3},{3,2},{4,5},{5,4},{6,7},{7,6},{8,9},{9,8},{10,11... | collective-permute-start | bytes 1032200 | tf_op jit(solution)/shard_map/pay_6/ppermute | solution.py:498
  37.0 7.3 %collective-permute-start.9 = (bf16[1,336,512]{2,1,0:T(8,128)(2,1)S(1)}, bf16[1,336,512]{2,1,0:T(8,128)(2,1)S(1)}, u32[]{:S(2)}, u32[]{:S(2)}) collective-permute-start(bf16[1,336,512]{2,1,0:T(8,128)(2,1)S(1)} %hold.5), channel_id=1, source_target_pairs={{0,1},{1,0},{2,3},{3,2},{4,5},{5,4},{6,7},{7,6},{8,9},{9,8},{10,11... | collective-permute-start | bytes 1032200 | tf_op jit(solution)/shard_map/pay_7/ppermute | solution.py:498
  46.7 3.1 %collective-permute-start.11 = (bf16[2,128,1024]{2,1,0:T(8,128)(2,1)S(1)}, bf16[2,128,1024]{2,1,0:T(8,128)(2,1)S(1)}, u32[]{:S(2)}, u32[]{:S(2)}) collective-permute-start(bf16[2,128,1024]{2,1,0:T(8,128)(2,1)S(1)} %get-tuple-element.118.refs_0_), channel_id=1, source_target_pairs={{0,16},{16,0},{1,17},{17,1},{2,18},{18,2},{3,19},{19,3},{4,20},{20... | collective-permute-start | bytes 1572872 | tf_op jit(solution)/shard_map/mixed_other/ppermute | solution.py:502
  46.8 3.0 %copy-start.3 = (bf16[2,128,64]{1,2,0:T(8,128)(2,1)S(1)}, bf16[2,128,64]{1,2,0:T(8,128)(2,1)}, u32[]{:S(2)}) copy-start(bf16[2,128,64]{1,2,0:T(8,128)(2,1)} %param.21) | copy-start | bytes 98308
  46.8 3.0 %copy-start.5 = (bf16[2]{0:T(256)(128)(2,1)S(1)}, bf16[2]{0:T(256)(128)(2,1)}, u32[]{:S(2)}) copy-start(bf16[2]{0:T(256)(128)(2,1)} %param.24) | copy-start | bytes 16
  46.8 3.0 %copy-start.6 = (bf16[2,64]{1,0:T(2,128)(2,1)S(1)}, bf16[2,64]{1,0:T(2,128)(2,1)}, u32[]{:S(2)}) copy-start(bf16[2,64]{1,0:T(2,128)(2,1)} %refs_6_.1) | copy-start | bytes 772
  46.9 3.0 %copy-start.7 = (bf16[2,64]{1,0:T(2,128)(2,1)S(1)}, bf16[2,64]{1,0:T(2,128)(2,1)}, u32[]{:S(2)}) copy-start(bf16[2,64]{1,0:T(2,128)(2,1)} %refs_7_.1) | copy-start | bytes 772
  49.3 2.6 %collective-permute-start.12 = (bf16[2,128,1024]{2,1,0:T(8,128)(2,1)S(1)}, bf16[2,128,1024]{2,1,0:T(8,128)(2,1)S(1)}, u32[]{:S(2)}, u32[]{:S(2)}) collective-permute-start(bf16[2,128,1024]{2,1,0:T(8,128)(2,1)S(1)} %get-tuple-element.117.mix_ref), channel_id=1, source_target_pairs={{0,16},{16,0},{1,17},{17,1},{2,18},{18,2},{3,19},{19,3},{4,20},{20... | collective-permute-start | bytes 1572872 | tf_op jit(solution)/shard_map/mixed_own/ppermute | solution.py:502
  56.3 12.4 %collective-permute-start.15 = (bf16[1,336,512]{2,1,0:T(8,128)(2,1)S(1)}, bf16[1,336,512]{2,1,0:T(8,128)(2,1)S(1)}, u32[]{:S(2)}, u32[]{:S(2)}) collective-permute-start(bf16[1,336,512]{2,1,0:T(8,128)(2,1)S(1)} %get-tuple-element.165), channel_id=1, source_target_pairs={{0,1},{1,0},{2,3},{3,2},{4,5},{5,4},{6,7},{7,6},{8,9},{9,8},{10,11... | collective-permute-start | bytes 1032200 | tf_op jit(solution)/shard_map/grad_six/ppermute | solution.py:498
  58.0 10.8 %collective-permute-start.16 = (bf16[1,336,512]{2,1,0:T(8,128)(2,1)S(1)}, bf16[1,336,512]{2,1,0:T(8,128)(2,1)S(1)}, u32[]{:S(2)}, u32[]{:S(2)}) collective-permute-start(bf16[1,336,512]{2,1,0:T(8,128)(2,1)S(1)} %get-tuple-element.166), channel_id=1, source_target_pairs={{0,1},{1,0},{2,3},{3,2},{4,5},{5,4},{6,7},{7,6},{8,9},{9,8},{10,11... | collective-permute-start | bytes 1032200 | tf_op jit(solution)/shard_map/grad_seven/ppermute | solution.py:498
  61.2 17.8 %collective-permute-start.13 = (bf16[1,336,512]{2,1,0:T(8,128)(2,1)S(1)}, bf16[1,336,512]{2,1,0:T(8,128)(2,1)S(1)}, u32[]{:S(2)}, u32[]{:S(2)}) collective-permute-start(bf16[1,336,512]{2,1,0:T(8,128)(2,1)S(1)} %get-tuple-element.157), channel_id=1, source_target_pairs={{0,1},{1,0},{2,3},{3,2},{4,5},{5,4},{6,7},{7,6},{8,9},{9,8},{10,11... | collective-permute-start | bytes 1032200 | tf_op jit(solution)/shard_map/grad_four/ppermute | solution.py:498
  62.8 16.2 %collective-permute-start.14 = (bf16[1,336,512]{2,1,0:T(8,128)(2,1)S(1)}, bf16[1,336,512]{2,1,0:T(8,128)(2,1)S(1)}, u32[]{:S(2)}, u32[]{:S(2)}) collective-permute-start(bf16[1,336,512]{2,1,0:T(8,128)(2,1)S(1)} %get-tuple-element.158), channel_id=1, source_target_pairs={{0,1},{1,0},{2,3},{3,2},{4,5},{5,4},{6,7},{7,6},{8,9},{9,8},{10,11... | collective-permute-start | bytes 1032200 | tf_op jit(solution)/shard_map/grad_five/ppermute | solution.py:498
  66.8 1.4 %collective-permute-start.17 = (f32[48,512]{1,0:T(8,128)S(1)}, f32[48,512]{1,0:T(8,128)S(1)}, u32[]{:S(2)}, u32[]{:S(2)}) collective-permute-start(f32[48,512]{1,0:T(8,128)S(1)} %get-tuple-element.168), channel_id=1, source_target_pairs={{0,16},{16,0},{1,17},{17,1},{2,18},{18,2},{3,19},{19,3},{4,20},{20... | collective-permute-start | bytes 294920 | tf_op jit(solution)/shard_map/give/ppermute | solution.py:502
  68.2 5.5 %collective-permute-start.18 = (f32[48,512]{1,0:T(8,128)S(1)}, f32[48,512]{1,0:T(8,128)S(1)}, u32[]{:S(2)}, u32[]{:S(2)}) collective-permute-start(f32[48,512]{1,0:T(8,128)S(1)} %add.11.refs_13_.refs_0_), channel_id=1, source_target_pairs={{0,4},{1,5},{2,6},{3,7},{4,0},{5,1},{6,2},{7,3},{8,12},{9,13},{10,... | collective-permute-start | bytes 294920 | tf_op jit(solution)/shard_map/shared_2/ppermute | solution.py:498
  71.6 14.7 %collective-permute-start.21 = (bf16[1,336,512]{2,1,0:T(8,128)(2,1)S(1)}, bf16[1,336,512]{2,1,0:T(8,128)(2,1)S(1)}, u32[]{:S(2)}, u32[]{:S(2)}) collective-permute-start(bf16[1,336,512]{2,1,0:T(8,128)(2,1)S(1)} %get-tuple-element.176), channel_id=1, source_target_pairs={{0,2},{1,3},{2,0},{3,1},{4,6},{5,7},{6,4},{7,5},{8,10},{9,11},{10,... | collective-permute-start | bytes 1032200 | tf_op jit(solution)/shard_map/grad_two/ppermute | solution.py:498
  72.7 15.1 %collective-permute-start.22 = (bf16[1,336,512]{2,1,0:T(8,128)(2,1)S(1)}, bf16[1,336,512]{2,1,0:T(8,128)(2,1)S(1)}, u32[]{:S(2)}, u32[]{:S(2)}) collective-permute-start(bf16[1,336,512]{2,1,0:T(8,128)(2,1)S(1)} %get-tuple-element.179), channel_id=1, source_target_pairs={{0,2},{1,3},{2,0},{3,1},{4,6},{5,7},{6,4},{7,5},{8,10},{9,11},{10,... | collective-permute-start | bytes 1032200 | tf_op jit(solution)/shard_map/grad_three/ppermute | solution.py:498
  73.7 9.4 %collective-permute-start.19 = (f32[48,512]{1,0:T(8,128)S(1)}, f32[48,512]{1,0:T(8,128)S(1)}, u32[]{:S(2)}, u32[]{:S(2)}) collective-permute-start(f32[48,512]{1,0:T(8,128)S(1)} %add.12.refs_14_.refs_0_), channel_id=1, source_target_pairs={{0,8},{1,9},{2,10},{3,11},{4,12},{5,13},{6,14},{7,15},{8,0},{9,1},... | collective-permute-start | bytes 294920 | tf_op jit(solution)/shard_map/shared_3/ppermute | solution.py:498
  79.0 4.1 %copy-start.2 = (bf16[2,512,16]{1,2,0:T(8,128)(2,1)S(1)}, bf16[2,512,16]{1,2,0:T(8,128)(2,1)}, u32[]{:S(2)}) copy-start(bf16[2,512,16]{1,2,0:T(8,128)(2,1)} %param.19) | copy-start | bytes 98308
  86.2 19.5 %collective-permute-start.20 = (bf16[1024,512]{1,0:T(8,128)(2,1)S(1)}, bf16[1024,512]{1,0:T(8,128)(2,1)S(1)}, u32[]{:S(2)}, u32[]{:S(2)}) collective-permute-start(bf16[1024,512]{1,0:T(8,128)(2,1)S(1)} %input_1.1.refs_2_), channel_id=1, source_target_pairs={{0,16},{16,0},{1,17},{17,1},{2,18},{18,2},{3,19},{19,3},{4,20},{20... | collective-permute-start | bytes 3145736 | tf_op jit(solution)/shard_map/over/ppermute | solution.py:502
  86.4 17.5 %collective-permute-start.25 = (bf16[1,336,512]{2,1,0:T(8,128)(2,1)S(1)}, bf16[1,336,512]{2,1,0:T(8,128)(2,1)S(1)}, u32[]{:S(2)}, u32[]{:S(2)}) collective-permute-start(bf16[1,336,512]{2,1,0:T(8,128)(2,1)S(1)} %get-tuple-element.180.refs_2_), channel_id=1, source_target_pairs={{8,0},{9,1},{10,2},{11,3},{12,4},{13,5},{14,6},{15,7},{16,24},{17,... | collective-permute-start | bytes 1032200 | tf_op jit(solution)/shard_map/far/ppermute | solution.py:498
  87.8 16.1 %collective-permute-start.24 = (bf16[1,336,512]{2,1,0:T(8,128)(2,1)S(1)}, bf16[1,336,512]{2,1,0:T(8,128)(2,1)S(1)}, u32[]{:S(2)}, u32[]{:S(2)}) collective-permute-start(bf16[1,336,512]{2,1,0:T(8,128)(2,1)S(1)} %add.15), channel_id=1, source_target_pairs={{8,4},{9,5},{10,6},{11,7},{12,0},{13,1},{14,2},{15,3},{16,28},{17,... | collective-permute-start | bytes 1032200 | tf_op jit(solution)/shard_map/cross/ppermute | solution.py:498
  89.1 16.4 %collective-permute-start.23 = (bf16[1,336,512]{2,1,0:T(8,128)(2,1)S(1)}, bf16[1,336,512]{2,1,0:T(8,128)(2,1)S(1)}, u32[]{:S(2)}, u32[]{:S(2)}) collective-permute-start(bf16[1,336,512]{2,1,0:T(8,128)(2,1)S(1)} %add.15), channel_id=1, source_target_pairs={{0,4},{1,5},{2,6},{3,7},{4,0},{5,1},{6,2},{7,3},{24,28},{25,29},{2... | collective-permute-start | bytes 1032200 | tf_op jit(solution)/shard_map/near/ppermute | solution.py:498
  91.0 4.7 %collective-permute-start.26 = (f32[48,512]{1,0:T(8,128)S(1)}, f32[48,512]{1,0:T(8,128)S(1)}, u32[]{:S(2)}, u32[]{:S(2)}) collective-permute-start(f32[48,512]{1,0:T(8,128)S(1)} %add.13.refs_18_.refs_0_), channel_id=1, source_target_pairs={{0,2},{1,3},{2,0},{3,1},{4,6},{5,7},{6,4},{7,5},{8,10},{9,11},{10,... | collective-permute-start | bytes 294920 | tf_op jit(solution)/shard_map/shared_1/ppermute | solution.py:498
  95.7 5.3 %collective-permute-start.27 = (f32[48,512]{1,0:T(8,128)S(1)}, f32[48,512]{1,0:T(8,128)S(1)}, u32[]{:S(2)}, u32[]{:S(2)}) collective-permute-start(f32[48,512]{1,0:T(8,128)S(1)} %add.16.refs_0_), channel_id=1, source_target_pairs={{0,1},{1,0},{2,3},{3,2},{4,5},{5,4},{6,7},{7,6},{8,9},{9,8},{10,11... | collective-permute-start | bytes 294920 | tf_op jit(solution)/shard_map/shared_0/ppermute | solution.py:498
  101.0 1.6 %collective-permute-start.28 = (f32[48,512]{1,0:T(8,128)S(1)}, f32[48,512]{1,0:T(8,128)S(1)}, u32[]{:S(2)}, u32[]{:S(2)}) collective-permute-start(f32[48,512]{1,0:T(8,128)S(1)} %add.17.keep_ref), channel_id=1, source_target_pairs={{0,16},{16,0},{1,17},{17,1},{2,18},{18,2},{3,19},{19,3},{4,20},{20... | collective-permute-start | bytes 294920 | tf_op jit(solution)/shard_map/keep/ppermute | solution.py:502
  105.7 2.2 %collective-permute-start.29 = (f32[1,336,512]{2,1,0:T(8,128)S(1)}, f32[1,336,512]{2,1,0:T(8,128)S(1)}, u32[]{:S(2)}, u32[]{:S(2)}) collective-permute-start(f32[1,336,512]{2,1,0:T(8,128)S(1)} %add.18.refs_2_.refs_1_), channel_id=1, source_target_pairs={{0,16},{16,0},{1,17},{17,1},{2,18},{18,2},{3,19},{19,3},{4,20},{20... | collective-permute-start | bytes 2064392 | tf_op jit(solution)/shard_map/final/ppermute | solution.py:502

commit v3 on v2

--- a/solution.py
+++ b/solution.py
@@ -647,7 +647,7 @@
     grad_two, grad_three, ones[2], ones[3] = back(2, 3, (six, seven), BF16, 1, [keep])
     three, two = send("grad_three", grad_three, mid_bit), send("grad_two", grad_two, mid_bit)
     stages = []
-    for b in range(2, bits):
+    for b in (bits - 1, *range(2, bits - 1)):
         (keep,) = add([keep, send(f"shared_{b}", keep, (b, b))], [F32], [ones[3]])
         stages.append(keep)
 

time: 110 us -> 109 us (level)
  waiting for transfers between devices: 15.7 us -> 14 us
    ppermute x21, waiting for transfers between devices: 12.8 us -> 10.9 us  [send(): return lax.ppermute(value, ('dp', 'expert'), pairs(bit_of_core, want, also))]
    ppermute x21, starting transfers between devices: 29.6 us -> 31 us  [send(): return lax.ppermute(value, ('dp', 'expert'), pairs(bit_of_core, want, also))]
  transfers between devices with their start and end apart: 30 -> 30, of which waited for: 10 -> 9; matrix products, arithmetic and copies ran while one was open for 1% -> 1% of each run, Pallas kernels for 41% -> 41%
where the time goes in v3:
time: 109 us
  Pallas kernels  53.4 us (49%)
  starting transfers between devices  36.2 us (33%)
  waiting for transfers between devices  14 us (13%)
  local copies, waits for them, and re-layouts  4.13 us (4%)
    pallas_call x27, Pallas kernels, call(): pl.pallas_call(body, name=name, in_specs=[SMEM] * scalars + [VMEM] * (cou...  50 us
    ppermute x21, starting transfers between devices, send(): return lax.ppermute(value, ('dp', 'expert'), pairs(bit_of_core, want, also))  31 us
    ppermute x21, waiting for transfers between devices, send(): return lax.ppermute(value, ('dp', 'expert'), pairs(bit_of_core, want, also))  10.9 us
    ppermute x1, starting transfers between devices, deal(): return lax.ppermute(value, ('dp', 'expert'), route)  3.66 us
    unnamed x19, local copies, waits for them, and re-layouts  3.38 us
    ppermute x8, waiting for transfers between devices, swap(): return lax.ppermute(value, 'dp', [(0, 1), (1, 0)])  3.09 us
    pallas_call x1, Pallas kernels, per_device(): pl.pallas_call(functools.partial(gate_kernel, masks, group_len.shape[0]),...  2.26 us
  transfers between devices with their start and end apart: 30, of which 9 were waited for; matrix products, arithmetic and copies ran while one was open for 1% of the time, Pallas kernels for 41%

profile of v3, /device:TPU:0, one launch (start us, length us, event | category | flops | bytes accessed | tf_op | source)
XLA Modules:
  0.0 108.9 jit_solution(11977388004522675123)
XLA Ops:
  1.2 1.2 %pack.1 = bf16[1,336,512]{2,1,0:T(8,128)(2,1)S(1)} custom-call(bf16[1,512,256]{2,1,0:T(8,128)(2,1)} %w1_ref.1, bf16[1,256,128]{2,1,0:T(8,128)(2,1)} %w2_ref.1, bf16[1,256]{1,0:T(2,128)(2,1)} %b1_ref.1, bf16[1,128]{1,0:T(2,128)(2,1)} %b2_ref.1), custom_call_target="tpu_custom_call" | custom-call | tf_op jit(solution)/shard_map/pack/pallas_call | solution.py:135
  2.4 3.7 %collective-permute-start.2 = (bf16[1,336,512]{2,1,0:T(8,128)(2,1)S(1)}, bf16[1,336,512]{2,1,0:T(8,128)(2,1)S(1)}, u32[]{:S(2)}, u32[]{:S(2)}) collective-permute-start(bf16[1,336,512]{2,1,0:T(8,128)(2,1)S(1)} %pack.1), channel_id=1, source_target_pairs={{0,8},{1,9},{2,10},{3,11},{4,12},{5,13},{6,14},{7,15},{8,24},{9,25... | collective-permute-start | bytes 1032200 | tf_op jit(solution)/shard_map/deal/ppermute | solution.py:511
  6.0 3.5 %collective-permute-start.5 = (bf16[1,336,512]{2,1,0:T(8,128)(2,1)S(1)}, bf16[1,336,512]{2,1,0:T(8,128)(2,1)S(1)}, u32[]{:S(2)}, u32[]{:S(2)}) collective-permute-start(bf16[1,336,512]{2,1,0:T(8,128)(2,1)S(1)} %pack.1), channel_id=1, source_target_pairs={{0,4},{1,5},{2,6},{3,7},{4,0},{5,1},{6,2},{7,3},{24,28},{25,29},{2... | collective-permute-start | bytes 1032200 | tf_op jit(solution)/shard_map/owners_near/ppermute | solution.py:498
  9.5 0.7 concatenate.3.int_ref.refs_0_.spot_ref
  10.3 1.2 %copy-done = bf16[1024,512]{1,0:T(8,128)(2,1)S(1)} copy-done((bf16[1024,512]{1,0:T(8,128)(2,1)S(1)}, bf16[1024,512]{1,0:T(8,128)(2,1)}, u32[]{:S(2)}) %copy-start) | copy-done | bytes 1048600
  11.5 0.8 copy-done.1
  12.3 0.7 copy-done.4
  13.0 0.7 copy-done.8
  13.6 2.3 %gate.1 = (f32[8,2,2048]{2,1,0:T(2,128)S(1)}, f32[8,2,2048]{2,1,0:T(2,128)S(1)}, f32[1,2048]{1,0:T(1,128)S(1)}, bf16[2048,512]{1,0:T(8,128)(2,1)S(1)}, f32[2,2048]{1,0:T(2,128)S(1)}) custom-call(s32[35]{0:T(128)S(1)} %concatenate.3.int_ref.refs_0_.spot_ref, s32[2,1024]{1,0:T(2,128)S(1)} %copy-done.4, s32[2,1024]{1,0:T(2,128)S(1)} %collective-permute-done.there_ref, ...), custom_call_target="tpu_custom_call" | custom-call | tf_op jit(solution)/shard_map/gate/pallas_call | solution.py:540
  15.9 1.6 %collective-permute-start.4 = (bf16[1,336,512]{2,1,0:T(8,128)(2,1)S(1)}, bf16[1,336,512]{2,1,0:T(8,128)(2,1)S(1)}, u32[]{:S(2)}, u32[]{:S(2)}) collective-permute-start(bf16[1,336,512]{2,1,0:T(8,128)(2,1)S(1)} %hold.3.refs_0_.refs_1_.refs_8_.refs_10_), channel_id=1, source_target_pairs={{0,1},{1,0},{2,3},{3,2},{4,5},{5,4},{6,7},{7,6},{8,9},{9,8},{10,11... | collective-permute-start | bytes 1032200 | tf_op jit(solution)/shard_map/pay_4/ppermute | solution.py:498
  17.5 1.5 %collective-permute-start.3 = (bf16[1,336,512]{2,1,0:T(8,128)(2,1)S(1)}, bf16[1,336,512]{2,1,0:T(8,128)(2,1)S(1)}, u32[]{:S(2)}, u32[]{:S(2)}) collective-permute-start(bf16[1,336,512]{2,1,0:T(8,128)(2,1)S(1)} %hold.3.refs_0_.refs_1_.refs_8_.refs_10_), channel_id=1, source_target_pairs={{0,2},{1,3},{2,0},{3,1},{4,6},{5,7},{6,4},{7,5},{8,10},{9,11},{10,... | collective-permute-start | bytes 1032200 | tf_op jit(solution)/shard_map/pay_2/ppermute | solution.py:498
  19.0 0.7 collective-permute-start.7
  19.7 2.9 %forward_0.1 = (bf16[1,256,2048]{2,1,0:T(8,128)(2,1)S(1)}, bf16[1,256,2048]{2,1,0:T(8,128)(2,1)S(1)}, bf16[1,128,2048]{2,1,0:T(8,128)(2,1)S(1)}, f32[1,128,2048]{2,1,0:T(8,128)S(1)}, f32[2,128,2048]{2,1,0:T(8,128)S(1)}) custom-call(bf16[2048,512]{1,0:T(8,128)(2,1)S(1)} %get-tuple-element.103.x_ref.refs_0_.refs_1_, ...), custom_call_target="tpu_custom_call" | custom-call | flops 675000000 | tf_op jit(solution)/shard_map/forward_0/pallas_call | solution.py:56
  22.6 3.3 %collective-permute-done.4.refs_1_.refs_12_.refs_14_ = bf16[1,336,512]{2,1,0:T(8,128)(2,1)S(1)} collective-permute-done((bf16[1,336,512]{2,1,0:T(8,128)(2,1)S(1)}, bf16[1,336,512]{2,1,0:T(8,128)(2,1)S(1)}, u32[]{:S(2)}, u32[]{:S(2)}) %collective-permute-start.4) | collective-permute-done | bytes 344096 | tf_op jit(solution)/shard_map/pay_4/ppermute | solution.py:498
  26.6 1.5 %collective-permute-start.10 = (bf16[1,336,512]{2,1,0:T(8,128)(2,1)S(1)}, bf16[1,336,512]{2,1,0:T(8,128)(2,1)S(1)}, u32[]{:S(2)}, u32[]{:S(2)}) collective-permute-start(bf16[1,336,512]{2,1,0:T(8,128)(2,1)S(1)} %add.10.refs_0_.refs_2_.refs_9_.refs_11_), channel_id=1, source_target_pairs={{0,1},{1,0},{2,3},{3,2},{4,5},{5,4},{6,7},{7,6},{8,9},{9,8},{10,11... | collective-permute-start | bytes 1032200 | tf_op jit(solution)/shard_map/pay_5/ppermute | solution.py:498
  28.6 4.9 %forward_14.1 = (bf16[1,256,2048]{2,1,0:T(8,128)(2,1)S(1)}, bf16[1,256,2048]{2,1,0:T(8,128)(2,1)S(1)}, bf16[1,128,2048]{2,1,0:T(8,128)(2,1)S(1)}, f32[1,128,2048...) custom-call(bf16[2048,512]{1,0:T(8,128)(2,1)S(1)} %get-tuple-element, ...), custom_call_target="tpu_custom_call" | custom-call | flops 1350000000 | tf_op jit(solution)/shard_map/forward_14/pallas_call | solution.py:56
  33.5 2.9 %forward_2.1 = (bf16[1,256,2048]{2,1,0:T(8,128)(2,1)S(1)}, bf16[1,256,2048]{2,1,0:T(8,128)(2,1)S(1)}, bf16[1,128,2048]{2,1,0:T(8,128)(2,1)S(1)}, f32[1,128,2048]{2,1,0:T(8,128)S(1)}, f32[2,128,2048]{2,1,0:T(8,128)S(1)}) custom-call(bf16[2048,512]{1,0:T(8,128)(2,1)S(1)} %get-tuple-element.103.x_ref.refs_0_.refs_1_, ...), custom_call_target="tpu_custom_call" | custom-call | flops 675000000 | tf_op jit(solution)/shard_map/forward_2/pallas_call | solution.py:56
  36.4 0.6 collective-permute-done.8.refs_0_.refs_2_.refs_11_.refs_13_
  37.0 1.6 %collective-permute-start.9 = (bf16[1,336,512]{2,1,0:T(8,128)(2,1)S(1)}, bf16[1,336,512]{2,1,0:T(8,128)(2,1)S(1)}, u32[]{:S(2)}, u32[]{:S(2)}) collective-permute-start(bf16[1,336,512]{2,1,0:T(8,128)(2,1)S(1)} %hold.5), channel_id=1, source_target_pairs={{0,1},{1,0},{2,3},{3,2},{4,5},{5,4},{6,7},{7,6},{8,9},{9,8},{10,11... | collective-permute-start | bytes 1032200 | tf_op jit(solution)/shard_map/pay_7/ppermute | solution.py:498
  38.7 5.1 %forward_35.1 = (bf16[1,256,2048]{2,1,0:T(8,128)(2,1)S(1)}, bf16[1,256,2048]{2,1,0:T(8,128)(2,1)S(1)}, bf16[1,128,2048]{2,1,0:T(8,128)(2,1)S(1)}, f32[1,128,2048...) custom-call(bf16[2048,512]{1,0:T(8,128)(2,1)S(1)} %get-tuple-element, ...), custom_call_target="tpu_custom_call" | custom-call | flops 1350000000 | tf_op jit(solution)/shard_map/forward_35/pallas_call | solution.py:56
  44.3 2.4 %forward_67_other.1 = (bf16[1,256,2048]{2,1,0:T(8,128)(2,1)S(1)}, bf16[1,256,2048]{2,1,0:T(8,128)(2,1)S(1)}, bf16[1,128,2048]{2,1,0:T(8,128)(2,1)S(1)}, f32[1,12...) custom-call(bf16[2048,512]{1,0:T(8,128)(2,1)S(1)} %get-tuple-element, ...), custom_call_target="tpu_custom_call" | custom-call | flops 675000000 | tf_op jit(solution)/shard_map/forward_67_other/pallas_call | solution.py:56
  46.9 2.4 %forward_67_own.1 = (bf16[1,256,2048]{2,1,0:T(8,128)(2,1)S(1)}, bf16[1,256,2048]{2,1,0:T(8,128)(2,1)S(1)}, bf16[1,128,2048]{2,1,0:T(8,128)(2,1)S(1)}, f32[1,128,...) custom-call(bf16[2048,512]{1,0:T(8,128)(2,1)S(1)} %get-tuple-element, ...), custom_call_target="tpu_custom_call", output_to_operand_aliasing={{0}: (5, {}), {1}: (6, {}), {2}: (7, {}), {3}: (8, {}), {4}... | custom-call | flops 675000000 | tf_op jit(solution)/shard_map/forward_67_own/pallas_call | solution.py:56
  49.8 2.1 %tower_own.1 = (f32[2,128,2048]{2,1,0:T(8,128)S(1)}, f32[2,2048]{1,0:T(2,128)S(1)}, f32[2,1024]{1,0:T(2,128)}, f32[48,512]{1,0:T(8,128)S(1)}) custom-call(bf16[2,128,1024]{2,1,0:T(8,128)(2,1)S(1)} %get-tuple-element.117.mix_ref, bf16[2,128,1024]{2,1,0:T(8,128)(2,1)S(1)} %collective-permute-done.11.come_ref, ...), custom_call_target="tpu_custom_call" | custom-call | flops 600000000 | tf_op jit(solution)/shard_map/tower_own/pallas_call | solution.py:56
  51.9 1.6 %tower_other.1 = (f32[2,128,2048]{2,1,0:T(8,128)S(1)}, f32[2,2048]{1,0:T(2,128)S(1)}) custom-call(bf16[2,128,1024]{2,1,0:T(8,128)(2,1)S(1)} %get-tuple-element.118.refs_0_, bf16[2,128,1024]{2,1,0:T(8,128)(2,1)S(1)} %collective-permute-done.12.refs_1_, ...), custom_call_target="tpu_custom_call", output_to_operand_aliasing={{0}: (8, {}), {1}: (9, {})} | custom-call | flops 600000000 | tf_op jit(solution)/shard_map/tower_other/pallas_call | solution.py:56
  53.5 2.8 %backward_67.1 = (bf16[1,336,512]{2,1,0:T(8,128)(2,1)S(1)}, bf16[1,336,512]{2,1,0:T(8,128)(2,1)S(1)}, bf16[1,256,2048]{2,1,0:T(8,128)(2,1)S(1)}, bf16[1,256,2048]{2,1,0:T(8,128)(2,1)S(1)}) custom-call(bf16[2048,512]{1,0:T(8,128)(2,1)S(1)} %get-tuple-element.103.x_ref.refs_0_.refs_1_, ...), custom_call_target="tpu_custom_call" | custom-call | flops 1500000000 | tf_op jit(solution)/shard_map/backward_67/pallas_call | solution.py:56
  56.3 1.6 %collective-permute-start.15 = (bf16[1,336,512]{2,1,0:T(8,128)(2,1)S(1)}, bf16[1,336,512]{2,1,0:T(8,128)(2,1)S(1)}, u32[]{:S(2)}, u32[]{:S(2)}) collective-permute-start(bf16[1,336,512]{2,1,0:T(8,128)(2,1)S(1)} %get-tuple-element.165), channel_id=1, source_target_pairs={{0,1},{1,0},{2,3},{3,2},{4,5},{5,4},{6,7},{7,6},{8,9},{9,8},{10,11... | collective-permute-start | bytes 1032200 | tf_op jit(solution)/shard_map/grad_six/ppermute | solution.py:498
  58.4 2.8 %backward_45.1 = (bf16[1,336,512]{2,1,0:T(8,128)(2,1)S(1)}, bf16[1,336,512]{2,1,0:T(8,128)(2,1)S(1)}, bf16[1,256,2048]{2,1,0:T(8,128)(2,1)S(1)}, bf16[1,256,2048]{2,1,0:T(8,128)(2,1)S(1)}) custom-call(bf16[2048,512]{1,0:T(8,128)(2,1)S(1)} %get-tuple-element.103.x_ref.refs_0_.refs_1_, ...), custom_call_target="tpu_custom_call" | custom-call | flops 300000000 | tf_op jit(solution)/shard_map/backward_45/pallas_call | solution.py:56
  61.2 1.6 %collective-permute-start.13 = (bf16[1,336,512]{2,1,0:T(8,128)(2,1)S(1)}, bf16[1,336,512]{2,1,0:T(8,128)(2,1)S(1)}, u32[]{:S(2)}, u32[]{:S(2)}) collective-permute-start(bf16[1,336,512]{2,1,0:T(8,128)(2,1)S(1)} %get-tuple-element.157), channel_id=1, source_target_pairs={{0,1},{1,0},{2,3},{3,2},{4,5},{5,4},{6,7},{7,6},{8,9},{9,8},{10,11... | collective-permute-start | bytes 1032200 | tf_op jit(solution)/shard_map/grad_four/ppermute | solution.py:498
  63.3 3.5 %gate_back.1 = (bf16[32,2048]{1,0:T(8,128)(2,1)S(1)}, f32[48,512]{1,0:T(8,128)S(1)}, f32[48,512]{1,0:T(8,128)S(1)}) custom-call(s32[35]{0:T(128)S(1)} %concatenate.3.int_ref.refs_0_.spot_ref, bf16[2048,512]{1,0:T(8,128)(2,1)S(1)} %get-tuple-element.103.x_ref.refs_0_.refs_1_, f32[2,128,2048]{2,1,0:T(8,128)S(1)} %get-tuple-element.124.dmix_ref.refs_4_.refs_2_, ...), custom_call_target="tpu_custom_call" | custom-call | flops 300000000 | tf_op jit(solution)/shard_map/gate_back/pallas_call | solution.py:56
  66.9 1.3 %collective-permute-done.17.refs_1_ = f32[48,512]{1,0:T(8,128)S(1)} collective-permute-done((f32[48,512]{1,0:T(8,128)S(1)}, f32[48,512]{1,0:T(8,128)S(1)}, u32[]{:S(2)}, u32[]{:S(2)}) %collective-permute-start.17) | collective-permute-done | bytes 98336 | tf_op jit(solution)/shard_map/give/ppermute | solution.py:502
  68.2 3.8 %collective-permute-start.18 = (f32[48,512]{1,0:T(8,128)S(1)}, f32[48,512]{1,0:T(8,128)S(1)}, u32[]{:S(2)}, u32[]{:S(2)}) collective-permute-start(f32[48,512]{1,0:T(8,128)S(1)} %add.11.refs_13_.refs_0_), channel_id=1, source_target_pairs={{0,8},{1,9},{2,10},{3,11},{4,12},{5,13},{6,14},{7,15},{8,0},{9,1},... | collective-permute-start | bytes 294920 | tf_op jit(solution)/shard_map/shared_3/ppermute | solution.py:498
  72.0 2.8 %backward_23.1 = (bf16[1,336,512]{2,1,0:T(8,128)(2,1)S(1)}, bf16[1,336,512]{2,1,0:T(8,128)(2,1)S(1)}, bf16[1,256,2048]{2,1,0:T(8,128)(2,1)S(1)}, bf16[1,256,2048]{2,1,0:T(8,128)(2,1)S(1)}) custom-call(bf16[2048,512]{1,0:T(8,128)(2,1)S(1)} %get-tuple-element.103.x_ref.refs_0_.refs_1_, bf16[1,336,512]{2,1,0:T(8,128)(2,1)S(1)} %hold.4.refs_2_.refs_0_.refs_1_.refs_10_.refs_12_, ...), custom_call_target="tpu_custom_call" | custom-call | flops 300000000 | tf_op jit(solution)/shard_map/backward_23/pallas_call | solution.py:56
  74.8 0.9 collective-permute-start.21
  75.8 1.2 %collective-permute-start.22 = (bf16[1,336,512]{2,1,0:T(8,128)(2,1)S(1)}, bf16[1,336,512]{2,1,0:T(8,128)(2,1)S(1)}, u32[]{:S(2)}, u32[]{:S(2)}) collective-permute-start(bf16[1,336,512]{2,1,0:T(8,128)(2,1)S(1)} %get-tuple-element.179), channel_id=1, source_target_pairs={{0,2},{1,3},{2,0},{3,1},{4,6},{5,7},{6,4},{7,5},{8,10},{9,11},{10,... | collective-permute-start | bytes 1032200 | tf_op jit(solution)/shard_map/grad_three/ppermute | solution.py:498
  77.2 1.8 %collective-permute-start.19 = (f32[48,512]{1,0:T(8,128)S(1)}, f32[48,512]{1,0:T(8,128)S(1)}, u32[]{:S(2)}, u32[]{:S(2)}) collective-permute-start(f32[48,512]{1,0:T(8,128)S(1)} %add.12.refs_14_.refs_0_), channel_id=1, source_target_pairs={{0,4},{1,5},{2,6},{3,7},{4,0},{5,1},{6,2},{7,3},{8,12},{9,13},{10,... | collective-permute-start | bytes 294920 | tf_op jit(solution)/shard_map/shared_2/ppermute | solution.py:498
  79.0 2.8 %backward_01.1 = (f32[1,336,512]{2,1,0:T(8,128)S(1)}, f32[1,336,512]{2,1,0:T(8,128)S(1)}, bf16[1,256,2048]{2,1,0:T(8,128)(2,1)S(1)}, bf16[1,256,2048]{2,1,0:T(8,128)(2,1)S(1)}) custom-call(bf16[2048,512]{1,0:T(8,128)(2,1)S(1)} %get-tuple-element.103.x_ref.refs_0_.refs_1_, bf16[1,336,512]{2,1,0:T(8,128)(2,1)S(1)} %hold.3.refs_0_.refs_1_.refs_8_.refs_10_, ...), custom_call_target="tpu_custom_call" | custom-call | flops 300000000 | tf_op jit(solution)/shard_map/backward_01/pallas_call | solution.py:56
  81.9 3.1 %input_1.1.refs_2_ = bf16[1024,512]{1,0:T(8,128)(2,1)S(1)} custom-call(bf16[32,2048]{1,0:T(8,128)(2,1)S(1)} %get-tuple-element.150.dgate_ref.refs_0_, bf16[2,16,512]{2,1,0:T(8,128)(2,1)S(1)} %bitcast.10, bf16[1,256,2048]{2,1,0:T(8,128)(2,1)S(1)} %get-tuple-element.170.refs_0_.refs_2_, bf16[1,256,2048]{2,1,0:T(8,128)(2,1)S(1)} %get-tuple-element.171.refs_1_.refs_3_, ...), custom_call_target="tpu_custom_call" | custom-call | flops 1050000000 | tf_op jit(solution)/shard_map/input_1/pallas_call | solution.py:56
  85.2 1.3 %collective-permute-start.25 = (bf16[1,336,512]{2,1,0:T(8,128)(2,1)S(1)}, bf16[1,336,512]{2,1,0:T(8,128)(2,1)S(1)}, u32[]{:S(2)}, u32[]{:S(2)}) collective-permute-start(bf16[1,336,512]{2,1,0:T(8,128)(2,1)S(1)} %get-tuple-element.180.refs_2_), channel_id=1, source_target_pairs={{8,0},{9,1},{10,2},{11,3},{12,4},{13,5},{14,6},{15,7},{16,24},{17,... | collective-permute-start | bytes 1032200 | tf_op jit(solution)/shard_map/far/ppermute | solution.py:498
  86.6 1.3 %collective-permute-start.24 = (bf16[1,336,512]{2,1,0:T(8,128)(2,1)S(1)}, bf16[1,336,512]{2,1,0:T(8,128)(2,1)S(1)}, u32[]{:S(2)}, u32[]{:S(2)}) collective-permute-start(bf16[1,336,512]{2,1,0:T(8,128)(2,1)S(1)} %add.15), channel_id=1, source_target_pairs={{8,4},{9,5},{10,6},{11,7},{12,0},{13,1},{14,2},{15,3},{16,28},{17,... | collective-permute-start | bytes 1032200 | tf_op jit(solution)/shard_map/cross/ppermute | solution.py:498
  87.9 3.6 %collective-permute-start.23 = (bf16[1,336,512]{2,1,0:T(8,128)(2,1)S(1)}, bf16[1,336,512]{2,1,0:T(8,128)(2,1)S(1)}, u32[]{:S(2)}, u32[]{:S(2)}) collective-permute-start(bf16[1,336,512]{2,1,0:T(8,128)(2,1)S(1)} %add.15), channel_id=1, source_target_pairs={{0,4},{1,5},{2,6},{3,7},{4,0},{5,1},{6,2},{7,3},{24,28},{25,29},{2... | collective-permute-start | bytes 1032200 | tf_op jit(solution)/shard_map/near/ppermute | solution.py:498
  91.5 0.9 collective-permute-start.26
  92.5 3.1 %input_0.1.refs_3_.refs_5_.refs_0_ = f32[1024,512]{1,0:T(8,128)S(1)} custom-call(bf16[32,2048]{1,0:T(8,128)(2,1)S(1)} %get-tuple-element.150.dgate_ref.refs_0_, bf16[2,16,512]{2,1,0:T(8,128)(2,1)S(1)} %bitcast.11, bf16[1,256,2048]{2,1,0:T(8,128)(2,1)S(1)} %get-tuple-element.170.refs_0_.refs_2_, bf16[1,256,2048]{2,1,0:T(8,128)(2,1)S(1)} %get-tuple-element.171.refs_1_.refs_3_, ...), custom_call_target="tpu_custom_call" | custom-call | flops 1050000000 | tf_op jit(solution)/shard_map/input_0/pallas_call | solution.py:56
  95.5 1.2 %collective-permute-done.26.refs_1_ = f32[48,512]{1,0:T(8,128)S(1)} collective-permute-done((f32[48,512]{1,0:T(8,128)S(1)}, f32[48,512]{1,0:T(8,128)S(1)}, u32[]{:S(2)}, u32[]{:S(2)}) %collective-permute-start.26) | collective-permute-done | bytes 98336 | tf_op jit(solution)/shard_map/shared_1/ppermute | solution.py:498
  97.3 4.8 %collective-permute-done.27.refs_1_ = f32[48,512]{1,0:T(8,128)S(1)} collective-permute-done((f32[48,512]{1,0:T(8,128)S(1)}, f32[48,512]{1,0:T(8,128)S(1)}, u32[]{:S(2)}, u32[]{:S(2)}) %collective-permute-start.27) | collective-permute-done | bytes 98336 | tf_op jit(solution)/shard_map/shared_0/ppermute | solution.py:498
  102.3 1.3 %collective-permute-done.28.give_ref = f32[48,512]{1,0:T(8,128)S(1)} collective-permute-done((f32[48,512]{1,0:T(8,128)S(1)}, f32[48,512]{1,0:T(8,128)S(1)}, u32[]{:S(2)}, u32[]{:S(2)}) %collective-permute-start.28) | collective-permute-done | bytes 98336 | tf_op jit(solution)/shard_map/keep/ppermute | solution.py:502
  103.5 1.3 %close.1 = (f32[2,16,512]{2,1,0:T(8,128)}, f32[2,16]{1,0:T(2,128)}, f32[2,64,128]{2,1,0:T(8,128)}, f32[2,64]{1,0:T(2,128)}, f32[2,64]{1,0:T(2,128)}, /*index=5*/f32[1,2]{1,0:T(1,128)}, f32[8,128]{1,0:T(8,128)S(1)}) custom-call(s32[35]{0:T(128)S(1)} %concatenate.3.int_ref.refs_0_.spot_ref, f32[48,512]{1,0:T(8,128)S(1)} %add.17.keep_ref, ...), custom_call_target="tpu_custom_call" | custom-call | flops 300000000 | tf_op jit(solution)/shard_map/close/pallas_call | solution.py:56
  105.3 1.5 %input_sum.1 = (f32[1024,512]{1,0:T(8,128)}, f32[8,128]{1,0:T(8,128)S(1)}) custom-call(f32[1024,512]{1,0:T(8,128)S(1)} %input_0.1.refs_3_.refs_5_.refs_0_, bf16[1024,512]{1,0:T(8,128)(2,1)S(1)} %collective-permute-done.20.refs_1_, f32[1,336,512]{2,1,0:T(8,128)S(1)} %add.18.refs_2_.refs_1_), custom_call_target="tpu_custom_call" | custom-call | flops 450000000 | tf_op jit(solution)/shard_map/input_sum/pallas_call | solution.py:56
  107.3 1.6 %finish.1 = (f32[1,512,256]{2,1,0:T(8,128)}, f32[1,256]{1,0:T(1,128)}, f32[1,256,128]{2,1,0:T(8,128)}, f32[1,128]{1,0:T(1,128)}) custom-call(s32[35]{0:T(128)S(1)} %concatenate.3.int_ref.refs_0_.spot_ref, f32[1,336,512]{2,1,0:T(8,128)S(1)} %add.18.refs_2_.refs_1_, f32[1,336,512]{2,1,0:T(8,128)S(1)} %collective-permute-done.29.refs_2_, ...), custom_call_target="tpu_custom_call" | custom-call | flops 3000000000 | tf_op jit(solution)/shard_map/finish/pallas_call | solution.py:56
  (64 shorter events, 6.1 us)
Async XLA Ops:
  0.6 9.6 %collective-permute-start.1 = (bf16[1024,512]{1,0:T(8,128)(2,1)}, bf16[1024,512]{1,0:T(8,128)(2,1)S(1)}, u32[]{:S(2)}, u32[]{:S(2)}) collective-permute-start(bf16[1024,512]{1,0:T(8,128)(2,1)} %mine_ref.1), channel_id=1, source_target_pairs={{0,16},{16,0},{1,17},{17,1},{2,18},{18,2},{3,19},{19,3},{4,20},{20... | collective-permute-start | bytes 3145736 | tf_op jit(solution)/shard_map/inputs/ppermute | solution.py:502
  2.4 13.5 %collective-permute-start.2 = (bf16[1,336,512]{2,1,0:T(8,128)(2,1)S(1)}, bf16[1,336,512]{2,1,0:T(8,128)(2,1)S(1)}, u32[]{:S(2)}, u32[]{:S(2)}) collective-permute-start(bf16[1,336,512]{2,1,0:T(8,128)(2,1)S(1)} %pack.1), channel_id=1, source_target_pairs={{0,8},{1,9},{2,10},{3,11},{4,12},{5,13},{6,14},{7,15},{8,24},{9,25... | collective-permute-start | bytes 1032200 | tf_op jit(solution)/shard_map/deal/ppermute | solution.py:511
  6.0 4.3 %collective-permute-start = (s32[2,1024]{1,0:T(2,128)}, s32[2,1024]{1,0:T(2,128)S(1)}, u32[]{:S(2)}, u32[]{:S(2)}) collective-permute-start(s32[2,1024]{1,0:T(2,128)} %label_ref.1), channel_id=1, source_target_pairs={{0,16},{16,0},{1,17},{17,1},{2,18},{18,2},{3,19},{19,3},{4,20},{20... | collective-permute-start | bytes 24584 | tf_op jit(solution)/shard_map/labels/ppermute | solution.py:502
  6.0 16.5 %collective-permute-start.5 = (bf16[1,336,512]{2,1,0:T(8,128)(2,1)S(1)}, bf16[1,336,512]{2,1,0:T(8,128)(2,1)S(1)}, u32[]{:S(2)}, u32[]{:S(2)}) collective-permute-start(bf16[1,336,512]{2,1,0:T(8,128)(2,1)S(1)} %pack.1), channel_id=1, source_target_pairs={{0,4},{1,5},{2,6},{3,7},{4,0},{5,1},{6,2},{7,3},{24,28},{25,29},{2... | collective-permute-start | bytes 1032200 | tf_op jit(solution)/shard_map/owners_near/ppermute | solution.py:498
  10.3 1.2 %copy-start = (bf16[1024,512]{1,0:T(8,128)(2,1)S(1)}, bf16[1024,512]{1,0:T(8,128)(2,1)}, u32[]{:S(2)}) copy-start(bf16[1024,512]{1,0:T(8,128)(2,1)} %mine_ref.1) | copy-start | bytes 3145732
  11.5 0.8 copy-start.1
  12.3 0.7 copy-start.4
  13.0 0.7 copy-start.8
  15.9 10.0 %collective-permute-start.4 = (bf16[1,336,512]{2,1,0:T(8,128)(2,1)S(1)}, bf16[1,336,512]{2,1,0:T(8,128)(2,1)S(1)}, u32[]{:S(2)}, u32[]{:S(2)}) collective-permute-start(bf16[1,336,512]{2,1,0:T(8,128)(2,1)S(1)} %hold.3.refs_0_.refs_1_.refs_8_.refs_10_), channel_id=1, source_target_pairs={{0,1},{1,0},{2,3},{3,2},{4,5},{5,4},{6,7},{7,6},{8,9},{9,8},{10,11... | collective-permute-start | bytes 1032200 | tf_op jit(solution)/shard_map/pay_4/ppermute | solution.py:498
  17.5 8.5 %collective-permute-start.3 = (bf16[1,336,512]{2,1,0:T(8,128)(2,1)S(1)}, bf16[1,336,512]{2,1,0:T(8,128)(2,1)S(1)}, u32[]{:S(2)}, u32[]{:S(2)}) collective-permute-start(bf16[1,336,512]{2,1,0:T(8,128)(2,1)S(1)} %hold.3.refs_0_.refs_1_.refs_8_.refs_10_), channel_id=1, source_target_pairs={{0,2},{1,3},{2,0},{3,1},{4,6},{5,7},{6,4},{7,5},{8,10},{9,11},{10,... | collective-permute-start | bytes 1032200 | tf_op jit(solution)/shard_map/pay_2/ppermute | solution.py:498
  19.0 6.9 %collective-permute-start.7 = (bf16[1,336,512]{2,1,0:T(8,128)(2,1)S(1)}, bf16[1,336,512]{2,1,0:T(8,128)(2,1)S(1)}, u32[]{:S(2)}, u32[]{:S(2)}) collective-permute-start(bf16[1,336,512]{2,1,0:T(8,128)(2,1)S(1)} %hold.3.refs_0_.refs_1_.refs_8_.refs_10_), channel_id=1, source_target_pairs={{8,12},{9,13},{10,14},{11,15},{12,8},{13,9},{14,10},{15,11},{16,20... | collective-permute-start | bytes 1032200 | tf_op jit(solution)/shard_map/pay_1/ppermute | solution.py:498
  26.0 11.0 %collective-permute-start.8 = (bf16[1,336,512]{2,1,0:T(8,128)(2,1)S(1)}, bf16[1,336,512]{2,1,0:T(8,128)(2,1)S(1)}, u32[]{:S(2)}, u32[]{:S(2)}) collective-permute-start(bf16[1,336,512]{2,1,0:T(8,128)(2,1)S(1)} %add.10.refs_0_.refs_2_.refs_9_.refs_11_), channel_id=1, source_target_pairs={{0,2},{1,3},{2,0},{3,1},{4,6},{5,7},{6,4},{7,5},{8,10},{9,11},{10,... | collective-permute-start | bytes 1032200 | tf_op jit(solution)/shard_map/pay_3/ppermute | solution.py:498
  26.6 12.1 %collective-permute-start.10 = (bf16[1,336,512]{2,1,0:T(8,128)(2,1)S(1)}, bf16[1,336,512]{2,1,0:T(8,128)(2,1)S(1)}, u32[]{:S(2)}, u32[]{:S(2)}) collective-permute-start(bf16[1,336,512]{2,1,0:T(8,128)(2,1)S(1)} %add.10.refs_0_.refs_2_.refs_9_.refs_11_), channel_id=1, source_target_pairs={{0,1},{1,0},{2,3},{3,2},{4,5},{5,4},{6,7},{7,6},{8,9},{9,8},{10,11... | collective-permute-start | bytes 1032200 | tf_op jit(solution)/shard_map/pay_5/ppermute | solution.py:498
  28.1 15.6 %collective-permute-start.6 = (bf16[1,336,512]{2,1,0:T(8,128)(2,1)S(1)}, bf16[1,336,512]{2,1,0:T(8,128)(2,1)S(1)}, u32[]{:S(2)}, u32[]{:S(2)}) collective-permute-start(bf16[1,336,512]{2,1,0:T(8,128)(2,1)S(1)} %hold.4.refs_2_.refs_0_.refs_1_.refs_10_.refs_12_), channel_id=1, source_target_pairs={{0,1},{1,0},{2,3},{3,2},{4,5},{5,4},{6,7},{7,6},{8,9},{9,8},{10,11... | collective-permute-start | bytes 1032200 | tf_op jit(solution)/shard_map/pay_6/ppermute | solution.py:498
  37.0 7.3 %collective-permute-start.9 = (bf16[1,336,512]{2,1,0:T(8,128)(2,1)S(1)}, bf16[1,336,512]{2,1,0:T(8,128)(2,1)S(1)}, u32[]{:S(2)}, u32[]{:S(2)}) collective-permute-start(bf16[1,336,512]{2,1,0:T(8,128)(2,1)S(1)} %hold.5), channel_id=1, source_target_pairs={{0,1},{1,0},{2,3},{3,2},{4,5},{5,4},{6,7},{7,6},{8,9},{9,8},{10,11... | collective-permute-start | bytes 1032200 | tf_op jit(solution)/shard_map/pay_7/ppermute | solution.py:498
  46.7 3.1 %collective-permute-start.11 = (bf16[2,128,1024]{2,1,0:T(8,128)(2,1)S(1)}, bf16[2,128,1024]{2,1,0:T(8,128)(2,1)S(1)}, u32[]{:S(2)}, u32[]{:S(2)}) collective-permute-start(bf16[2,128,1024]{2,1,0:T(8,128)(2,1)S(1)} %get-tuple-element.118.refs_0_), channel_id=1, source_target_pairs={{0,16},{16,0},{1,17},{17,1},{2,18},{18,2},{3,19},{19,3},{4,20},{20... | collective-permute-start | bytes 1572872 | tf_op jit(solution)/shard_map/mixed_other/ppermute | solution.py:502
  46.8 3.0 %copy-start.3 = (bf16[2,128,64]{1,2,0:T(8,128)(2,1)S(1)}, bf16[2,128,64]{1,2,0:T(8,128)(2,1)}, u32[]{:S(2)}) copy-start(bf16[2,128,64]{1,2,0:T(8,128)(2,1)} %param.21) | copy-start | bytes 98308
  46.8 3.0 %copy-start.5 = (bf16[2]{0:T(256)(128)(2,1)S(1)}, bf16[2]{0:T(256)(128)(2,1)}, u32[]{:S(2)}) copy-start(bf16[2]{0:T(256)(128)(2,1)} %param.24) | copy-start | bytes 16
  46.8 3.0 %copy-start.6 = (bf16[2,64]{1,0:T(2,128)(2,1)S(1)}, bf16[2,64]{1,0:T(2,128)(2,1)}, u32[]{:S(2)}) copy-start(bf16[2,64]{1,0:T(2,128)(2,1)} %refs_6_.1) | copy-start | bytes 772
  46.9 3.0 %copy-start.7 = (bf16[2,64]{1,0:T(2,128)(2,1)S(1)}, bf16[2,64]{1,0:T(2,128)(2,1)}, u32[]{:S(2)}) copy-start(bf16[2,64]{1,0:T(2,128)(2,1)} %refs_7_.1) | copy-start | bytes 772
  49.3 2.6 %collective-permute-start.12 = (bf16[2,128,1024]{2,1,0:T(8,128)(2,1)S(1)}, bf16[2,128,1024]{2,1,0:T(8,128)(2,1)S(1)}, u32[]{:S(2)}, u32[]{:S(2)}) collective-permute-start(bf16[2,128,1024]{2,1,0:T(8,128)(2,1)S(1)} %get-tuple-element.117.mix_ref), channel_id=1, source_target_pairs={{0,16},{16,0},{1,17},{17,1},{2,18},{18,2},{3,19},{19,3},{4,20},{20... | collective-permute-start | bytes 1572872 | tf_op jit(solution)/shard_map/mixed_own/ppermute | solution.py:502
  56.3 15.7 %collective-permute-start.15 = (bf16[1,336,512]{2,1,0:T(8,128)(2,1)S(1)}, bf16[1,336,512]{2,1,0:T(8,128)(2,1)S(1)}, u32[]{:S(2)}, u32[]{:S(2)}) collective-permute-start(bf16[1,336,512]{2,1,0:T(8,128)(2,1)S(1)} %get-tuple-element.165), channel_id=1, source_target_pairs={{0,1},{1,0},{2,3},{3,2},{4,5},{5,4},{6,7},{7,6},{8,9},{9,8},{10,11... | collective-permute-start | bytes 1032200 | tf_op jit(solution)/shard_map/grad_six/ppermute | solution.py:498
  58.0 14.0 %collective-permute-start.16 = (bf16[1,336,512]{2,1,0:T(8,128)(2,1)S(1)}, bf16[1,336,512]{2,1,0:T(8,128)(2,1)S(1)}, u32[]{:S(2)}, u32[]{:S(2)}) collective-permute-start(bf16[1,336,512]{2,1,0:T(8,128)(2,1)S(1)} %get-tuple-element.166), channel_id=1, source_target_pairs={{0,1},{1,0},{2,3},{3,2},{4,5},{5,4},{6,7},{7,6},{8,9},{9,8},{10,11... | collective-permute-start | bytes 1032200 | tf_op jit(solution)/shard_map/grad_seven/ppermute | solution.py:498
  61.2 17.8 %collective-permute-start.13 = (bf16[1,336,512]{2,1,0:T(8,128)(2,1)S(1)}, bf16[1,336,512]{2,1,0:T(8,128)(2,1)S(1)}, u32[]{:S(2)}, u32[]{:S(2)}) collective-permute-start(bf16[1,336,512]{2,1,0:T(8,128)(2,1)S(1)} %get-tuple-element.157), channel_id=1, source_target_pairs={{0,1},{1,0},{2,3},{3,2},{4,5},{5,4},{6,7},{7,6},{8,9},{9,8},{10,11... | collective-permute-start | bytes 1032200 | tf_op jit(solution)/shard_map/grad_four/ppermute | solution.py:498
  62.8 16.2 %collective-permute-start.14 = (bf16[1,336,512]{2,1,0:T(8,128)(2,1)S(1)}, bf16[1,336,512]{2,1,0:T(8,128)(2,1)S(1)}, u32[]{:S(2)}, u32[]{:S(2)}) collective-permute-start(bf16[1,336,512]{2,1,0:T(8,128)(2,1)S(1)} %get-tuple-element.158), channel_id=1, source_target_pairs={{0,1},{1,0},{2,3},{3,2},{4,5},{5,4},{6,7},{7,6},{8,9},{9,8},{10,11... | collective-permute-start | bytes 1032200 | tf_op jit(solution)/shard_map/grad_five/ppermute | solution.py:498
  66.8 1.4 %collective-permute-start.17 = (f32[48,512]{1,0:T(8,128)S(1)}, f32[48,512]{1,0:T(8,128)S(1)}, u32[]{:S(2)}, u32[]{:S(2)}) collective-permute-start(f32[48,512]{1,0:T(8,128)S(1)} %get-tuple-element.168), channel_id=1, source_target_pairs={{0,16},{16,0},{1,17},{17,1},{2,18},{18,2},{3,19},{19,3},{4,20},{20... | collective-permute-start | bytes 294920 | tf_op jit(solution)/shard_map/give/ppermute | solution.py:502
  68.2 9.0 %collective-permute-start.18 = (f32[48,512]{1,0:T(8,128)S(1)}, f32[48,512]{1,0:T(8,128)S(1)}, u32[]{:S(2)}, u32[]{:S(2)}) collective-permute-start(f32[48,512]{1,0:T(8,128)S(1)} %add.11.refs_13_.refs_0_), channel_id=1, source_target_pairs={{0,8},{1,9},{2,10},{3,11},{4,12},{5,13},{6,14},{7,15},{8,0},{9,1},... | collective-permute-start | bytes 294920 | tf_op jit(solution)/shard_map/shared_3/ppermute | solution.py:498
  74.8 10.3 %collective-permute-start.21 = (bf16[1,336,512]{2,1,0:T(8,128)(2,1)S(1)}, bf16[1,336,512]{2,1,0:T(8,128)(2,1)S(1)}, u32[]{:S(2)}, u32[]{:S(2)}) collective-permute-start(bf16[1,336,512]{2,1,0:T(8,128)(2,1)S(1)} %get-tuple-element.176), channel_id=1, source_target_pairs={{0,2},{1,3},{2,0},{3,1},{4,6},{5,7},{6,4},{7,5},{8,10},{9,11},{10,... | collective-permute-start | bytes 1032200 | tf_op jit(solution)/shard_map/grad_two/ppermute | solution.py:498
  75.8 10.8 %collective-permute-start.22 = (bf16[1,336,512]{2,1,0:T(8,128)(2,1)S(1)}, bf16[1,336,512]{2,1,0:T(8,128)(2,1)S(1)}, u32[]{:S(2)}, u32[]{:S(2)}) collective-permute-start(bf16[1,336,512]{2,1,0:T(8,128)(2,1)S(1)} %get-tuple-element.179), channel_id=1, source_target_pairs={{0,2},{1,3},{2,0},{3,1},{4,6},{5,7},{6,4},{7,5},{8,10},{9,11},{10,... | collective-permute-start | bytes 1032200 | tf_op jit(solution)/shard_map/grad_three/ppermute | solution.py:498
  77.2 4.7 %collective-permute-start.19 = (f32[48,512]{1,0:T(8,128)S(1)}, f32[48,512]{1,0:T(8,128)S(1)}, u32[]{:S(2)}, u32[]{:S(2)}) collective-permute-start(f32[48,512]{1,0:T(8,128)S(1)} %add.12.refs_14_.refs_0_), channel_id=1, source_target_pairs={{0,4},{1,5},{2,6},{3,7},{4,0},{5,1},{6,2},{7,3},{8,12},{9,13},{10,... | collective-permute-start | bytes 294920 | tf_op jit(solution)/shard_map/shared_2/ppermute | solution.py:498
  79.0 2.9 %copy-start.2 = (bf16[2,512,16]{1,2,0:T(8,128)(2,1)S(1)}, bf16[2,512,16]{1,2,0:T(8,128)(2,1)}, u32[]{:S(2)}) copy-start(bf16[2,512,16]{1,2,0:T(8,128)(2,1)} %param.19) | copy-start | bytes 98308
  85.0 20.3 %collective-permute-start.20 = (bf16[1024,512]{1,0:T(8,128)(2,1)S(1)}, bf16[1024,512]{1,0:T(8,128)(2,1)S(1)}, u32[]{:S(2)}, u32[]{:S(2)}) collective-permute-start(bf16[1024,512]{1,0:T(8,128)(2,1)S(1)} %input_1.1.refs_2_), channel_id=1, source_target_pairs={{0,16},{16,0},{1,17},{17,1},{2,18},{18,2},{3,19},{19,3},{4,20},{20... | collective-permute-start | bytes 3145736 | tf_op jit(solution)/shard_map/over/ppermute | solution.py:502
  85.2 19.7 %collective-permute-start.25 = (bf16[1,336,512]{2,1,0:T(8,128)(2,1)S(1)}, bf16[1,336,512]{2,1,0:T(8,128)(2,1)S(1)}, u32[]{:S(2)}, u32[]{:S(2)}) collective-permute-start(bf16[1,336,512]{2,1,0:T(8,128)(2,1)S(1)} %get-tuple-element.180.refs_2_), channel_id=1, source_target_pairs={{8,0},{9,1},{10,2},{11,3},{12,4},{13,5},{14,6},{15,7},{16,24},{17,... | collective-permute-start | bytes 1032200 | tf_op jit(solution)/shard_map/far/ppermute | solution.py:498
  86.6 18.3 %collective-permute-start.24 = (bf16[1,336,512]{2,1,0:T(8,128)(2,1)S(1)}, bf16[1,336,512]{2,1,0:T(8,128)(2,1)S(1)}, u32[]{:S(2)}, u32[]{:S(2)}) collective-permute-start(bf16[1,336,512]{2,1,0:T(8,128)(2,1)S(1)} %add.15), channel_id=1, source_target_pairs={{8,4},{9,5},{10,6},{11,7},{12,0},{13,1},{14,2},{15,3},{16,28},{17,... | collective-permute-start | bytes 1032200 | tf_op jit(solution)/shard_map/cross/ppermute | solution.py:498
  87.9 17.0 %collective-permute-start.23 = (bf16[1,336,512]{2,1,0:T(8,128)(2,1)S(1)}, bf16[1,336,512]{2,1,0:T(8,128)(2,1)S(1)}, u32[]{:S(2)}, u32[]{:S(2)}) collective-permute-start(bf16[1,336,512]{2,1,0:T(8,128)(2,1)S(1)} %add.15), channel_id=1, source_target_pairs={{0,4},{1,5},{2,6},{3,7},{4,0},{5,1},{6,2},{7,3},{24,28},{25,29},{2... | collective-permute-start | bytes 1032200 | tf_op jit(solution)/shard_map/near/ppermute | solution.py:498
  91.5 5.2 %collective-permute-start.26 = (f32[48,512]{1,0:T(8,128)S(1)}, f32[48,512]{1,0:T(8,128)S(1)}, u32[]{:S(2)}, u32[]{:S(2)}) collective-permute-start(f32[48,512]{1,0:T(8,128)S(1)} %add.13.refs_18_.refs_0_), channel_id=1, source_target_pairs={{0,2},{1,3},{2,0},{3,1},{4,6},{5,7},{6,4},{7,5},{8,10},{9,11},{10,... | collective-permute-start | bytes 294920 | tf_op jit(solution)/shard_map/shared_1/ppermute | solution.py:498
  96.8 5.4 %collective-permute-start.27 = (f32[48,512]{1,0:T(8,128)S(1)}, f32[48,512]{1,0:T(8,128)S(1)}, u32[]{:S(2)}, u32[]{:S(2)}) collective-permute-start(f32[48,512]{1,0:T(8,128)S(1)} %add.16.refs_0_), channel_id=1, source_target_pairs={{0,1},{1,0},{2,3},{3,2},{4,5},{5,4},{6,7},{7,6},{8,9},{9,8},{10,11... | collective-permute-start | bytes 294920 | tf_op jit(solution)/shard_map/shared_0/ppermute | solution.py:498
  102.2 1.4 %collective-permute-start.28 = (f32[48,512]{1,0:T(8,128)S(1)}, f32[48,512]{1,0:T(8,128)S(1)}, u32[]{:S(2)}, u32[]{:S(2)}) collective-permute-start(f32[48,512]{1,0:T(8,128)S(1)} %add.17.keep_ref), channel_id=1, source_target_pairs={{0,16},{16,0},{1,17},{17,1},{2,18},{18,2},{3,19},{19,3},{4,20},{20... | collective-permute-start | bytes 294920 | tf_op jit(solution)/shard_map/keep/ppermute | solution.py:502
  105.1 2.2 %collective-permute-start.29 = (f32[1,336,512]{2,1,0:T(8,128)S(1)}, f32[1,336,512]{2,1,0:T(8,128)S(1)}, u32[]{:S(2)}, u32[]{:S(2)}) collective-permute-start(f32[1,336,512]{2,1,0:T(8,128)S(1)} %add.18.refs_2_.refs_1_), channel_id=1, source_target_pairs={{0,16},{16,0},{1,17},{17,1},{2,18},{18,2},{3,19},{19,3},{4,20},{20... | collective-permute-start | bytes 2064392 | tf_op jit(solution)/shard_map/final/ppermute | solution.py:502

commit v4 on v3

--- a/solution.py
+++ b/solution.py
@@ -337,19 +337,21 @@
     give_ref[...] = shared_ref[pl.ds(pl.multiple_of((1 - spot_ref[0]) * deep, 8), deep), :]
 
 
-def backward_kernel(bundles, add, block, x_ref, pay_a, pay_b, low_ref, dmix_ref, *refs):
-    kept, refs = (refs[:3], refs[3:6]), refs[6:]
+def backward_kernel(bundles, add, block, x_ref, low_ref, dmix_ref, *refs):
+    count = len(bundles)
+    pays, refs = refs[:count], refs[count:]
+    kept, refs = [refs[3 * n : 3 * n + 3] for n in range(count)], refs[3 * count :]
     if add:
-        come, refs = refs[:2], refs[2:]
-    grads, dones, d_two, sums = refs[:2], refs[2:4], refs[4], refs[5]
-    depth = pay_a.shape[0]
+        come, refs = refs[:count], refs[count:]
+    grads, dones, d_two, sums = refs[:count], refs[count : 2 * count], refs[-2], refs[-1]
+    depth = pays[0].shape[0]
     for k in range(depth):
-        weights = [second_weight(pay[k]) for pay in (pay_a, pay_b)]
+        weights = [second_weight(pay[k]) for pay in pays]
         sums[...] = jnp.zeros_like(sums)
 
         def step(i, _, k=k, weights=weights):
             at = pl.ds(pl.multiple_of(i * block, block), block)
-            for n in range(2):
+            for n in range(count):
                 _, g1_ref, g2_ref = kept[n]
                 j = bundles[n] * depth + k
                 d_out = low_ref[j, 0:1, at] * dmix_ref[0, :, at] + low_ref[j, 1:2, at] * dmix_ref[1, :, at]
@@ -367,7 +369,7 @@
             return 0
 
         lax.fori_loop(0, x_ref.shape[0] // block, step, 0)
-        for n in range(2):
+        for n in range(count):
             h_ref = kept[n][0]
             first = dot(dones[n][k], x_ref[...], NN)
             second = dot(d_two[n], h_ref[k], NT)
@@ -610,16 +612,17 @@
         kernel = functools.partial(tower_kernel, 1, 512)
         dmix, centre = call("tower_other", kernel, ins, tower_outs, pin, 2, alias=begun)
 
-    def back(a, b, come, dtype, cost, after=()):
+    def back(bundles, come, dtype, cost, after=()):
         grad = ((depth, PAY_ROWS, 512), dtype, False)
         done = ((depth, 256, 2 * rows), BF16, True)
         return call(
-            f"backward_{a}{b}",
-            functools.partial(backward_kernel, (a, b), come is not None, BACK_CHUNK),
-            [x, pays[a], pays[b], low, dmix]
-            + [saved[n][m] for n in (a, b) for m in (0, 1, 3)]
+            "backward_" + "".join(str(n) for n in bundles),
+            functools.partial(backward_kernel, bundles, come is not None, BACK_CHUNK),
+            [x, low, dmix]
+            + [pays[n] for n in bundles]
+            + [saved[n][m] for n in bundles for m in (0, 1, 3)]
             + list(come or ()),
-            [grad, grad, done, done],
+            [grad] * len(bundles) + [done] * len(bundles),
             pin,
             cost,
             [pltpu.VMEM((2, 128, 2 * rows), BF16), pltpu.VMEM((2, 384, 128), F32)],
@@ -627,9 +630,10 @@
         )
 
     ones = [None] * 8
-    grad_six, grad_seven, ones[6], ones[7] = back(6, 7, None, BF16, 5)
+    grad_seven, ones[7] = back((7,), None, BF16, 2)
+    grad_six, ones[6] = back((6,), None, BF16, 2, [ones[7]])
     six, seven = send("grad_six", grad_six, end_bit), send("grad_seven", grad_seven, end_bit)
-    grad_four, grad_five, ones[4], ones[5] = back(4, 5, None, BF16, 1, [ones[7]])
+    grad_four, grad_five, ones[4], ones[5] = back((4, 5), None, BF16, 1, [ones[6]])
     five, four = send("grad_five", grad_five, end_bit), send("grad_four", grad_four, end_bit)
     deep = shared_rows(experts) // 2
     dgate, keep, give = call(
@@ -644,14 +648,14 @@
         after=[ones[5]],
     )
     (keep,) = add([keep, swap("give", give)], [F32])
-    grad_two, grad_three, ones[2], ones[3] = back(2, 3, (six, seven), BF16, 1, [keep])
+    grad_two, grad_three, ones[2], ones[3] = back((2, 3), (six, seven), BF16, 1, [keep])
     three, two = send("grad_three", grad_three, mid_bit), send("grad_two", grad_two, mid_bit)
     stages = []
     for b in (bits - 1, *range(2, bits - 1)):
         (keep,) = add([keep, send(f"shared_{b}", keep, (b, b))], [F32], [ones[3]])
         stages.append(keep)
 
-    grad_zero, grad_one, ones[0], ones[1] = back(0, 1, (four, five), F32, 1, [ones[3], stages[0]])
+    grad_zero, grad_one, ones[0], ones[1] = back((0, 1), (four, five), F32, 1, [ones[3], stages[0]])
     def input_gradient(side, dtype, after=()):
         (out,) = call(
             f"input_{side}",

time: 109 us -> 109 us (level)
    pallas_call x27 -> x28, Pallas kernels: 50 us -> 49.9 us  [call(): pl.pallas_call(body, name=name, in_specs=[SMEM] * scalars + [VMEM] * (cou...]
  transfers between devices with their start and end apart: 30 -> 30, of which waited for: 9 -> 10; matrix products, arithmetic and copies ran while one was open for 1% -> 1% of each run, Pallas kernels for 41% -> 41%
where the time goes in v4:
time: 109 us
  Pallas kernels  53.4 us (49%)
  starting transfers between devices  36.2 us (33%)
  waiting for transfers between devices  14 us (13%)
  local copies, waits for them, and re-layouts  4.13 us (4%)
    pallas_call x28, Pallas kernels, call(): pl.pallas_call(body, name=name, in_specs=[SMEM] * scalars + [VMEM] * (cou...  49.9 us
    ppermute x21, starting transfers between devices, send(): return lax.ppermute(value, ('dp', 'expert'), pairs(bit_of_core, want, also))  31 us
    ppermute x21, waiting for transfers between devices, send(): return lax.ppermute(value, ('dp', 'expert'), pairs(bit_of_core, want, also))  10.9 us
    ppermute x1, starting transfers between devices, deal(): return lax.ppermute(value, ('dp', 'expert'), route)  3.66 us
    unnamed x19, local copies, waits for them, and re-layouts  3.38 us
    ppermute x8, waiting for transfers between devices, swap(): return lax.ppermute(value, 'dp', [(0, 1), (1, 0)])  3.09 us
    pallas_call x1, Pallas kernels, per_device(): pl.pallas_call(functools.partial(gate_kernel, masks, group_len.shape[0]),...  2.26 us
  transfers between devices with their start and end apart: 30, of which 10 were waited for; matrix products, arithmetic and copies ran while one was open for 1% of the time, Pallas kernels for 41%

profile of v4, /device:TPU:0, one launch (start us, length us, event | category | flops | bytes accessed | tf_op | source)
XLA Modules:
  0.0 108.8 jit_solution(15722440886029456995)
XLA Ops:
  1.2 1.2 %pack.1 = bf16[1,336,512]{2,1,0:T(8,128)(2,1)S(1)} custom-call(bf16[1,512,256]{2,1,0:T(8,128)(2,1)} %w1_ref.1, bf16[1,256,128]{2,1,0:T(8,128)(2,1)} %w2_ref.1, bf16[1,256]{1,0:T(2,128)(2,1)} %b1_ref.1, bf16[1,128]{1,0:T(2,128)(2,1)} %b2_ref.1), custom_call_target="tpu_custom_call" | custom-call | tf_op jit(solution)/shard_map/pack/pallas_call | solution.py:135
  2.4 3.7 %collective-permute-start.2 = (bf16[1,336,512]{2,1,0:T(8,128)(2,1)S(1)}, bf16[1,336,512]{2,1,0:T(8,128)(2,1)S(1)}, u32[]{:S(2)}, u32[]{:S(2)}) collective-permute-start(bf16[1,336,512]{2,1,0:T(8,128)(2,1)S(1)} %pack.1), channel_id=1, source_target_pairs={{0,8},{1,9},{2,10},{3,11},{4,12},{5,13},{6,14},{7,15},{8,24},{9,25... | collective-permute-start | bytes 1032200 | tf_op jit(solution)/shard_map/deal/ppermute | solution.py:513
  6.0 3.5 %collective-permute-start.5 = (bf16[1,336,512]{2,1,0:T(8,128)(2,1)S(1)}, bf16[1,336,512]{2,1,0:T(8,128)(2,1)S(1)}, u32[]{:S(2)}, u32[]{:S(2)}) collective-permute-start(bf16[1,336,512]{2,1,0:T(8,128)(2,1)S(1)} %pack.1), channel_id=1, source_target_pairs={{0,4},{1,5},{2,6},{3,7},{4,0},{5,1},{6,2},{7,3},{24,28},{25,29},{2... | collective-permute-start | bytes 1032200 | tf_op jit(solution)/shard_map/owners_near/ppermute | solution.py:500
  9.5 0.7 concatenate.3.int_ref.refs_0_.spot_ref
  10.3 1.2 %copy-done = bf16[1024,512]{1,0:T(8,128)(2,1)S(1)} copy-done((bf16[1024,512]{1,0:T(8,128)(2,1)S(1)}, bf16[1024,512]{1,0:T(8,128)(2,1)}, u32[]{:S(2)}) %copy-start) | copy-done | bytes 1048600
  11.5 0.8 copy-done.1
  12.3 0.7 copy-done.4
  13.0 0.7 copy-done.8
  13.6 2.3 %gate.1 = (f32[8,2,2048]{2,1,0:T(2,128)S(1)}, f32[8,2,2048]{2,1,0:T(2,128)S(1)}, f32[1,2048]{1,0:T(1,128)S(1)}, bf16[2048,512]{1,0:T(8,128)(2,1)S(1)}, f32[2,2048]{1,0:T(2,128)S(1)}) custom-call(s32[35]{0:T(128)S(1)} %concatenate.3.int_ref.refs_0_.spot_ref, s32[2,1024]{1,0:T(2,128)S(1)} %copy-done.4, s32[2,1024]{1,0:T(2,128)S(1)} %collective-permute-done.there_ref, ...), custom_call_target="tpu_custom_call" | custom-call | tf_op jit(solution)/shard_map/gate/pallas_call | solution.py:542
  15.9 1.6 %collective-permute-start.4 = (bf16[1,336,512]{2,1,0:T(8,128)(2,1)S(1)}, bf16[1,336,512]{2,1,0:T(8,128)(2,1)S(1)}, u32[]{:S(2)}, u32[]{:S(2)}) collective-permute-start(bf16[1,336,512]{2,1,0:T(8,128)(2,1)S(1)} %hold.3.refs_0_.refs_3_.refs_8_.refs_10_), channel_id=1, source_target_pairs={{0,1},{1,0},{2,3},{3,2},{4,5},{5,4},{6,7},{7,6},{8,9},{9,8},{10,11... | collective-permute-start | bytes 1032200 | tf_op jit(solution)/shard_map/pay_4/ppermute | solution.py:500
  17.5 1.5 %collective-permute-start.3 = (bf16[1,336,512]{2,1,0:T(8,128)(2,1)S(1)}, bf16[1,336,512]{2,1,0:T(8,128)(2,1)S(1)}, u32[]{:S(2)}, u32[]{:S(2)}) collective-permute-start(bf16[1,336,512]{2,1,0:T(8,128)(2,1)S(1)} %hold.3.refs_0_.refs_3_.refs_8_.refs_10_), channel_id=1, source_target_pairs={{0,2},{1,3},{2,0},{3,1},{4,6},{5,7},{6,4},{7,5},{8,10},{9,11},{10,... | collective-permute-start | bytes 1032200 | tf_op jit(solution)/shard_map/pay_2/ppermute | solution.py:500
  19.0 0.7 collective-permute-start.7
  19.7 2.9 %forward_0.1 = (bf16[1,256,2048]{2,1,0:T(8,128)(2,1)S(1)}, bf16[1,256,2048]{2,1,0:T(8,128)(2,1)S(1)}, bf16[1,128,2048]{2,1,0:T(8,128)(2,1)S(1)}, f32[1,128,2048]{2,1,0:T(8,128)S(1)}, f32[2,128,2048]{2,1,0:T(8,128)S(1)}) custom-call(bf16[2048,512]{1,0:T(8,128)(2,1)S(1)} %get-tuple-element.103.x_ref.refs_0_.refs_1_, ...), custom_call_target="tpu_custom_call" | custom-call | flops 675000000 | tf_op jit(solution)/shard_map/forward_0/pallas_call | solution.py:56
  22.6 3.3 %collective-permute-done.4.refs_1_.refs_3_.refs_12_.refs_14_ = bf16[1,336,512]{2,1,0:T(8,128)(2,1)S(1)} collective-permute-done((bf16[1,336,512]{2,1,0:T(8,128)(2,1)S(1)}, bf16[1,336,512]{2,1,0:T(8,128)(2,1)S(1)}, u32[]{:S(2)}, u32[]{:S(2)}) %collective-permute-start.4) | collective-permute-done | bytes 344096 | tf_op jit(solution)/shard_map/pay_4/ppermute | solution.py:500
  26.6 1.5 %collective-permute-start.10 = (bf16[1,336,512]{2,1,0:T(8,128)(2,1)S(1)}, bf16[1,336,512]{2,1,0:T(8,128)(2,1)S(1)}, u32[]{:S(2)}, u32[]{:S(2)}) collective-permute-start(bf16[1,336,512]{2,1,0:T(8,128)(2,1)S(1)} %add.10.refs_0_.refs_4_.refs_9_.refs_11_), channel_id=1, source_target_pairs={{0,1},{1,0},{2,3},{3,2},{4,5},{5,4},{6,7},{7,6},{8,9},{9,8},{10,11... | collective-permute-start | bytes 1032200 | tf_op jit(solution)/shard_map/pay_5/ppermute | solution.py:500
  28.6 4.9 %forward_14.1 = (bf16[1,256,2048]{2,1,0:T(8,128)(2,1)S(1)}, bf16[1,256,2048]{2,1,0:T(8,128)(2,1)S(1)}, bf16[1,128,2048]{2,1,0:T(8,128)(2,1)S(1)}, f32[1,128,2048...) custom-call(bf16[2048,512]{1,0:T(8,128)(2,1)S(1)} %get-tuple-element, ...), custom_call_target="tpu_custom_call" | custom-call | flops 1350000000 | tf_op jit(solution)/shard_map/forward_14/pallas_call | solution.py:56
  33.5 2.9 %forward_2.1 = (bf16[1,256,2048]{2,1,0:T(8,128)(2,1)S(1)}, bf16[1,256,2048]{2,1,0:T(8,128)(2,1)S(1)}, bf16[1,128,2048]{2,1,0:T(8,128)(2,1)S(1)}, f32[1,128,2048]{2,1,0:T(8,128)S(1)}, f32[2,128,2048]{2,1,0:T(8,128)S(1)}) custom-call(bf16[2048,512]{1,0:T(8,128)(2,1)S(1)} %get-tuple-element.103.x_ref.refs_0_.refs_1_, ...), custom_call_target="tpu_custom_call" | custom-call | flops 675000000 | tf_op jit(solution)/shard_map/forward_2/pallas_call | solution.py:56
  37.0 1.6 %collective-permute-start.9 = (bf16[1,336,512]{2,1,0:T(8,128)(2,1)S(1)}, bf16[1,336,512]{2,1,0:T(8,128)(2,1)S(1)}, u32[]{:S(2)}, u32[]{:S(2)}) collective-permute-start(bf16[1,336,512]{2,1,0:T(8,128)(2,1)S(1)} %hold.5), channel_id=1, source_target_pairs={{0,1},{1,0},{2,3},{3,2},{4,5},{5,4},{6,7},{7,6},{8,9},{9,8},{10,11... | collective-permute-start | bytes 1032200 | tf_op jit(solution)/shard_map/pay_7/ppermute | solution.py:500
  38.7 5.1 %forward_35.1 = (bf16[1,256,2048]{2,1,0:T(8,128)(2,1)S(1)}, bf16[1,256,2048]{2,1,0:T(8,128)(2,1)S(1)}, bf16[1,128,2048]{2,1,0:T(8,128)(2,1)S(1)}, f32[1,128,2048...) custom-call(bf16[2048,512]{1,0:T(8,128)(2,1)S(1)} %get-tuple-element, ...), custom_call_target="tpu_custom_call" | custom-call | flops 1350000000 | tf_op jit(solution)/shard_map/forward_35/pallas_call | solution.py:56
  44.3 2.4 %forward_67_other.1 = (bf16[1,256,2048]{2,1,0:T(8,128)(2,1)S(1)}, bf16[1,256,2048]{2,1,0:T(8,128)(2,1)S(1)}, bf16[1,128,2048]{2,1,0:T(8,128)(2,1)S(1)}, f32[1,12...) custom-call(bf16[2048,512]{1,0:T(8,128)(2,1)S(1)} %get-tuple-element, ...), custom_call_target="tpu_custom_call" | custom-call | flops 675000000 | tf_op jit(solution)/shard_map/forward_67_other/pallas_call | solution.py:56
  46.9 2.4 %forward_67_own.1 = (bf16[1,256,2048]{2,1,0:T(8,128)(2,1)S(1)}, bf16[1,256,2048]{2,1,0:T(8,128)(2,1)S(1)}, bf16[1,128,2048]{2,1,0:T(8,128)(2,1)S(1)}, f32[1,128,...) custom-call(bf16[2048,512]{1,0:T(8,128)(2,1)S(1)} %get-tuple-element, ...), custom_call_target="tpu_custom_call", output_to_operand_aliasing={{0}: (5, {}), {1}: (6, {}), {2}: (7, {}), {3}: (8, {}), {4}... | custom-call | flops 675000000 | tf_op jit(solution)/shard_map/forward_67_own/pallas_call | solution.py:56
  49.8 2.1 %tower_own.1 = (f32[2,128,2048]{2,1,0:T(8,128)S(1)}, f32[2,2048]{1,0:T(2,128)S(1)}, f32[2,1024]{1,0:T(2,128)}, f32[48,512]{1,0:T(8,128)S(1)}) custom-call(bf16[2,128,1024]{2,1,0:T(8,128)(2,1)S(1)} %get-tuple-element.117.mix_ref, bf16[2,128,1024]{2,1,0:T(8,128)(2,1)S(1)} %collective-permute-done.11.come_ref, ...), custom_call_target="tpu_custom_call" | custom-call | flops 600000000 | tf_op jit(solution)/shard_map/tower_own/pallas_call | solution.py:56
  51.9 1.6 %tower_other.1 = (f32[2,128,2048]{2,1,0:T(8,128)S(1)}, f32[2,2048]{1,0:T(2,128)S(1)}) custom-call(bf16[2,128,1024]{2,1,0:T(8,128)(2,1)S(1)} %get-tuple-element.118.refs_0_, bf16[2,128,1024]{2,1,0:T(8,128)(2,1)S(1)} %collective-permute-done.12.refs_1_, ...), custom_call_target="tpu_custom_call", output_to_operand_aliasing={{0}: (8, {}), {1}: (9, {})} | custom-call | flops 600000000 | tf_op jit(solution)/shard_map/tower_other/pallas_call | solution.py:56
  53.5 1.4 %backward_7.1 = (bf16[1,336,512]{2,1,0:T(8,128)(2,1)S(1)}, bf16[1,256,2048]{2,1,0:T(8,128)(2,1)S(1)}) custom-call(bf16[2048,512]{1,0:T(8,128)(2,1)S(1)} %get-tuple-element.103.x_ref.refs_0_.refs_1_, f32[8,2,2048]{2,1,0:T(2,128)S(1)} %get-tuple-element.104.refs_1_.low_ref, f32[2,128,2048]{2,1,0:T(8,128)S(1)} %get-tuple-element.124.dmix_ref.refs_2_, ...), custom_call_target="tpu_custom_call" | custom-call | flops 600000000 | tf_op jit(solution)/shard_map/backward_7/pallas_call | solution.py:56
  54.9 1.4 %backward_6.1 = (bf16[1,336,512]{2,1,0:T(8,128)(2,1)S(1)}, bf16[1,256,2048]{2,1,0:T(8,128)(2,1)S(1)}) custom-call(bf16[2048,512]{1,0:T(8,128)(2,1)S(1)} %get-tuple-element.103.x_ref.refs_0_.refs_1_, f32[8,2,2048]{2,1,0:T(2,128)S(1)} %get-tuple-element.104.refs_1_.low_ref, f32[2,128,2048]{2,1,0:T(8,128)S(1)} %get-tuple-element.124.dmix_ref.refs_2_, ...), custom_call_target="tpu_custom_call" | custom-call | flops 600000000 | tf_op jit(solution)/shard_map/backward_6/pallas_call | solution.py:56
  56.2 1.6 %collective-permute-start.15 = (bf16[1,336,512]{2,1,0:T(8,128)(2,1)S(1)}, bf16[1,336,512]{2,1,0:T(8,128)(2,1)S(1)}, u32[]{:S(2)}, u32[]{:S(2)}) collective-permute-start(bf16[1,336,512]{2,1,0:T(8,128)(2,1)S(1)} %get-tuple-element.166), channel_id=1, source_target_pairs={{0,1},{1,0},{2,3},{3,2},{4,5},{5,4},{6,7},{7,6},{8,9},{9,8},{10,11... | collective-permute-start | bytes 1032200 | tf_op jit(solution)/shard_map/grad_six/ppermute | solution.py:500
  58.3 2.8 %backward_45.1 = (bf16[1,336,512]{2,1,0:T(8,128)(2,1)S(1)}, bf16[1,336,512]{2,1,0:T(8,128)(2,1)S(1)}, bf16[1,256,2048]{2,1,0:T(8,128)(2,1)S(1)}, bf16[1,256,2048]{2,1,0:T(8,128)(2,1)S(1)}) custom-call(bf16[2048,512]{1,0:T(8,128)(2,1)S(1)} %get-tuple-element.103.x_ref.refs_0_.refs_1_, f32[8,2,2048]{2,1,0:T(2,128)S(1)} %get-tuple-element.104.refs_1_.low_ref, ...), custom_call_target="tpu_custom_call" | custom-call | flops 300000000 | tf_op jit(solution)/shard_map/backward_45/pallas_call | solution.py:56
  61.1 1.6 %collective-permute-start.13 = (bf16[1,336,512]{2,1,0:T(8,128)(2,1)S(1)}, bf16[1,336,512]{2,1,0:T(8,128)(2,1)S(1)}, u32[]{:S(2)}, u32[]{:S(2)}) collective-permute-start(bf16[1,336,512]{2,1,0:T(8,128)(2,1)S(1)} %get-tuple-element.158), channel_id=1, source_target_pairs={{0,1},{1,0},{2,3},{3,2},{4,5},{5,4},{6,7},{7,6},{8,9},{9,8},{10,11... | collective-permute-start | bytes 1032200 | tf_op jit(solution)/shard_map/grad_four/ppermute | solution.py:500
  63.2 3.5 %gate_back.1 = (bf16[32,2048]{1,0:T(8,128)(2,1)S(1)}, f32[48,512]{1,0:T(8,128)S(1)}, f32[48,512]{1,0:T(8,128)S(1)}) custom-call(s32[35]{0:T(128)S(1)} %concatenate.3.int_ref.refs_0_.spot_ref, bf16[2048,512]{1,0:T(8,128)(2,1)S(1)} %get-tuple-element.103.x_ref.refs_0_.refs_1_, f32[2,128,2048]{2,1,0:T(8,128)S(1)} %get-tuple-element.124.dmix_ref.refs_2_, ...), custom_call_target="tpu_custom_call" | custom-call | flops 300000000 | tf_op jit(solution)/shard_map/gate_back/pallas_call | solution.py:56
  66.8 1.3 %collective-permute-done.17.refs_1_ = f32[48,512]{1,0:T(8,128)S(1)} collective-permute-done((f32[48,512]{1,0:T(8,128)S(1)}, f32[48,512]{1,0:T(8,128)S(1)}, u32[]{:S(2)}, u32[]{:S(2)}) %collective-permute-start.17) | collective-permute-done | bytes 98336 | tf_op jit(solution)/shard_map/give/ppermute | solution.py:504
  68.1 3.8 %collective-permute-start.18 = (f32[48,512]{1,0:T(8,128)S(1)}, f32[48,512]{1,0:T(8,128)S(1)}, u32[]{:S(2)}, u32[]{:S(2)}) collective-permute-start(f32[48,512]{1,0:T(8,128)S(1)} %add.11.refs_13_.refs_0_), channel_id=1, source_target_pairs={{0,8},{1,9},{2,10},{3,11},{4,12},{5,13},{6,14},{7,15},{8,0},{9,1},... | collective-permute-start | bytes 294920 | tf_op jit(solution)/shard_map/shared_3/ppermute | solution.py:500
  71.9 2.8 %backward_23.1 = (bf16[1,336,512]{2,1,0:T(8,128)(2,1)S(1)}, bf16[1,336,512]{2,1,0:T(8,128)(2,1)S(1)}, bf16[1,256,2048]{2,1,0:T(8,128)(2,1)S(1)}, bf16[1,256,2048]{2,1,0:T(8,128)(2,1)S(1)}) custom-call(bf16[2048,512]{1,0:T(8,128)(2,1)S(1)} %get-tuple-element.103.x_ref.refs_0_.refs_1_, f32[8,2,2048]{2,1,0:T(2,128)S(1)} %get-tuple-element.104.refs_1_.low_ref, ...), custom_call_target="tpu_custom_call" | custom-call | flops 300000000 | tf_op jit(solution)/shard_map/backward_23/pallas_call | solution.py:56
  74.8 0.9 collective-permute-start.21
  75.7 1.2 %collective-permute-start.22 = (bf16[1,336,512]{2,1,0:T(8,128)(2,1)S(1)}, bf16[1,336,512]{2,1,0:T(8,128)(2,1)S(1)}, u32[]{:S(2)}, u32[]{:S(2)}) collective-permute-start(bf16[1,336,512]{2,1,0:T(8,128)(2,1)S(1)} %get-tuple-element.179), channel_id=1, source_target_pairs={{0,2},{1,3},{2,0},{3,1},{4,6},{5,7},{6,4},{7,5},{8,10},{9,11},{10,... | collective-permute-start | bytes 1032200 | tf_op jit(solution)/shard_map/grad_three/ppermute | solution.py:500
  77.2 1.8 %collective-permute-start.19 = (f32[48,512]{1,0:T(8,128)S(1)}, f32[48,512]{1,0:T(8,128)S(1)}, u32[]{:S(2)}, u32[]{:S(2)}) collective-permute-start(f32[48,512]{1,0:T(8,128)S(1)} %add.12.refs_14_.refs_0_), channel_id=1, source_target_pairs={{0,4},{1,5},{2,6},{3,7},{4,0},{5,1},{6,2},{7,3},{8,12},{9,13},{10,... | collective-permute-start | bytes 294920 | tf_op jit(solution)/shard_map/shared_2/ppermute | solution.py:500
  79.0 2.8 %backward_01.1 = (f32[1,336,512]{2,1,0:T(8,128)S(1)}, f32[1,336,512]{2,1,0:T(8,128)S(1)}, bf16[1,256,2048]{2,1,0:T(8,128)(2,1)S(1)}, bf16[1,256,2048]{2,1,0:T(8,128)(2,1)S(1)}) custom-call(bf16[2048,512]{1,0:T(8,128)(2,1)S(1)} %get-tuple-element.103.x_ref.refs_0_.refs_1_, f32[8,2,2048]{2,1,0:T(2,128)S(1)} %get-tuple-element.104.refs_1_.low_ref, ...), custom_call_target="tpu_custom_call" | custom-call | flops 300000000 | tf_op jit(solution)/shard_map/backward_01/pallas_call | solution.py:56
  81.9 3.1 %input_1.1.refs_2_ = bf16[1024,512]{1,0:T(8,128)(2,1)S(1)} custom-call(bf16[32,2048]{1,0:T(8,128)(2,1)S(1)} %get-tuple-element.151.dgate_ref.refs_0_, bf16[2,16,512]{2,1,0:T(8,128)(2,1)S(1)} %bitcast.10, bf16[1,256,2048]{2,1,0:T(8,128)(2,1)S(1)} %get-tuple-element.171.refs_0_.refs_2_, bf16[1,256,2048]{2,1,0:T(8,128)(2,1)S(1)} %get-tuple-element.172.refs_1_.refs_3_, ...), custom_call_target="tpu_custom_call" | custom-call | flops 1050000000 | tf_op jit(solution)/shard_map/input_1/pallas_call | solution.py:56
  85.2 1.3 %collective-permute-start.25 = (bf16[1,336,512]{2,1,0:T(8,128)(2,1)S(1)}, bf16[1,336,512]{2,1,0:T(8,128)(2,1)S(1)}, u32[]{:S(2)}, u32[]{:S(2)}) collective-permute-start(bf16[1,336,512]{2,1,0:T(8,128)(2,1)S(1)} %get-tuple-element.180.refs_2_), channel_id=1, source_target_pairs={{8,0},{9,1},{10,2},{11,3},{12,4},{13,5},{14,6},{15,7},{16,24},{17,... | collective-permute-start | bytes 1032200 | tf_op jit(solution)/shard_map/far/ppermute | solution.py:500
  86.5 1.3 %collective-permute-start.24 = (bf16[1,336,512]{2,1,0:T(8,128)(2,1)S(1)}, bf16[1,336,512]{2,1,0:T(8,128)(2,1)S(1)}, u32[]{:S(2)}, u32[]{:S(2)}) collective-permute-start(bf16[1,336,512]{2,1,0:T(8,128)(2,1)S(1)} %add.15), channel_id=1, source_target_pairs={{8,4},{9,5},{10,6},{11,7},{12,0},{13,1},{14,2},{15,3},{16,28},{17,... | collective-permute-start | bytes 1032200 | tf_op jit(solution)/shard_map/cross/ppermute | solution.py:500
  87.8 3.6 %collective-permute-start.23 = (bf16[1,336,512]{2,1,0:T(8,128)(2,1)S(1)}, bf16[1,336,512]{2,1,0:T(8,128)(2,1)S(1)}, u32[]{:S(2)}, u32[]{:S(2)}) collective-permute-start(bf16[1,336,512]{2,1,0:T(8,128)(2,1)S(1)} %add.15), channel_id=1, source_target_pairs={{0,4},{1,5},{2,6},{3,7},{4,0},{5,1},{6,2},{7,3},{24,28},{25,29},{2... | collective-permute-start | bytes 1032200 | tf_op jit(solution)/shard_map/near/ppermute | solution.py:500
  91.5 0.9 collective-permute-start.26
  92.4 3.1 %input_0.1.refs_3_.refs_5_.refs_0_ = f32[1024,512]{1,0:T(8,128)S(1)} custom-call(bf16[32,2048]{1,0:T(8,128)(2,1)S(1)} %get-tuple-element.151.dgate_ref.refs_0_, bf16[2,16,512]{2,1,0:T(8,128)(2,1)S(1)} %bitcast.11, bf16[1,256,2048]{2,1,0:T(8,128)(2,1)S(1)} %get-tuple-element.171.refs_0_.refs_2_, bf16[1,256,2048]{2,1,0:T(8,128)(2,1)S(1)} %get-tuple-element.172.refs_1_.refs_3_, ...), custom_call_target="tpu_custom_call" | custom-call | flops 1050000000 | tf_op jit(solution)/shard_map/input_0/pallas_call | solution.py:56
  95.5 1.2 %collective-permute-done.26.refs_1_ = f32[48,512]{1,0:T(8,128)S(1)} collective-permute-done((f32[48,512]{1,0:T(8,128)S(1)}, f32[48,512]{1,0:T(8,128)S(1)}, u32[]{:S(2)}, u32[]{:S(2)}) %collective-permute-start.26) | collective-permute-done | bytes 98336 | tf_op jit(solution)/shard_map/shared_1/ppermute | solution.py:500
  97.3 4.8 %collective-permute-done.27.refs_1_ = f32[48,512]{1,0:T(8,128)S(1)} collective-permute-done((f32[48,512]{1,0:T(8,128)S(1)}, f32[48,512]{1,0:T(8,128)S(1)}, u32[]{:S(2)}, u32[]{:S(2)}) %collective-permute-start.27) | collective-permute-done | bytes 98336 | tf_op jit(solution)/shard_map/shared_0/ppermute | solution.py:500
  102.2 1.3 %collective-permute-done.28.give_ref = f32[48,512]{1,0:T(8,128)S(1)} collective-permute-done((f32[48,512]{1,0:T(8,128)S(1)}, f32[48,512]{1,0:T(8,128)S(1)}, u32[]{:S(2)}, u32[]{:S(2)}) %collective-permute-start.28) | collective-permute-done | bytes 98336 | tf_op jit(solution)/shard_map/keep/ppermute | solution.py:504
  103.5 1.3 %close.1 = (f32[2,16,512]{2,1,0:T(8,128)}, f32[2,16]{1,0:T(2,128)}, f32[2,64,128]{2,1,0:T(8,128)}, f32[2,64]{1,0:T(2,128)}, f32[2,64]{1,0:T(2,128)}, /*index=5*/f32[1,2]{1,0:T(1,128)}, f32[8,128]{1,0:T(8,128)S(1)}) custom-call(s32[35]{0:T(128)S(1)} %concatenate.3.int_ref.refs_0_.spot_ref, f32[48,512]{1,0:T(8,128)S(1)} %add.17.keep_ref, ...), custom_call_target="tpu_custom_call" | custom-call | flops 300000000 | tf_op jit(solution)/shard_map/close/pallas_call | solution.py:56
  105.2 1.5 %input_sum.1 = (f32[1024,512]{1,0:T(8,128)}, f32[8,128]{1,0:T(8,128)S(1)}) custom-call(f32[1024,512]{1,0:T(8,128)S(1)} %input_0.1.refs_3_.refs_5_.refs_0_, bf16[1024,512]{1,0:T(8,128)(2,1)S(1)} %collective-permute-done.20.refs_1_, f32[1,336,512]{2,1,0:T(8,128)S(1)} %add.18.refs_2_.refs_1_), custom_call_target="tpu_custom_call" | custom-call | flops 450000000 | tf_op jit(solution)/shard_map/input_sum/pallas_call | solution.py:56
  107.2 1.6 %finish.1 = (f32[1,512,256]{2,1,0:T(8,128)}, f32[1,256]{1,0:T(1,128)}, f32[1,256,128]{2,1,0:T(8,128)}, f32[1,128]{1,0:T(1,128)}) custom-call(s32[35]{0:T(128)S(1)} %concatenate.3.int_ref.refs_0_.spot_ref, f32[1,336,512]{2,1,0:T(8,128)S(1)} %add.18.refs_2_.refs_1_, f32[1,336,512]{2,1,0:T(8,128)S(1)} %collective-permute-done.29.refs_2_, ...), custom_call_target="tpu_custom_call" | custom-call | flops 3000000000 | tf_op jit(solution)/shard_map/finish/pallas_call | solution.py:56
  (65 shorter events, 6.7 us)
Async XLA Ops:
  0.6 9.6 %collective-permute-start.1 = (bf16[1024,512]{1,0:T(8,128)(2,1)}, bf16[1024,512]{1,0:T(8,128)(2,1)S(1)}, u32[]{:S(2)}, u32[]{:S(2)}) collective-permute-start(bf16[1024,512]{1,0:T(8,128)(2,1)} %mine_ref.1), channel_id=1, source_target_pairs={{0,16},{16,0},{1,17},{17,1},{2,18},{18,2},{3,19},{19,3},{4,20},{20... | collective-permute-start | bytes 3145736 | tf_op jit(solution)/shard_map/inputs/ppermute | solution.py:504
  2.4 13.5 %collective-permute-start.2 = (bf16[1,336,512]{2,1,0:T(8,128)(2,1)S(1)}, bf16[1,336,512]{2,1,0:T(8,128)(2,1)S(1)}, u32[]{:S(2)}, u32[]{:S(2)}) collective-permute-start(bf16[1,336,512]{2,1,0:T(8,128)(2,1)S(1)} %pack.1), channel_id=1, source_target_pairs={{0,8},{1,9},{2,10},{3,11},{4,12},{5,13},{6,14},{7,15},{8,24},{9,25... | collective-permute-start | bytes 1032200 | tf_op jit(solution)/shard_map/deal/ppermute | solution.py:513
  6.0 4.3 %collective-permute-start = (s32[2,1024]{1,0:T(2,128)}, s32[2,1024]{1,0:T(2,128)S(1)}, u32[]{:S(2)}, u32[]{:S(2)}) collective-permute-start(s32[2,1024]{1,0:T(2,128)} %label_ref.1), channel_id=1, source_target_pairs={{0,16},{16,0},{1,17},{17,1},{2,18},{18,2},{3,19},{19,3},{4,20},{20... | collective-permute-start | bytes 24584 | tf_op jit(solution)/shard_map/labels/ppermute | solution.py:504
  6.0 16.5 %collective-permute-start.5 = (bf16[1,336,512]{2,1,0:T(8,128)(2,1)S(1)}, bf16[1,336,512]{2,1,0:T(8,128)(2,1)S(1)}, u32[]{:S(2)}, u32[]{:S(2)}) collective-permute-start(bf16[1,336,512]{2,1,0:T(8,128)(2,1)S(1)} %pack.1), channel_id=1, source_target_pairs={{0,4},{1,5},{2,6},{3,7},{4,0},{5,1},{6,2},{7,3},{24,28},{25,29},{2... | collective-permute-start | bytes 1032200 | tf_op jit(solution)/shard_map/owners_near/ppermute | solution.py:500
  10.3 1.2 %copy-start = (bf16[1024,512]{1,0:T(8,128)(2,1)S(1)}, bf16[1024,512]{1,0:T(8,128)(2,1)}, u32[]{:S(2)}) copy-start(bf16[1024,512]{1,0:T(8,128)(2,1)} %mine_ref.1) | copy-start | bytes 3145732
  11.5 0.8 copy-start.1
  12.3 0.7 copy-start.4
  13.0 0.7 copy-start.8
  15.9 10.0 %collective-permute-start.4 = (bf16[1,336,512]{2,1,0:T(8,128)(2,1)S(1)}, bf16[1,336,512]{2,1,0:T(8,128)(2,1)S(1)}, u32[]{:S(2)}, u32[]{:S(2)}) collective-permute-start(bf16[1,336,512]{2,1,0:T(8,128)(2,1)S(1)} %hold.3.refs_0_.refs_3_.refs_8_.refs_10_), channel_id=1, source_target_pairs={{0,1},{1,0},{2,3},{3,2},{4,5},{5,4},{6,7},{7,6},{8,9},{9,8},{10,11... | collective-permute-start | bytes 1032200 | tf_op jit(solution)/shard_map/pay_4/ppermute | solution.py:500
  17.5 8.5 %collective-permute-start.3 = (bf16[1,336,512]{2,1,0:T(8,128)(2,1)S(1)}, bf16[1,336,512]{2,1,0:T(8,128)(2,1)S(1)}, u32[]{:S(2)}, u32[]{:S(2)}) collective-permute-start(bf16[1,336,512]{2,1,0:T(8,128)(2,1)S(1)} %hold.3.refs_0_.refs_3_.refs_8_.refs_10_), channel_id=1, source_target_pairs={{0,2},{1,3},{2,0},{3,1},{4,6},{5,7},{6,4},{7,5},{8,10},{9,11},{10,... | collective-permute-start | bytes 1032200 | tf_op jit(solution)/shard_map/pay_2/ppermute | solution.py:500
  19.0 6.9 %collective-permute-start.7 = (bf16[1,336,512]{2,1,0:T(8,128)(2,1)S(1)}, bf16[1,336,512]{2,1,0:T(8,128)(2,1)S(1)}, u32[]{:S(2)}, u32[]{:S(2)}) collective-permute-start(bf16[1,336,512]{2,1,0:T(8,128)(2,1)S(1)} %hold.3.refs_0_.refs_3_.refs_8_.refs_10_), channel_id=1, source_target_pairs={{8,12},{9,13},{10,14},{11,15},{12,8},{13,9},{14,10},{15,11},{16,20... | collective-permute-start | bytes 1032200 | tf_op jit(solution)/shard_map/pay_1/ppermute | solution.py:500
  26.0 11.0 %collective-permute-start.8 = (bf16[1,336,512]{2,1,0:T(8,128)(2,1)S(1)}, bf16[1,336,512]{2,1,0:T(8,128)(2,1)S(1)}, u32[]{:S(2)}, u32[]{:S(2)}) collective-permute-start(bf16[1,336,512]{2,1,0:T(8,128)(2,1)S(1)} %add.10.refs_0_.refs_4_.refs_9_.refs_11_), channel_id=1, source_target_pairs={{0,2},{1,3},{2,0},{3,1},{4,6},{5,7},{6,4},{7,5},{8,10},{9,11},{10,... | collective-permute-start | bytes 1032200 | tf_op jit(solution)/shard_map/pay_3/ppermute | solution.py:500
  26.6 12.1 %collective-permute-start.10 = (bf16[1,336,512]{2,1,0:T(8,128)(2,1)S(1)}, bf16[1,336,512]{2,1,0:T(8,128)(2,1)S(1)}, u32[]{:S(2)}, u32[]{:S(2)}) collective-permute-start(bf16[1,336,512]{2,1,0:T(8,128)(2,1)S(1)} %add.10.refs_0_.refs_4_.refs_9_.refs_11_), channel_id=1, source_target_pairs={{0,1},{1,0},{2,3},{3,2},{4,5},{5,4},{6,7},{7,6},{8,9},{9,8},{10,11... | collective-permute-start | bytes 1032200 | tf_op jit(solution)/shard_map/pay_5/ppermute | solution.py:500
  28.1 15.6 %collective-permute-start.6 = (bf16[1,336,512]{2,1,0:T(8,128)(2,1)S(1)}, bf16[1,336,512]{2,1,0:T(8,128)(2,1)S(1)}, u32[]{:S(2)}, u32[]{:S(2)}) collective-permute-start(bf16[1,336,512]{2,1,0:T(8,128)(2,1)S(1)} %hold.4.refs_2_.refs_0_.refs_3_.refs_10_.refs_12_), channel_id=1, source_target_pairs={{0,1},{1,0},{2,3},{3,2},{4,5},{5,4},{6,7},{7,6},{8,9},{9,8},{10,11... | collective-permute-start | bytes 1032200 | tf_op jit(solution)/shard_map/pay_6/ppermute | solution.py:500
  37.0 7.3 %collective-permute-start.9 = (bf16[1,336,512]{2,1,0:T(8,128)(2,1)S(1)}, bf16[1,336,512]{2,1,0:T(8,128)(2,1)S(1)}, u32[]{:S(2)}, u32[]{:S(2)}) collective-permute-start(bf16[1,336,512]{2,1,0:T(8,128)(2,1)S(1)} %hold.5), channel_id=1, source_target_pairs={{0,1},{1,0},{2,3},{3,2},{4,5},{5,4},{6,7},{7,6},{8,9},{9,8},{10,11... | collective-permute-start | bytes 1032200 | tf_op jit(solution)/shard_map/pay_7/ppermute | solution.py:500
  46.7 3.1 %collective-permute-start.11 = (bf16[2,128,1024]{2,1,0:T(8,128)(2,1)S(1)}, bf16[2,128,1024]{2,1,0:T(8,128)(2,1)S(1)}, u32[]{:S(2)}, u32[]{:S(2)}) collective-permute-start(bf16[2,128,1024]{2,1,0:T(8,128)(2,1)S(1)} %get-tuple-element.118.refs_0_), channel_id=1, source_target_pairs={{0,16},{16,0},{1,17},{17,1},{2,18},{18,2},{3,19},{19,3},{4,20},{20... | collective-permute-start | bytes 1572872 | tf_op jit(solution)/shard_map/mixed_other/ppermute | solution.py:504
  46.8 3.0 %copy-start.3 = (bf16[2,128,64]{1,2,0:T(8,128)(2,1)S(1)}, bf16[2,128,64]{1,2,0:T(8,128)(2,1)}, u32[]{:S(2)}) copy-start(bf16[2,128,64]{1,2,0:T(8,128)(2,1)} %param.21) | copy-start | bytes 98308
  46.8 3.0 %copy-start.5 = (bf16[2]{0:T(256)(128)(2,1)S(1)}, bf16[2]{0:T(256)(128)(2,1)}, u32[]{:S(2)}) copy-start(bf16[2]{0:T(256)(128)(2,1)} %param.24) | copy-start | bytes 16
  46.8 3.0 %copy-start.6 = (bf16[2,64]{1,0:T(2,128)(2,1)S(1)}, bf16[2,64]{1,0:T(2,128)(2,1)}, u32[]{:S(2)}) copy-start(bf16[2,64]{1,0:T(2,128)(2,1)} %refs_6_.1) | copy-start | bytes 772
  46.9 3.0 %copy-start.7 = (bf16[2,64]{1,0:T(2,128)(2,1)S(1)}, bf16[2,64]{1,0:T(2,128)(2,1)}, u32[]{:S(2)}) copy-start(bf16[2,64]{1,0:T(2,128)(2,1)} %refs_7_.1) | copy-start | bytes 772
  49.3 2.6 %collective-permute-start.12 = (bf16[2,128,1024]{2,1,0:T(8,128)(2,1)S(1)}, bf16[2,128,1024]{2,1,0:T(8,128)(2,1)S(1)}, u32[]{:S(2)}, u32[]{:S(2)}) collective-permute-start(bf16[2,128,1024]{2,1,0:T(8,128)(2,1)S(1)} %get-tuple-element.117.mix_ref), channel_id=1, source_target_pairs={{0,16},{16,0},{1,17},{17,1},{2,18},{18,2},{3,19},{19,3},{4,20},{20... | collective-permute-start | bytes 1572872 | tf_op jit(solution)/shard_map/mixed_own/ppermute | solution.py:504
  56.2 15.7 %collective-permute-start.15 = (bf16[1,336,512]{2,1,0:T(8,128)(2,1)S(1)}, bf16[1,336,512]{2,1,0:T(8,128)(2,1)S(1)}, u32[]{:S(2)}, u32[]{:S(2)}) collective-permute-start(bf16[1,336,512]{2,1,0:T(8,128)(2,1)S(1)} %get-tuple-element.166), channel_id=1, source_target_pairs={{0,1},{1,0},{2,3},{3,2},{4,5},{5,4},{6,7},{7,6},{8,9},{9,8},{10,11... | collective-permute-start | bytes 1032200 | tf_op jit(solution)/shard_map/grad_six/ppermute | solution.py:500
  57.9 14.1 %collective-permute-start.16 = (bf16[1,336,512]{2,1,0:T(8,128)(2,1)S(1)}, bf16[1,336,512]{2,1,0:T(8,128)(2,1)S(1)}, u32[]{:S(2)}, u32[]{:S(2)}) collective-permute-start(bf16[1,336,512]{2,1,0:T(8,128)(2,1)S(1)} %get-tuple-element.167), channel_id=1, source_target_pairs={{0,1},{1,0},{2,3},{3,2},{4,5},{5,4},{6,7},{7,6},{8,9},{9,8},{10,11... | collective-permute-start | bytes 1032200 | tf_op jit(solution)/shard_map/grad_seven/ppermute | solution.py:500
  61.1 17.8 %collective-permute-start.13 = (bf16[1,336,512]{2,1,0:T(8,128)(2,1)S(1)}, bf16[1,336,512]{2,1,0:T(8,128)(2,1)S(1)}, u32[]{:S(2)}, u32[]{:S(2)}) collective-permute-start(bf16[1,336,512]{2,1,0:T(8,128)(2,1)S(1)} %get-tuple-element.158), channel_id=1, source_target_pairs={{0,1},{1,0},{2,3},{3,2},{4,5},{5,4},{6,7},{7,6},{8,9},{9,8},{10,11... | collective-permute-start | bytes 1032200 | tf_op jit(solution)/shard_map/grad_four/ppermute | solution.py:500
  62.7 16.2 %collective-permute-start.14 = (bf16[1,336,512]{2,1,0:T(8,128)(2,1)S(1)}, bf16[1,336,512]{2,1,0:T(8,128)(2,1)S(1)}, u32[]{:S(2)}, u32[]{:S(2)}) collective-permute-start(bf16[1,336,512]{2,1,0:T(8,128)(2,1)S(1)} %get-tuple-element.159), channel_id=1, source_target_pairs={{0,1},{1,0},{2,3},{3,2},{4,5},{5,4},{6,7},{7,6},{8,9},{9,8},{10,11... | collective-permute-start | bytes 1032200 | tf_op jit(solution)/shard_map/grad_five/ppermute | solution.py:500
  66.7 1.4 %collective-permute-start.17 = (f32[48,512]{1,0:T(8,128)S(1)}, f32[48,512]{1,0:T(8,128)S(1)}, u32[]{:S(2)}, u32[]{:S(2)}) collective-permute-start(f32[48,512]{1,0:T(8,128)S(1)} %get-tuple-element.169), channel_id=1, source_target_pairs={{0,16},{16,0},{1,17},{17,1},{2,18},{18,2},{3,19},{19,3},{4,20},{20... | collective-permute-start | bytes 294920 | tf_op jit(solution)/shard_map/give/ppermute | solution.py:504
  68.1 9.0 %collective-permute-start.18 = (f32[48,512]{1,0:T(8,128)S(1)}, f32[48,512]{1,0:T(8,128)S(1)}, u32[]{:S(2)}, u32[]{:S(2)}) collective-permute-start(f32[48,512]{1,0:T(8,128)S(1)} %add.11.refs_13_.refs_0_), channel_id=1, source_target_pairs={{0,8},{1,9},{2,10},{3,11},{4,12},{5,13},{6,14},{7,15},{8,0},{9,1},... | collective-permute-start | bytes 294920 | tf_op jit(solution)/shard_map/shared_3/ppermute | solution.py:500
  74.8 10.3 %collective-permute-start.21 = (bf16[1,336,512]{2,1,0:T(8,128)(2,1)S(1)}, bf16[1,336,512]{2,1,0:T(8,128)(2,1)S(1)}, u32[]{:S(2)}, u32[]{:S(2)}) collective-permute-start(bf16[1,336,512]{2,1,0:T(8,128)(2,1)S(1)} %get-tuple-element.176), channel_id=1, source_target_pairs={{0,2},{1,3},{2,0},{3,1},{4,6},{5,7},{6,4},{7,5},{8,10},{9,11},{10,... | collective-permute-start | bytes 1032200 | tf_op jit(solution)/shard_map/grad_two/ppermute | solution.py:500
  75.7 10.8 %collective-permute-start.22 = (bf16[1,336,512]{2,1,0:T(8,128)(2,1)S(1)}, bf16[1,336,512]{2,1,0:T(8,128)(2,1)S(1)}, u32[]{:S(2)}, u32[]{:S(2)}) collective-permute-start(bf16[1,336,512]{2,1,0:T(8,128)(2,1)S(1)} %get-tuple-element.179), channel_id=1, source_target_pairs={{0,2},{1,3},{2,0},{3,1},{4,6},{5,7},{6,4},{7,5},{8,10},{9,11},{10,... | collective-permute-start | bytes 1032200 | tf_op jit(solution)/shard_map/grad_three/ppermute | solution.py:500
  77.2 4.7 %collective-permute-start.19 = (f32[48,512]{1,0:T(8,128)S(1)}, f32[48,512]{1,0:T(8,128)S(1)}, u32[]{:S(2)}, u32[]{:S(2)}) collective-permute-start(f32[48,512]{1,0:T(8,128)S(1)} %add.12.refs_14_.refs_0_), channel_id=1, source_target_pairs={{0,4},{1,5},{2,6},{3,7},{4,0},{5,1},{6,2},{7,3},{8,12},{9,13},{10,... | collective-permute-start | bytes 294920 | tf_op jit(solution)/shard_map/shared_2/ppermute | solution.py:500
  79.0 2.9 %copy-start.2 = (bf16[2,512,16]{1,2,0:T(8,128)(2,1)S(1)}, bf16[2,512,16]{1,2,0:T(8,128)(2,1)}, u32[]{:S(2)}) copy-start(bf16[2,512,16]{1,2,0:T(8,128)(2,1)} %param.19) | copy-start | bytes 98308
  85.0 20.3 %collective-permute-start.20 = (bf16[1024,512]{1,0:T(8,128)(2,1)S(1)}, bf16[1024,512]{1,0:T(8,128)(2,1)S(1)}, u32[]{:S(2)}, u32[]{:S(2)}) collective-permute-start(bf16[1024,512]{1,0:T(8,128)(2,1)S(1)} %input_1.1.refs_2_), channel_id=1, source_target_pairs={{0,16},{16,0},{1,17},{17,1},{2,18},{18,2},{3,19},{19,3},{4,20},{20... | collective-permute-start | bytes 3145736 | tf_op jit(solution)/shard_map/over/ppermute | solution.py:504
  85.2 19.7 %collective-permute-start.25 = (bf16[1,336,512]{2,1,0:T(8,128)(2,1)S(1)}, bf16[1,336,512]{2,1,0:T(8,128)(2,1)S(1)}, u32[]{:S(2)}, u32[]{:S(2)}) collective-permute-start(bf16[1,336,512]{2,1,0:T(8,128)(2,1)S(1)} %get-tuple-element.180.refs_2_), channel_id=1, source_target_pairs={{8,0},{9,1},{10,2},{11,3},{12,4},{13,5},{14,6},{15,7},{16,24},{17,... | collective-permute-start | bytes 1032200 | tf_op jit(solution)/shard_map/far/ppermute | solution.py:500
  86.5 18.3 %collective-permute-start.24 = (bf16[1,336,512]{2,1,0:T(8,128)(2,1)S(1)}, bf16[1,336,512]{2,1,0:T(8,128)(2,1)S(1)}, u32[]{:S(2)}, u32[]{:S(2)}) collective-permute-start(bf16[1,336,512]{2,1,0:T(8,128)(2,1)S(1)} %add.15), channel_id=1, source_target_pairs={{8,4},{9,5},{10,6},{11,7},{12,0},{13,1},{14,2},{15,3},{16,28},{17,... | collective-permute-start | bytes 1032200 | tf_op jit(solution)/shard_map/cross/ppermute | solution.py:500
  87.8 17.0 %collective-permute-start.23 = (bf16[1,336,512]{2,1,0:T(8,128)(2,1)S(1)}, bf16[1,336,512]{2,1,0:T(8,128)(2,1)S(1)}, u32[]{:S(2)}, u32[]{:S(2)}) collective-permute-start(bf16[1,336,512]{2,1,0:T(8,128)(2,1)S(1)} %add.15), channel_id=1, source_target_pairs={{0,4},{1,5},{2,6},{3,7},{4,0},{5,1},{6,2},{7,3},{24,28},{25,29},{2... | collective-permute-start | bytes 1032200 | tf_op jit(solution)/shard_map/near/ppermute | solution.py:500
  91.5 5.2 %collective-permute-start.26 = (f32[48,512]{1,0:T(8,128)S(1)}, f32[48,512]{1,0:T(8,128)S(1)}, u32[]{:S(2)}, u32[]{:S(2)}) collective-permute-start(f32[48,512]{1,0:T(8,128)S(1)} %add.13.refs_18_.refs_0_), channel_id=1, source_target_pairs={{0,2},{1,3},{2,0},{3,1},{4,6},{5,7},{6,4},{7,5},{8,10},{9,11},{10,... | collective-permute-start | bytes 294920 | tf_op jit(solution)/shard_map/shared_1/ppermute | solution.py:500
  96.7 5.4 %collective-permute-start.27 = (f32[48,512]{1,0:T(8,128)S(1)}, f32[48,512]{1,0:T(8,128)S(1)}, u32[]{:S(2)}, u32[]{:S(2)}) collective-permute-start(f32[48,512]{1,0:T(8,128)S(1)} %add.16.refs_0_), channel_id=1, source_target_pairs={{0,1},{1,0},{2,3},{3,2},{4,5},{5,4},{6,7},{7,6},{8,9},{9,8},{10,11... | collective-permute-start | bytes 294920 | tf_op jit(solution)/shard_map/shared_0/ppermute | solution.py:500
  102.1 1.4 %collective-permute-start.28 = (f32[48,512]{1,0:T(8,128)S(1)}, f32[48,512]{1,0:T(8,128)S(1)}, u32[]{:S(2)}, u32[]{:S(2)}) collective-permute-start(f32[48,512]{1,0:T(8,128)S(1)} %add.17.keep_ref), channel_id=1, source_target_pairs={{0,16},{16,0},{1,17},{17,1},{2,18},{18,2},{3,19},{19,3},{4,20},{20... | collective-permute-start | bytes 294920 | tf_op jit(solution)/shard_map/keep/ppermute | solution.py:504
  105.0 2.2 %collective-permute-start.29 = (f32[1,336,512]{2,1,0:T(8,128)S(1)}, f32[1,336,512]{2,1,0:T(8,128)S(1)}, u32[]{:S(2)}, u32[]{:S(2)}) collective-permute-start(f32[1,336,512]{2,1,0:T(8,128)S(1)} %add.18.refs_2_.refs_1_), channel_id=1, source_target_pairs={{0,16},{16,0},{1,17},{17,1},{2,18},{18,2},{3,19},{19,3},{4,20},{20... | collective-permute-start | bytes 2064392 | tf_op jit(solution)/shard_map/final/ppermute | solution.py:504
